TPU v7x, 32 devices: a whole 2x2x4 slice. The times are simulated.
32 devices in a mesh: ctx: 8 (over z, x), tensor: 4 (over y, core).
Axes of the slice: x: 2, y: 2, z: 4, core: 2. Of those that a mesh axis runs over, the one named last changes fastest.
Arguments:
- queries: bfloat16 [3072, 8192], P('ctx', 'tensor'), may hold values from -64 to 64
- key_layout_rows: bfloat16 [3072, 1024], P('ctx', 'tensor'), may hold values from -5 to 5
- value_layout_rows: bfloat16 [3072, 1024], P('ctx', 'tensor'), may hold values from -6 to 6
- output_gradient: bfloat16 [3072, 8192], P('ctx', 'tensor'), may hold values from -6 to 6
- doc_starts: int32 [24], P('ctx'), may hold values from 0 to 1, as said below
- block_mapping: int32 [24], replicated, may hold values from 0 to 23, as said below
Outputs:
- query_grad: bfloat16 [3072, 8192], P(('ctx', 'tensor'))
- key_grad: bfloat16 [3072, 1024], P(('ctx', 'tensor'))
- value_grad: bfloat16 [3072, 1024], P(('ctx', 'tensor'))
Inputs may be any that keep to these rules, and one draw needn't show every extreme that they name: `doc_starts`: the first block of every index of ctx begins a document, so in the executing layout every document lies whole within the 384 tokens of one index of ctx. A permutation of the blocks. Block s lies on index s // 3 of ctx; block_mapping[s] lies on that index or on the index 4 away. At least one and at most 2 blocks of each index come from the other index of its pair; indices 0 and 4 take exactly 2.
All inputs are finite; a program needn't handle non-finite values.
Results may differ from a plain program's by a relative error of at most 0.006.
Values may be sent and summed in bfloat16 or wider, within the bound.
No kernel may reach another device: no remote copies, remote signals or barrier semaphores. Data moves between devices by JAX's collectives and lax.ppermute only.
A program may use at most 64 MiB of HBM per device.

v0:
```python
import jax
import jax.numpy as jnp
import numpy as np
from jax import lax
from jax.sharding import PartitionSpec as P

HEAD_SIZE = 128


def passed_along(x, axis, by):
    peers = lax.axis_size(axis)
    return lax.ppermute(x, axis, [(i, (i + by) % peers) for i in range(peers)])


def on_device(
    queries, key_layout_rows, value_layout_rows, output_gradient, doc_starts, block_mapping
):
    rows_dev = queries.shape[0]
    block_count = doc_starts.shape[0]
    block_rows = rows_dev // block_count
    groups = key_layout_rows.shape[1] // HEAD_SIZE
    head_repeats = queries.shape[1] // key_layout_rows.shape[1]
    scaling = HEAD_SIZE ** (-0.5)
    document = jnp.cumsum(doc_starts)
    query_all = queries.reshape(rows_dev, groups, head_repeats, HEAD_SIZE)
    grad_all = output_gradient.reshape(rows_dev, groups, head_repeats, HEAD_SIZE)
    key_all = key_layout_rows.reshape(rows_dev, groups, HEAD_SIZE)
    value_all = value_layout_rows.reshape(rows_dev, groups, HEAD_SIZE)
    lower_query, lower_key = np.tril_indices(block_count)
    tile_query = jnp.asarray(lower_query, jnp.int32)
    tile_key = jnp.asarray(lower_key, jnp.int32)
    live_tiles = document[tile_query] == document[tile_key]
    slot_rank = jnp.cumsum(live_tiles.astype(jnp.int32)) - 1
    target_slot = jnp.where(live_tiles, slot_rank, tile_query.shape[0])
    packed_query = jnp.zeros_like(tile_query).at[target_slot].set(tile_query, mode="drop")
    packed_key = jnp.zeros_like(tile_key).at[target_slot].set(tile_key, mode="drop")
    tile_query, tile_key = (packed_query, packed_key)
    tile_count = jnp.sum(live_tiles.astype(jnp.int32))
    offsets = jnp.arange(block_rows, dtype=jnp.int32)

    def tile_inputs(tile_index):
        query_block = tile_query[tile_index]
        key_block = tile_key[tile_index]
        query_tile = lax.dynamic_slice_in_dim(query_all, query_block * block_rows, block_rows, 0)
        grad_tile = lax.dynamic_slice_in_dim(grad_all, query_block * block_rows, block_rows, 0)
        key_tile = lax.dynamic_slice_in_dim(key_all, key_block * block_rows, block_rows, 0)
        value_tile = lax.dynamic_slice_in_dim(value_all, key_block * block_rows, block_rows, 0)
        visible = (document[query_block] == document[key_block]) & (
            query_block * block_rows + offsets[:, None] >= key_block * block_rows + offsets[None, :]
        )
        scores = (
            jnp.einsum("qgrd,kgd->grqk", query_tile, key_tile, preferred_element_type=jnp.float32)
            * scaling
        )
        dprobs = jnp.einsum(
            "qgrd,kgd->grqk", grad_tile, value_tile, preferred_element_type=jnp.float32
        )
        return (query_block, key_block, query_tile, grad_tile, key_tile, visible, scores, dprobs)

    def row_slice(stat, query_block):
        return lax.dynamic_slice_in_dim(stat, query_block * block_rows, block_rows, 2)

    def row_store(stat, update, query_block):
        return lax.dynamic_update_slice_in_dim(stat, update, query_block * block_rows, 2)

    def first_pass(tile_index, carried):
        row_top, row_total, moment = carried
        query_block, key_block, query_tile, grad_tile, key_tile, visible, scores, dprobs = (
            tile_inputs(tile_index)
        )
        old_top = row_slice(row_top, query_block)
        tile_top = jnp.max(jnp.where(visible, scores, -1e30), axis=-1)
        new_top = jnp.maximum(old_top, tile_top)
        decay = jnp.exp(old_top - new_top)
        weights = jnp.where(visible, jnp.exp(scores - new_top[..., None]), 0.0)
        new_total = row_slice(row_total, query_block) * decay + jnp.sum(weights, axis=-1)
        new_moment = row_slice(moment, query_block) * decay + jnp.sum(weights * dprobs, axis=-1)
        return (
            row_store(row_top, new_top, query_block),
            row_store(row_total, new_total, query_block),
            row_store(moment, new_moment, query_block),
        )

    stat_shape = (groups, head_repeats, rows_dev)
    row_top, row_total, moment = lax.fori_loop(
        0,
        tile_count,
        first_pass,
        (
            jnp.full(stat_shape, -1e30, jnp.float32),
            jnp.zeros(stat_shape, jnp.float32),
            jnp.zeros(stat_shape, jnp.float32),
        ),
    )
    row_delta = moment / row_total

    def add_rows(total, piece, block_index):
        current = lax.dynamic_slice_in_dim(total, block_index * block_rows, block_rows, 0)
        return lax.dynamic_update_slice_in_dim(total, current + piece, block_index * block_rows, 0)

    def second_pass(tile_index, gradients):
        query_acc, key_acc, value_acc = gradients
        query_block, key_block, query_tile, grad_tile, key_tile, visible, scores, dprobs = (
            tile_inputs(tile_index)
        )
        tile_top = row_slice(row_top, query_block)[..., None]
        tile_total = row_slice(row_total, query_block)[..., None]
        tile_delta = row_slice(row_delta, query_block)[..., None]
        weights = jnp.where(visible, jnp.exp(scores - tile_top), 0.0) / tile_total
        weights_low = weights.astype(jnp.bfloat16)
        value_piece = jnp.einsum(
            "grqk,qgrd->kgd", weights_low, grad_tile, preferred_element_type=jnp.float32
        )
        dscores = (weights * (dprobs - tile_delta)).astype(jnp.bfloat16)
        query_piece = (
            jnp.einsum("grqk,kgd->qgrd", dscores, key_tile, preferred_element_type=jnp.float32)
            * scaling
        )
        key_piece = (
            jnp.einsum("grqk,qgrd->kgd", dscores, query_tile, preferred_element_type=jnp.float32)
            * scaling
        )
        return (
            add_rows(query_acc, query_piece, query_block),
            add_rows(key_acc, key_piece, key_block),
            add_rows(value_acc, value_piece, key_block),
        )

    query_acc, key_acc, value_acc = lax.fori_loop(
        0,
        tile_count,
        second_pass,
        (
            jnp.zeros((rows_dev, groups, head_repeats, HEAD_SIZE), jnp.float32),
            jnp.zeros((rows_dev, groups, HEAD_SIZE), jnp.float32),
            jnp.zeros((rows_dev, groups, HEAD_SIZE), jnp.float32),
        ),
    )
    query_low = query_acc.reshape(rows_dev, -1).astype(jnp.bfloat16)
    key_low = key_acc.reshape(rows_dev, -1).astype(jnp.bfloat16)
    value_low = value_acc.reshape(rows_dev, -1).astype(jnp.bfloat16)
    query_cols = query_low.shape[1]
    key_cols = key_low.shape[1]
    joined = jnp.concatenate([query_low, key_low, value_low], axis=1)
    blocks = joined.reshape(block_count, block_rows, joined.shape[1])
    axis_length = lax.axis_size("ctx")
    half_axis = axis_length // 2
    position = lax.axis_index("ctx")
    partner = (position + half_axis) % axis_length
    own_plan = lax.dynamic_slice_in_dim(block_mapping, position * block_count, block_count)
    peer_plan = lax.dynamic_slice_in_dim(block_mapping, partner * block_count, block_count)
    slot_ids = jnp.arange(block_count, dtype=jnp.int32)
    wanted = position * block_count + slot_ids
    own_match = (own_plan[:, None] == wanted[None, :]).astype(jnp.int32)
    peer_match = (peer_plan[:, None] == wanted[None, :]).astype(jnp.int32)
    arrived = passed_along(blocks, "ctx", half_axis)
    source = jnp.sum(own_match * slot_ids[:, None], axis=0) + jnp.sum(
        peer_match * (block_count + slot_ids)[:, None], axis=0
    )
    stacked = jnp.concatenate([blocks, arrived], axis=0)
    owned = jnp.take(stacked, source, axis=0).reshape(rows_dev, joined.shape[1])
    query_piece = owned[:, :query_cols]
    key_piece = owned[:, query_cols : query_cols + key_cols]
    value_piece = owned[:, query_cols + key_cols :]
    return (
        lax.all_to_all(query_piece, "tensor", split_axis=0, concat_axis=1, tiled=True),
        lax.all_to_all(key_piece, "tensor", split_axis=0, concat_axis=1, tiled=True),
        lax.all_to_all(value_piece, "tensor", split_axis=0, concat_axis=1, tiled=True),
    )


def solution(mesh):
    return jax.shard_map(
        on_device,
        mesh=mesh,
        in_specs=(
            P("ctx", "tensor"),
            P("ctx", "tensor"),
            P("ctx", "tensor"),
            P("ctx", "tensor"),
            P("ctx"),
            P(),
        ),
        out_specs=(
            P(("ctx", "tensor"), None),
            P(("ctx", "tensor"), None),
            P(("ctx", "tensor"), None),
        ),
        check_vma=False,
    )
```

profile of v0, /device:TPU:24, one launch (start us, length us, event | category | flops | bytes accessed | tf_op | source)
XLA Modules:
  0.0 289.4 jit_solution(9998188772146268891)
XLA Ops:
  0.7 1.0 reduce-window.14
  5.9 1.1 copy.68
  7.5 0.9 copy.69
  8.4 1.0 copy.77
  9.3 1.9 copy.71
  11.2 1.6 copy.75
  12.9 66.7 %while.32 = (s32[]{:T(128)}, f32[2,8,384]{2,1,0:T(8,128)S(1)}, f32[2,8,384]{2,1,0:T(8,128)S(1)}, f32[2,8,384]{2,1,0:T(8,128)S(1)}, s32[]{:T(128)}, /*index=5*/s3...) while((s32[]{:T(128)}, f32[2,8,384]{2,1,0:T(8,128)S(1)}, ...), condition=%wide.region_11.12_spmd.clone.clone, body=%wide.region_7.11_spmd.clone.clone.sunk | while | flops 136878352 | bytes 4630985 | solution.py:85
  22.2 1.4 fusion.85
  33.2 1.4 fusion.85
  44.2 1.4 fusion.85
  55.2 1.4 fusion.85
  66.2 1.4 fusion.85
  77.3 1.4 fusion.85
  80.9 0.8 broadcast.146
  81.9 97.7 %while.33 = (s32[]{:T(128)}, f32[384,2,8,128]{0,3,2,1:T(8,128)S(1)}, f32[384,2,128]{0,2,1:T(8,128)}, f32[384,2,128]{0,2,1:T(8,128)S(1)}, s32[]{:T(128)}, /*index...) while((s32[]{:T(128)}, ...), condition=%wide.region_13.14_spmd.clone.clone, body=%wide.region_12.13_spmd.clone.clone.sunk | while | flops 338297088 | bytes 19180108 | solution.py:129
  91.5 0.7 constant_dynamic-slice_fusion.5
  92.3 1.6 fusion.98
  94.2 1.2 fusion.99
  95.4 1.4 fusion.101
  96.8 1.3 fusion.100
  107.7 0.7 constant_dynamic-slice_fusion.5
  108.4 1.6 fusion.98
  110.4 1.2 fusion.99
  111.6 1.4 fusion.101
  113.0 1.3 fusion.100
  123.9 0.7 constant_dynamic-slice_fusion.5
  124.6 1.6 fusion.98
  126.6 1.2 fusion.99
  127.8 1.4 fusion.101
  129.2 1.3 fusion.100
  140.1 0.7 constant_dynamic-slice_fusion.5
  140.8 1.6 fusion.98
  142.8 1.2 fusion.99
  144.0 1.4 fusion.101
  145.4 1.3 fusion.100
  156.3 0.7 constant_dynamic-slice_fusion.5
  157.0 1.6 fusion.98
  159.0 1.2 fusion.99
  160.1 1.4 fusion.101
  161.6 1.3 fusion.100
  172.5 0.7 constant_dynamic-slice_fusion.5
  173.2 1.6 fusion.98
  175.2 1.2 fusion.99
  176.3 1.4 fusion.101
  177.7 1.3 fusion.100
  180.4 1.1 copy.82
  181.6 1.0 convert_element_type.46
  182.6 0.9 copy.81
  183.5 1.1 convert_element_type.47
  184.5 1.4 convert_element_type.44
  185.9 2.3 copy.80
  188.2 2.1 convert_element_type.45
  190.3 1.5 constant_dynamic-update-slice_fusion.3
  192.3 45.2 %collective-permute-done = bf16[3,128,2560]{2,1,0:T(8,128)(2,1)} collective-permute-done((bf16[3,128,2560]{2,1,0:T(8,128)(2,1)S(1)}, bf16[3,128,2560]{2,1,0:T(8,128)(2,1)}, u32[]{:S(2)}, u32[]{:S(2)}) %collective-permute-start) | collective-permute-done | bytes 1966112 | tf_op jit(solution)/shard_map/ppermute | solution.py:12
  237.5 3.7 %pad_maximum_fusion = bf16[6,128,2560]{2,1,0:T(8,128)(2,1)} fusion(bf16[3,128,2560]{2,1,0:T(8,128)(2,1)} %collective-permute-done, bf16[3,128,2560]{2,1,0:T(8,128)(2,1)S(1)} %constant_dynamic-update-slice_fusion.1), kind=kLoop, calls=%fused_computation.75 | loop fusion | flops 1966080 | bytes 7864320 | tf_op jit(solution)/shard_map/concatenate | solution.py:160
  241.3 4.1 %gather_fusion.2 = bf16[3,128,2560]{2,1,0:T(8,128)(2,1)} fusion(bf16[6,128,2560]{2,1,0:T(8,128)(2,1)} %pad_maximum_fusion, s32[1024]{0:T(1024)S(1)} %pad_clamp_fusion), kind=kCustom, calls=%fused_computation.2 | custom fusion | bytes 3932172 | tf_op jit(solution)/shard_map/jit(_take)/gather | solution.py:161
  245.4 1.8 bitcast_select_fusion
  247.9 7.9 %all_to_all.57 = bf16[4,96,256]{2,1,0:T(8,128)(2,1)S(1)} all-to-all(bf16[4,96,256]{2,1,0:T(8,128)(2,1)S(1)} %bitcast.184), channel_id=1, replica_groups=mesh['ctx'=8,'tensor'=4] {'tensor'}, dimensions={0} | all-to-all | bytes 393216 | tf_op jit(solution)/shard_map/all_to_all | solution.py:167
  255.8 3.4 %all-to-all-start.2 = ((bf16[4,96,256]{2,1,0:T(8,128)(2,1)}), bf16[4,96,256]{2,1,0:T(8,128)(2,1)S(1)}, u32[]{:S(2)}, u32[]{:S(2)}) async-start(bf16[4,96,256]{2,1,0:T(8,128)(2,1)} %bitcast.16), calls=%async_computation.2 | async-start | bytes 393216 | tf_op jit(solution)/shard_map/all_to_all | solution.py:168
  259.2 1.3 slice.18
  260.5 4.0 %all-to-all-done.2 = bf16[4,96,256]{2,1,0:T(8,128)(2,1)S(1)} async-done(((bf16[4,96,256]{2,1,0:T(8,128)(2,1)}), bf16[4,96,256]{2,1,0:T(8,128)(2,1)S(1)}, u32[]{:S(2)}, u32[]{:S(2)}) %all-to-all-start.2) | async-done | bytes 196640 | tf_op jit(solution)/shard_map/all_to_all | solution.py:168
  264.5 3.6 %all-to-all-start = ((bf16[4,96,2048]{2,1,0:T(8,128)(2,1)}), bf16[4,96,2048]{2,1,0:T(8,128)(2,1)S(1)}, u32[]{:S(2)}, u32[]{:S(2)}) async-start(bf16[4,96,2048]{2,1,0:T(8,128)(2,1)} %bitcast.175), calls=%async_computation | async-start | bytes 3145728 | tf_op jit(solution)/shard_map/all_to_all | solution.py:166
  269.5 18.7 %all-to-all-done = bf16[4,96,2048]{2,1,0:T(8,128)(2,1)S(1)} async-done(((bf16[4,96,2048]{2,1,0:T(8,128)(2,1)}), bf16[4,96,2048]{2,1,0:T(8,128)(2,1)S(1)}, u32[]{:S(2)}, u32[]{:S(2)}) %all-to-all-start) | async-done | bytes 1572896 | tf_op jit(solution)/shard_map/all_to_all | solution.py:166
  288.1 1.3 copy.100
  (193 shorter events, 42.9 us)
Async XLA Ops:
  0.6 6.5 %copy-start.9 = (bf16[384,256]{1,0:T(8,128)(2,1)S(1)}, bf16[384,256]{1,0:T(8,128)(2,1)}, u32[]{:S(2)}) copy-start(bf16[384,256]{1,0:T(8,128)(2,1)} %param.14) | copy-start | bytes 589828
  0.6 6.9 %copy-start.6 = (bf16[384,2048]{1,0:T(8,128)(2,1)S(1)}, bf16[384,2048]{1,0:T(8,128)(2,1)}, u32[]{:S(2)}) copy-start(bf16[384,2048]{1,0:T(8,128)(2,1)} %param.12) | copy-start | bytes 4718596
  79.5 0.8 copy-start.4
  79.6 0.7 copy-start.7
  79.6 1.3 copy-start
  79.6 1.3 copy-start.5
  79.6 1.3 copy-start.8
  92.3 1.6 copy-start.1
  93.9 1.5 copy-start.2
  96.8 1.3 copy-start.3
  108.4 1.6 copy-start.1
  110.0 1.5 copy-start.2
  113.0 1.3 copy-start.3
  124.6 1.6 copy-start.1
  126.2 1.5 copy-start.2
  129.2 1.3 copy-start.3
  140.8 1.6 copy-start.1
  142.4 1.5 copy-start.2
  145.4 1.3 copy-start.3
  157.0 1.6 copy-start.1
  158.6 1.5 copy-start.2
  161.5 1.3 copy-start.3
  173.2 1.6 copy-start.1
  174.8 1.5 copy-start.2
  177.7 1.3 copy-start.3
  190.3 1.7 copy-start.10
  191.9 45.6 %collective-permute-start = (bf16[3,128,2560]{2,1,0:T(8,128)(2,1)S(1)}, bf16[3,128,2560]{2,1,0:T(8,128)(2,1)}, u32[]{:S(2)}, u32[]{:S(2)}) collective-permute-start(bf16[3,128,2560]{2,1,0:T(8,128)(2,1)S(1)} %constant_dynamic-update-slice_fusion.1), channel_id=1, source_target_pairs={{0,16},{4,20},{8,24},{12,28},{16,0},{20,4},{24,8},{28,12},{1,17},{... | collective-permute-start | bytes 5898248 | tf_op jit(solution)/shard_map/ppermute | solution.py:12
  255.8 8.7 %all-to-all-start.2 = ((bf16[4,96,256]{2,1,0:T(8,128)(2,1)}), bf16[4,96,256]{2,1,0:T(8,128)(2,1)S(1)}, u32[]{:S(2)}, u32[]{:S(2)}) async-start(bf16[4,96,256]{2,1,0:T(8,128)(2,1)} %bitcast.16), calls=%async_computation.2 | async-start | bytes 393216 | tf_op jit(solution)/shard_map/all_to_all | solution.py:168
  264.5 23.6 %all-to-all-start = ((bf16[4,96,2048]{2,1,0:T(8,128)(2,1)}), bf16[4,96,2048]{2,1,0:T(8,128)(2,1)S(1)}, u32[]{:S(2)}, u32[]{:S(2)}) async-start(bf16[4,96,2048]{2,1,0:T(8,128)(2,1)} %bitcast.175), calls=%async_computation | async-start | bytes 3145728 | tf_op jit(solution)/shard_map/all_to_all | solution.py:166
where the time goes:
time: 293 us; the launch traced here: 289 us
  loops' own time  85.8 us (29%)
  waiting for transfers between devices  67.8 us (23%)
  local copies, waits for them, and re-layouts  60.5 us (21%)
  matrix products  45.1 us (15%)
  other arithmetic  14.4 us (5%)
  blocking collectives  7.92 us (3%)
  starting transfers between devices  7 us (2%)
    ppermute x1, waiting for transfers between devices, passed_along(): return lax.ppermute(x, axis, [(i, (i + by) % peers) for i in range(peers)])  45.2 us
    another operation x1, loops' own time, on_device(): lax.fori_loop(0, tile_count, first_pass, (jnp.full(stat_shape, -1e+30, jn...  43.5 us
    another operation x1, loops' own time, on_device(): lax.fori_loop(0, tile_count, second_pass, (jnp.zeros((rows_dev, groups, h...  42.3 us
    all_to_all x1, waiting for transfers between devices, on_device(): lax.all_to_all(query_piece, 'tensor', split_axis=0, concat_axis=1, tiled=...  18.7 us
    dot_general x12, matrix products, tile_inputs(): jnp.einsum('qgrd,kgd->grqk', grad_tile, value_tile, preferred_element_typ...  15.4 us
    dot_general x12, matrix products, tile_inputs(): jnp.einsum('qgrd,kgd->grqk', query_tile, key_tile, preferred_element_type...  11.4 us
    unnamed x26, local copies, waits for them, and re-layouts  9.03 us
    dynamic_slice x12, local copies, waits for them, and re-layouts, row_slice(): lax.dynamic_slice_in_dim(stat, query_block * block_rows, block_rows, 2)  8.58 us
  transfers between devices with their start and end apart: 3, of which 3 were waited for; matrix products, arithmetic and copies ran while one was open for 1% of the time, Pallas kernels for 0%

commit v1 on v0

v1 whole, which is shorter than its diff:
```python
import functools
import math

import jax
import jax.numpy as jnp
from jax import lax
from jax.experimental import pallas as pl
from jax.experimental.pallas import tpu as pltpu
from jax.sharding import PartitionSpec as P

HEAD_SIZE = 128
CAP = 2
HIDDEN = -1e30
VMEM_LIMIT = 60 * 1024 * 1024
KEYS_AND_VALUES = -1
PACK = 4
NO_COST = pl.CostEstimate(flops=1000, bytes_accessed=1000, transcendentals=0)
PARAMS = pltpu.CompilerParams(vmem_limit_bytes=VMEM_LIMIT)
IN_SMEM = pl.BlockSpec(memory_space=pltpu.SMEM)
IN_VMEM = pl.BlockSpec(memory_space=pltpu.VMEM)
ANYWHERE = pl.BlockSpec(memory_space=pl.ANY)


def contract(a, b, dims):
    return lax.dot_general(a, b, ((dims[:1], dims[1:]), ((), ())), preferred_element_type=jnp.float32)


def aligned(start, size, step):
    return pl.ds(pl.multiple_of(start, step), size)


def own_sources(mapping_ref, position, block_count):
    sources = [jnp.int32(-1)] * block_count
    for block in range(block_count):
        target = mapping_ref[position * block_count + block] - position * block_count
        for slot in range(block_count):
            sources[slot] = jnp.where(target == slot, block, sources[slot])
    return sources


def moved_blocks(mapping_ref, position, block_count):
    moved = [jnp.int32(0)] * CAP
    seen = jnp.int32(0)
    for block in range(block_count):
        target = mapping_ref[position * block_count + block] - position * block_count
        leaves = (target < 0) | (target >= block_count)
        for slot in range(CAP):
            moved[slot] = jnp.where(leaves & (seen <= slot), block, moved[slot])
        seen = seen + jnp.where(leaves, 1, 0)
    return moved


def heads_gradients(q_ref, g_ref, k_ref, v_ref, bias_ref, columns, block_count, block_rows):
    rate = HEAD_SIZE ** (-0.5) * math.log2(math.e)
    weights_low, dscores, query_pieces = [], [], []
    for block in range(block_count):
        rows = slice(block * block_rows, (block + 1) * block_rows)
        width = (block + 1) * block_rows
        q = jnp.concatenate([q_ref[rows, c] for c in columns], axis=0)
        g = jnp.concatenate([g_ref[rows, c] for c in columns], axis=0)
        k, v = k_ref[:width, :], v_ref[:width, :]
        bias = jnp.concatenate([bias_ref[:width, rows]] * len(columns), axis=1)
        scores = contract(k, q, (1, 1)) + bias
        top = jnp.max(scores, axis=0, keepdims=True)
        weights = jnp.exp2((scores - top) * rate)
        dprobs = contract(v, g, (1, 1))
        share = 1.0 / jnp.sum(weights, axis=0, keepdims=True)
        delta = jnp.sum(weights * dprobs, axis=0, keepdims=True) * share
        weights = weights * share
        weights_low.append(weights.astype(jnp.bfloat16))
        dscores.append((weights * (dprobs - delta)).astype(jnp.bfloat16))
        query_pieces.append((contract(dscores[-1], k, (0, 0)) * HEAD_SIZE ** (-0.5)).astype(jnp.bfloat16))
    return query_pieces, dscores, weights_low


def grads_kernel(block_count, block_rows, first, last, heads, sets, *refs):
    position_ref, starts_ref, mapping_ref, q_ref, g_ref, k_ref, v_ref, _, *refs = refs
    if not first:
        key_in, value_in, *refs = refs
    outs, refs = refs[: 2 * len(sets)], refs[2 * len(sets) :]
    if not last:
        key_out, value_out, *refs = refs
    bias_ref, low_ref, key_acc, value_acc = refs
    position = position_ref[0]
    rows = block_count * block_rows

    document_row = jnp.int32(0)
    for block in range(block_count):
        document_row = jnp.where(starts_ref[block] != 0, block * block_rows, document_row)
        width = (block + 1) * block_rows
        at_key = lax.broadcasted_iota(jnp.int32, (width, block_rows), 0)
        at_row = lax.broadcasted_iota(jnp.int32, (width, block_rows), 1) + block * block_rows
        visible = (at_key <= at_row) & (at_key >= document_row)
        bias_ref[:width, block * block_rows : width] = jnp.where(visible, 0.0, HIDDEN)
    if first:
        key_acc[...] = jnp.zeros_like(key_acc)
        value_acc[...] = jnp.zeros_like(value_acc)
    else:
        key_acc[...] = key_in[...]
        value_acc[...] = value_in[...]

    owned = [jnp.maximum(source, 0) for source in own_sources(mapping_ref, position, block_count)]
    moved = moved_blocks(mapping_ref, position, block_count)

    def put(own_ref, send_ref, at):
        columns = slice(at * HEAD_SIZE, (at + 1) * HEAD_SIZE)
        for slot, source in enumerate(owned):
            own_ref[slot * block_rows : (slot + 1) * block_rows, columns] = low_ref[
                aligned(source * block_rows, block_rows, block_rows), :
            ]
        for slot, source in enumerate(moved):
            send_ref[slot * block_rows : (slot + 1) * block_rows, columns] = low_ref[
                aligned(source * block_rows, block_rows, block_rows), :
            ]

    places = {unit: (outs[2 * i], outs[2 * i + 1], at) for i, units in enumerate(sets) for at, unit in enumerate(units)}
    for head in range(0, heads, PACK):
        packed = range(head, min(head + PACK, heads))
        columns = [slice(h * HEAD_SIZE, (h + 1) * HEAD_SIZE) for h in packed]
        query_pieces, dscores, weights_low = heads_gradients(
            q_ref, g_ref, k_ref, v_ref, bias_ref, columns, block_count, block_rows
        )
        stacked = lambda ref, block: [ref[b * block_rows : (b + 1) * block_rows, c] for b in range(block, block_count) for c in columns]
        for block in range(block_count):
            seen = slice(block * block_rows, (block + 1) * block_rows)
            joined = lambda pieces: jnp.concatenate([p[seen, :] for p in pieces[block:]], axis=1)
            value_acc[seen, :] += contract(joined(weights_low), jnp.concatenate(stacked(g_ref, block), axis=0), (1, 0))
            key_acc[seen, :] += contract(joined(dscores), jnp.concatenate(stacked(q_ref, block), axis=0), (1, 0))
        for index, h in enumerate(packed):
            for block in range(block_count):
                low_ref[block * block_rows : (block + 1) * block_rows, :] = query_pieces[block][
                    index * block_rows : (index + 1) * block_rows, :
                ]
            put(*places[h])
    if last:
        own_ref, send_ref, at = places[KEYS_AND_VALUES]
        low_ref[...] = (key_acc[...] * HEAD_SIZE ** (-0.5)).astype(jnp.bfloat16)
        put(own_ref, send_ref, at)
        low_ref[...] = value_acc[...].astype(jnp.bfloat16)
        put(own_ref, send_ref, at + 1)
    else:
        key_out[...] = key_acc[...]
        value_out[...] = value_acc[...]


def unit_columns(units):
    return (len(units) + units.count(KEYS_AND_VALUES)) * HEAD_SIZE


def grads_chunk(
    position, starts, mapping, queries, gradient, keys, values, after, carried, start_head, heads, group, sets
):
    rows = queries.shape[0]
    block_count = starts.shape[0]
    block_rows = rows // block_count
    first = carried is None
    last = any(KEYS_AND_VALUES in units for units in sets)
    whole = lambda r, c: pl.BlockSpec((r, c), lambda i: (0, 0))
    cut = pl.BlockSpec((pl.Element(rows), pl.Element(heads * HEAD_SIZE)), lambda i: (0, start_head * HEAD_SIZE))
    group_spec = pl.BlockSpec((rows, HEAD_SIZE), lambda i: (0, group))
    running = jax.ShapeDtypeStruct((rows, HEAD_SIZE), jnp.float32)
    out_shape = []
    for units in sets:
        out_shape.append(jax.ShapeDtypeStruct((rows, unit_columns(units)), jnp.bfloat16))
        out_shape.append(jax.ShapeDtypeStruct((CAP * block_rows, unit_columns(units)), jnp.bfloat16))
    if not last:
        out_shape += [running, running]
    out = pl.pallas_call(
        functools.partial(grads_kernel, block_count, block_rows, first, last, heads, sets),
        grid=(1,),
        in_specs=[IN_SMEM] * 3
        + [cut, cut, group_spec, group_spec, ANYWHERE]
        + ([] if first else [whole(rows, HEAD_SIZE)] * 2),
        out_specs=[whole(*s.shape) for s in out_shape],
        out_shape=out_shape,
        scratch_shapes=[
            pltpu.VMEM((rows, rows), jnp.float32),
            pltpu.VMEM((rows, HEAD_SIZE), jnp.bfloat16),
            pltpu.VMEM((rows, HEAD_SIZE), jnp.float32),
            pltpu.VMEM((rows, HEAD_SIZE), jnp.float32),
        ],
        compiler_params=PARAMS,
        cost_estimate=NO_COST,
    )(position, starts, mapping, queries, gradient, keys, values, after, *(carried or ()))
    pairs = [(out[2 * i], out[2 * i + 1]) for i in range(len(sets))]
    return pairs, (None if last else tuple(out[2 * len(sets) :]))


def sort_kernel(block_count, block_rows, half_axis, peers, position_ref, mapping_ref, own_ref, arrived_ref, *refs):
    outs = refs[-peers:]
    at, peer = position_ref[0], position_ref[1]
    partner = lax.rem(at + half_axis, 2 * half_axis)
    arrived_slot = [jnp.int32(-1)] * block_count
    for index, block in enumerate(moved_blocks(mapping_ref, partner, block_count)):
        target = mapping_ref[partner * block_count + block] - at * block_count
        for slot in range(block_count):
            arrived_slot[slot] = jnp.where(target == slot, index, arrived_slot[slot])
    share = block_count * block_rows // peers
    step = math.gcd(share, block_rows)
    for hop, out_ref in enumerate(outs):
        to_peer = jnp.bitwise_xor(peer, hop)
        for piece in range(share // step):
            row = to_peer * share + piece * step
            block = lax.div(row, block_rows)
            slot = jnp.int32(-1)
            for b in range(block_count):
                slot = jnp.where(block == b, arrived_slot[b], slot)
            from_own = own_ref[aligned(row, step, step), :]
            from_pair = arrived_ref[
                aligned(jnp.maximum(slot, 0) * block_rows + lax.rem(row, block_rows), step, step), :
            ]
            out_ref[piece * step : (piece + 1) * step, :] = jnp.where(slot >= 0, from_pair, from_own)


def sort_rows(position, mapping, own, arrived, after, block_count, half_axis, peers):
    rows, columns = own.shape
    out = jax.ShapeDtypeStruct((rows // peers, columns), own.dtype)
    return pl.pallas_call(
        functools.partial(sort_kernel, block_count, rows // block_count, half_axis, peers),
        in_specs=[IN_SMEM, IN_SMEM, IN_VMEM, IN_VMEM] + [ANYWHERE] * len(after),
        out_specs=[IN_VMEM] * peers,
        out_shape=[out] * peers,
        compiler_params=PARAMS,
        cost_estimate=NO_COST,
    )(position, mapping, own, arrived, *after)


def place_kernel(peers, columns_here, places, held, position_ref, *refs):
    pieces = refs[: peers * len(places)]
    outs, sem = refs[-len(columns_here) - 1 : -1], refs[-1]
    peer = position_ref[1]
    copies = []
    for index, parts in enumerate(places):
        for hop in range(peers):
            from_peer = jnp.bitwise_xor(peer, hop)
            piece = pieces[index * peers + hop]
            for at, size, out, column in parts:
                copies.append(
                    pltpu.make_async_copy(
                        piece.at[:, at : at + size],
                        outs[out].at[:, aligned(from_peer * columns_here[out] + column, size, HEAD_SIZE)],
                        sem.at[len(copies)],
                    )
                )
                copies[-1].start()
    for copy in copies:
        copy.wait()


def place_columns(position, pieces, places, columns_here, held, peers):
    rows = pieces[0][0].shape[0]
    flat = [p for chunk in pieces for p in chunk]
    count = peers * sum(len(parts) for parts in places)
    out_shape = [jax.ShapeDtypeStruct((rows, peers * c), pieces[0][0].dtype) for c in columns_here]
    return pl.pallas_call(
        functools.partial(place_kernel, peers, columns_here, places, len(held)),
        in_specs=[IN_SMEM] + [IN_VMEM] * len(flat) + [ANYWHERE] * len(held),
        out_specs=[ANYWHERE] * len(out_shape),
        out_shape=out_shape,
        input_output_aliases={1 + len(flat) + i: i for i in range(len(held))},
        scratch_shapes=[pltpu.SemaphoreType.DMA((count,))],
        compiler_params=PARAMS,
        cost_estimate=NO_COST,
    )(position, *flat, *held)


def plan_of(groups, repeats):
    lead, most = max(1, repeats // 2), max(1, 3 * repeats // 4)
    kernels = [(0, 0, lead, [list(range(lead))])]
    kernels.append((0, lead, repeats - lead, [list(range(repeats - lead)) + [KEYS_AND_VALUES]]))
    for group in range(1, groups):
        heads = list(range(repeats))
        kernels.append((group, 0, repeats, [heads[:most], heads[most:] + [KEYS_AND_VALUES]]))
    return kernels


def on_device(queries, key_layout_rows, value_layout_rows, output_gradient, doc_starts, block_mapping):
    rows = queries.shape[0]
    block_count = doc_starts.shape[0]
    groups = key_layout_rows.shape[1] // HEAD_SIZE
    repeats = queries.shape[1] // key_layout_rows.shape[1]
    axis_length = lax.axis_size("ctx")
    half_axis = axis_length // 2
    peers = lax.axis_size("tensor")
    position = jnp.stack([lax.axis_index("ctx"), lax.axis_index("tensor")]).astype(jnp.int32)
    pairs = [(i, (i + half_axis) % axis_length) for i in range(axis_length)]

    carried, after, sent = None, key_layout_rows, []
    for group, start, heads, sets in plan_of(groups, repeats):
        made, carried = grads_chunk(
            position, doc_starts, block_mapping, queries, output_gradient, key_layout_rows, value_layout_rows,
            after, carried, group * repeats + start, heads, group, sets,
        )
        after = made[0][0]
        for units, (own, send) in zip(sets, made):
            sent.append((group, start, units, own, lax.ppermute(send, "ctx", pairs)))

    order, pieces, places = [after], [], []
    for group, start, units, own, arrived in sent:

        def exchange(own, arrived, *order):
            parts = sort_rows(position, block_mapping, own, arrived, order, block_count, half_axis, peers)
            return [parts[0]] + [
                lax.ppermute(parts[hop], "tensor", [(i, i ^ hop) for i in range(peers)]) for hop in range(1, peers)
            ]

        def nothing(own, arrived, *order):
            return [jnp.zeros((rows // peers, own.shape[1]), own.dtype)] * peers

        if len(pieces) < len(sent) - 1:
            got = lax.cond(block_mapping[0] >= 0, exchange, nothing, own, arrived, *order)
        else:
            got = exchange(own, arrived, *order)
        order = [got[0]]
        pieces.append(got)
        parts, at = [], 0
        queries_here = [u for u in units if u != KEYS_AND_VALUES]
        if queries_here:
            size = len(queries_here) * HEAD_SIZE
            parts.append((0, size, 0, (group * repeats + start + queries_here[0]) * HEAD_SIZE))
            at = size
        if KEYS_AND_VALUES in units:
            parts.append((at, HEAD_SIZE, 1, group * HEAD_SIZE))
            parts.append((at + HEAD_SIZE, HEAD_SIZE, 2, group * HEAD_SIZE))
        places.append(parts)
    columns_here = [queries.shape[1], key_layout_rows.shape[1], value_layout_rows.shape[1]]
    held = []
    if len(pieces) > 1:
        held = place_columns(position, pieces[:-1], places[:-1], columns_here, [], peers)
    return tuple(place_columns(position, pieces[-1:], places[-1:], columns_here, held, peers))


def solution(mesh):
    return jax.shard_map(
        on_device,
        mesh=mesh,
        in_specs=(
            P("ctx", "tensor"),
            P("ctx", "tensor"),
            P("ctx", "tensor"),
            P("ctx", "tensor"),
            P("ctx"),
            P(),
        ),
        out_specs=(
            P(("ctx", "tensor"), None),
            P(("ctx", "tensor"), None),
            P(("ctx", "tensor"), None),
        ),
        check_vma=False,
    )
```

time: 293 us -> 84.6 us (0.29)
  the two profiles are of different devices: /device:TPU:24 before, /device:TPU:0 now
where the time goes in v1:
time: 84.6 us; the launch traced here: 84.3 us
  waiting for transfers between devices  42.2 us (50%)
  Pallas kernels  24.8 us (29%)
  starting transfers between devices  15 us (18%)
  local copies, waits for them, and re-layouts  1.35 us (2%)
    ppermute x12, waiting for transfers between devices, exchange(): lax.ppermute(parts[hop], 'tensor', [(i, i ^ hop) for i in range(peers)])  22.4 us
    ppermute x4, waiting for transfers between devices, on_device(): sent.append((group, start, units, own, lax.ppermute(send, 'ctx', pairs)))  19.8 us
    pallas_call x3, Pallas kernels, grads_chunk(): pl.pallas_call(functools.partial(grads_kernel, block_count, block_rows, f...  14.2 us
    ppermute x12, starting transfers between devices, exchange(): lax.ppermute(parts[hop], 'tensor', [(i, i ^ hop) for i in range(peers)])  8.04 us
    ppermute x4, starting transfers between devices, on_device(): sent.append((group, start, units, own, lax.ppermute(send, 'ctx', pairs)))  6.98 us
    pallas_call x4, Pallas kernels, sort_rows(): pl.pallas_call(functools.partial(sort_kernel, block_count, rows // block_...  6.08 us
    pallas_call x2, Pallas kernels, place_columns(): pl.pallas_call(functools.partial(place_kernel, peers, columns_here, place...  4.52 us
  transfers between devices with their start and end apart: 16, of which 10 were waited for; matrix products, arithmetic and copies ran while one was open for 0% of the time, Pallas kernels for 20%

profile of v1, /device:TPU:0, one launch (start us, length us, event | category | flops | bytes accessed | tf_op | source)
XLA Modules:
  0.0 84.3 jit_solution(4410530251474658090)
XLA Ops:
  0.6 0.1 pad_add_fusion.refs_0_.position_ref
  0.7 0.0 copy-start.4
  0.7 3.9 %shard_map.85 = (bf16[384,512]{1,0:T(8,128)(2,1)S(1)}, bf16[256,512]{1,0:T(8,128)(2,1)}, f32[384,128]{1,0:T(8,128)}, f32[384,128]{1,0:T(8,128)}) custom-call(s32[2]{0:T(128)S(1)} %pad_add_fusion.refs_0_.position_ref, s32[3]{0:T(128)} %refs_1_.5, s32[24]{0:T(128)} %mapping_ref.1, bf16[384,2048]{1,0:T(8,128)(2,1)} %refs_3_.5, bf16[384,2048]{1,0:T(8,128)(2,1)} %refs_4_.5, ...), custom_call_target="tpu_custom_call" | custom-call | flops 1000 | bytes 1000 | tf_op jit(solution)/shard_map/pallas_call | solution.py:168
  4.6 4.0 %collective-permute-start.12 = (bf16[256,512]{1,0:T(8,128)(2,1)}, bf16[256,512]{1,0:T(8,128)(2,1)S(1)}, u32[]{:S(2)}, u32[]{:S(2)}) collective-permute-start(bf16[256,512]{1,0:T(8,128)(2,1)} %get-tuple-element.98), channel_id=1, source_target_pairs={{0,16},{4,20},{8,24},{12,28},{16,0},{20,4},{24,8},{28,12},{1,17},{... | collective-permute-start | bytes 786440 | tf_op jit(solution)/shard_map/ppermute | solution.py:296
  8.7 0.0 copy-done.4
  8.7 4.1 %shard_map.86 = (bf16[384,768]{1,0:T(8,128)(2,1)S(1)}, bf16[256,768]{1,0:T(8,128)(2,1)}) custom-call(s32[2]{0:T(128)S(1)} %pad_add_fusion.refs_0_.position_ref, s32[3]{0:T(128)} %refs_1_.5, s32[24]{0:T(128)S(1)} %copy-done.4, bf16[384,2048]{1,0:T(8,128)(2,1)} %refs_3_.5, bf16[384,2048]{1,0:T(8,128)(2,1)} %refs_4_.5, bf16[384,256]{1,0:T(8,128)(2,1)} %refs_5_.5, ...), custom_call_target="tpu_custom_call" | custom-call | flops 1000 | bytes 1000 | tf_op jit(solution)/shard_map/pallas_call | solution.py:168
  12.8 0.0 collective-permute-start.11
  12.8 6.2 %shard_map.87 = (bf16[384,768]{1,0:T(8,128)(2,1)S(1)}, bf16[256,768]{1,0:T(8,128)(2,1)}, bf16[384,512]{1,0:T(8,128)(2,1)}, bf16[256,512]{1,0:T(8,128)(2,1)}) custom-call(s32[2]{0:T(128)S(1)} %pad_add_fusion.refs_0_.position_ref, s32[3]{0:T(128)} %refs_1_.5, s32[24]{0:T(128)S(1)} %copy-done.4, bf16[384,2048]{1,0:T(8,128)(2,1)} %refs_3_.5, ...), custom_call_target="tpu_custom_call" | custom-call | flops 1000 | bytes 1000 | tf_op jit(solution)/shard_map/pallas_call | solution.py:168
  19.0 0.0 copy-start.5
  19.0 2.9 %collective-permute-start.10 = (bf16[256,768]{1,0:T(8,128)(2,1)}, bf16[256,768]{1,0:T(8,128)(2,1)S(1)}, u32[]{:S(2)}, u32[]{:S(2)}) collective-permute-start(bf16[256,768]{1,0:T(8,128)(2,1)} %get-tuple-element.96), channel_id=1, source_target_pairs={{0,16},{4,20},{8,24},{12,28},{16,0},{20,4},{24,8},{28,12},{1,17},{... | collective-permute-start | bytes 1179656 | tf_op jit(solution)/shard_map/ppermute | solution.py:296
  22.0 16.5 %collective-permute-done.12 = bf16[256,512]{1,0:T(8,128)(2,1)S(1)} collective-permute-done((bf16[256,512]{1,0:T(8,128)(2,1)}, bf16[256,512]{1,0:T(8,128)(2,1)S(1)}, u32[]{:S(2)}, u32[]{:S(2)}) %collective-permute-start.12) | collective-permute-done | bytes 262176 | tf_op jit(solution)/shard_map/ppermute | solution.py:296
  38.5 8.8 %conditional.3 = (bf16[96,512]{1,0:T(8,128)(2,1)S(1)}, bf16[96,512]{1,0:T(8,128)(2,1)}, bf16[96,512]{1,0:T(8,128)(2,1)}, bf16[96,512]{1,0:T(8,128)(2,1)}) conditional(s32[]{:T(128)} %bitcast.2, () %tuple.33, (s32[2]{0:T(128)S(1)}, s32[24]{0:T(128)S(1)}, bf16[384,512]{1,0:T(8,128)(2,1)S(1)}, bf16[256,512]{1,0:T(8,128)(2,1)S(1)}, ...), branch_computations={%region_0.0_spmd, %region_1.0_spmd} | conditional | flops 1000 | bytes 1180800 | solution.py:311
  38.5 1.3 %branch_1_fun.3 = (bf16[96,512]{1,0:T(8,128)(2,1)S(1)}, bf16[96,512]{1,0:T(8,128)(2,1)}, bf16[96,512]{1,0:T(8,128)(2,1)}, bf16[96,512]{1,0:T(8,128)(2,1)}) custom-call(s32[2]{0:T(128)S(1)} %get-tuple-element.30.position_ref, s32[24]{0:T(128)S(1)} %get-tuple-element.31.mapping_ref, bf16[384,512]{1,0:T(8,128)(2,1)S(1)} %get-tuple-element.32.own_ref, ...), custom_call_target="tpu_custom_call" | custom-call | flops 1000 | bytes 1000 | tf_op jit(solution)/shard_map/cond/branch_1_fun/pallas_call | solution.py:218
  39.8 0.0 collective-permute-start
  39.8 1.9 %collective-permute-start.1 = (bf16[96,512]{1,0:T(8,128)(2,1)}, bf16[96,512]{1,0:T(8,128)(2,1)}, u32[]{:S(2)}, u32[]{:S(2)}) collective-permute-start(bf16[96,512]{1,0:T(8,128)(2,1)} %get-tuple-element.37), channel_id=1, source_target_pairs={{0,2},{1,3},{2,0},{3,1},{4,6},{5,7},{6,4},{7,5},{8,10},{9,11},{10,... | collective-permute-start | bytes 294920 | tf_op jit(solution)/shard_map/cond/branch_1_fun/ppermute | solution.py:304
  41.7 0.1 collective-permute-start.2
  41.9 0.0 collective-permute-done
  41.9 4.0 %collective-permute-done.1 = bf16[96,512]{1,0:T(8,128)(2,1)} collective-permute-done((bf16[96,512]{1,0:T(8,128)(2,1)}, bf16[96,512]{1,0:T(8,128)(2,1)}, u32[]{:S(2)}, u32[]{:S(2)}) %collective-permute-start.1) | collective-permute-done | bytes 98336 | tf_op jit(solution)/shard_map/cond/branch_1_fun/ppermute | solution.py:304
  45.8 1.4 %collective-permute-done.2 = bf16[96,512]{1,0:T(8,128)(2,1)} collective-permute-done((bf16[96,512]{1,0:T(8,128)(2,1)}, bf16[96,512]{1,0:T(8,128)(2,1)}, u32[]{:S(2)}, u32[]{:S(2)}) %collective-permute-start.2) | collective-permute-done | bytes 98336 | tf_op jit(solution)/shard_map/cond/branch_1_fun/ppermute | solution.py:304
  47.2 0.0 copy-done.5
  47.2 0.0 collective-permute-start.9
  47.3 0.0 collective-permute-done.11
  47.3 10.4 %conditional.4 = (bf16[96,768]{1,0:T(8,128)(2,1)S(1)}, bf16[96,768]{1,0:T(8,128)(2,1)}, bf16[96,768]{1,0:T(8,128)(2,1)}, bf16[96,768]{1,0:T(8,128)(2,1)}) conditional(s32[]{:T(128)} %bitcast.2, () %tuple.32, (s32[2]{0:T(128)S(1)}, s32[24]{0:T(128)S(1)}, bf16[384,768]{1,0:T(8,128)(2,1)S(1)}, bf16[256,768]{1,0:T(8,128)(2,1)S(1)}, ...), branch_computations={%region_2.0_spmd, %region_3.0_spmd} | conditional | flops 1000 | bytes 1770624 | solution.py:311
  47.3 1.4 %branch_1_fun.4 = (bf16[96,768]{1,0:T(8,128)(2,1)S(1)}, bf16[96,768]{1,0:T(8,128)(2,1)}, bf16[96,768]{1,0:T(8,128)(2,1)}, bf16[96,768]{1,0:T(8,128)(2,1)}) custom-call(s32[2]{0:T(128)S(1)} %get-tuple-element.39.position_ref, s32[24]{0:T(128)S(1)} %get-tuple-element.40.mapping_ref, bf16[384,768]{1,0:T(8,128)(2,1)S(1)} %get-tuple-element.41.own_ref, ...), custom_call_target="tpu_custom_call" | custom-call | flops 1000 | bytes 1000 | tf_op jit(solution)/shard_map/cond/branch_1_fun/pallas_call | solution.py:218
  48.7 0.4 collective-permute-start.3
  49.0 1.7 %collective-permute-start.4 = (bf16[96,768]{1,0:T(8,128)(2,1)}, bf16[96,768]{1,0:T(8,128)(2,1)}, u32[]{:S(2)}, u32[]{:S(2)}) collective-permute-start(bf16[96,768]{1,0:T(8,128)(2,1)} %get-tuple-element.46), channel_id=1, source_target_pairs={{0,2},{1,3},{2,0},{3,1},{4,6},{5,7},{6,4},{7,5},{8,10},{9,11},{10,... | collective-permute-start | bytes 442376 | tf_op jit(solution)/shard_map/cond/branch_1_fun/ppermute | solution.py:304
  50.8 0.0 collective-permute-start.5
  50.8 0.0 collective-permute-done.3
  50.8 5.3 %collective-permute-done.4 = bf16[96,768]{1,0:T(8,128)(2,1)} collective-permute-done((bf16[96,768]{1,0:T(8,128)(2,1)}, bf16[96,768]{1,0:T(8,128)(2,1)}, u32[]{:S(2)}, u32[]{:S(2)}) %collective-permute-start.4) | collective-permute-done | bytes 147488 | tf_op jit(solution)/shard_map/cond/branch_1_fun/ppermute | solution.py:304
  56.0 1.6 %collective-permute-done.5 = bf16[96,768]{1,0:T(8,128)(2,1)} collective-permute-done((bf16[96,768]{1,0:T(8,128)(2,1)}, bf16[96,768]{1,0:T(8,128)(2,1)}, u32[]{:S(2)}, u32[]{:S(2)}) %collective-permute-start.5) | collective-permute-done | bytes 147488 | tf_op jit(solution)/shard_map/cond/branch_1_fun/ppermute | solution.py:304
  57.6 3.3 %collective-permute-done.10 = bf16[256,768]{1,0:T(8,128)(2,1)S(1)} collective-permute-done((bf16[256,768]{1,0:T(8,128)(2,1)}, bf16[256,768]{1,0:T(8,128)(2,1)S(1)}, u32[]{:S(2)}, u32[]{:S(2)}) %collective-permute-start.10) | collective-permute-done | bytes 393248 | tf_op jit(solution)/shard_map/ppermute | solution.py:296
  61.0 10.9 %conditional.5 = (bf16[96,768]{1,0:T(8,128)(2,1)S(1)}, bf16[96,768]{1,0:T(8,128)(2,1)}, bf16[96,768]{1,0:T(8,128)(2,1)}, bf16[96,768]{1,0:T(8,128)(2,1)}) conditional(s32[]{:T(128)} %bitcast.2, () %tuple.31, (s32[2]{0:T(128)S(1)}, s32[24]{0:T(128)S(1)}, bf16[384,768]{1,0:T(8,128)(2,1)S(1)}, bf16[256,768]{1,0:T(8,128)(2,1)S(1)}, ...), branch_computations={%region_4.0_spmd, %region_5.0_spmd} | conditional | flops 1000 | bytes 1770624 | solution.py:311
  61.0 1.4 %branch_1_fun.5 = (bf16[96,768]{1,0:T(8,128)(2,1)S(1)}, bf16[96,768]{1,0:T(8,128)(2,1)}, bf16[96,768]{1,0:T(8,128)(2,1)}, bf16[96,768]{1,0:T(8,128)(2,1)}) custom-call(s32[2]{0:T(128)S(1)} %get-tuple-element.48.position_ref, s32[24]{0:T(128)S(1)} %get-tuple-element.49.mapping_ref, bf16[384,768]{1,0:T(8,128)(2,1)S(1)} %get-tuple-element.50.own_ref, ...), custom_call_target="tpu_custom_call" | custom-call | flops 1000 | bytes 1000 | tf_op jit(solution)/shard_map/cond/branch_1_fun/pallas_call | solution.py:218
  62.4 0.0 collective-permute-start.6
  62.4 1.9 %collective-permute-start.7 = (bf16[96,768]{1,0:T(8,128)(2,1)}, bf16[96,768]{1,0:T(8,128)(2,1)}, u32[]{:S(2)}, u32[]{:S(2)}) collective-permute-start(bf16[96,768]{1,0:T(8,128)(2,1)} %get-tuple-element.55), channel_id=1, source_target_pairs={{0,2},{1,3},{2,0},{3,1},{4,6},{5,7},{6,4},{7,5},{8,10},{9,11},{10,... | collective-permute-start | bytes 442376 | tf_op jit(solution)/shard_map/cond/branch_1_fun/ppermute | solution.py:304
  64.2 0.1 collective-permute-start.8
  64.4 0.0 collective-permute-done.6
  64.4 5.0 %collective-permute-done.7 = bf16[96,768]{1,0:T(8,128)(2,1)} collective-permute-done((bf16[96,768]{1,0:T(8,128)(2,1)}, bf16[96,768]{1,0:T(8,128)(2,1)}, u32[]{:S(2)}, u32[]{:S(2)}) %collective-permute-start.7) | collective-permute-done | bytes 147488 | tf_op jit(solution)/shard_map/cond/branch_1_fun/ppermute | solution.py:304
  69.4 2.5 %collective-permute-done.8 = bf16[96,768]{1,0:T(8,128)(2,1)} collective-permute-done((bf16[96,768]{1,0:T(8,128)(2,1)}, bf16[96,768]{1,0:T(8,128)(2,1)}, u32[]{:S(2)}, u32[]{:S(2)}) %collective-permute-start.8) | collective-permute-done | bytes 147488 | tf_op jit(solution)/shard_map/cond/branch_1_fun/ppermute | solution.py:304
  71.9 0.0 collective-permute-done.9.arrived_ref
  71.9 0.0 copy-start
  71.9 0.7 copy-done
  72.6 1.9 %shard_map.88 = (bf16[96,512]{1,0:T(8,128)(2,1)}, bf16[96,512]{1,0:T(8,128)(2,1)}, bf16[96,512]{1,0:T(8,128)(2,1)}, bf16[96,512]{1,0:T(8,128)(2,1)}) custom-call(s32[2]{0:T(128)S(1)} %pad_add_fusion.refs_0_.position_ref, s32[24]{0:T(128)S(1)} %copy-done.4, bf16[384,512]{1,0:T(8,128)(2,1)} %get-tuple-element.93.own_ref, bf16[256,512]{1,0:T(8,128)(2,1)} %copy-done, ...), custom_call_target="tpu_custom_call" | custom-call | flops 1000 | bytes 1000 | tf_op jit(solution)/shard_map/pallas_call | solution.py:218
  74.5 0.2 collective-permute-start.13
  74.7 1.7 %collective-permute-start.14 = (bf16[96,512]{1,0:T(8,128)(2,1)}, bf16[96,512]{1,0:T(8,128)(2,1)S(1)}, u32[]{:S(2)}, u32[]{:S(2)}) collective-permute-start(bf16[96,512]{1,0:T(8,128)(2,1)} %get-tuple-element.104), channel_id=1, source_target_pairs={{0,2},{1,3},{2,0},{3,1},{4,6},{5,7},{6,4},{7,5},{8,10},{9,11},{10,... | collective-permute-start | bytes 294920 | tf_op jit(solution)/shard_map/ppermute | solution.py:304
  76.4 0.0 collective-permute-start.15
  76.4 2.6 %shard_map.89 = (bf16[96,8192]{1,0:T(8,128)(2,1)}, bf16[96,1024]{1,0:T(8,128)(2,1)}, bf16[96,1024]{1,0:T(8,128)(2,1)}) custom-call(s32[2]{0:T(128)S(1)} %pad_add_fusion.refs_0_.position_ref, bf16[96,512]{1,0:T(8,128)(2,1)S(1)} %get-tuple-element.99.refs_0_, bf16[96,512]{1,0:T(8,128)(2,1)} %get-tuple-element.106.refs_1_, ...), custom_call_target="tpu_custom_call" | custom-call | flops 1000 | bytes 1000 | tf_op jit(solution)/shard_map/pallas_call | solution.py:255
  79.1 0.0 collective-permute-done.13.refs_1_
  79.1 0.0 copy-start.1
  79.1 1.1 %collective-permute-done.14.refs_2_ = bf16[96,512]{1,0:T(8,128)(2,1)S(1)} collective-permute-done((bf16[96,512]{1,0:T(8,128)(2,1)}, bf16[96,512]{1,0:T(8,128)(2,1)S(1)}, u32[]{:S(2)}, u32[]{:S(2)}) %collective-permute-start.14) | collective-permute-done | bytes 98336 | tf_op jit(solution)/shard_map/ppermute | solution.py:304
  80.2 0.0 copy-start.2
  80.2 1.5 %collective-permute-done.15.refs_3_ = bf16[96,512]{1,0:T(8,128)(2,1)S(1)} collective-permute-done((bf16[96,512]{1,0:T(8,128)(2,1)}, bf16[96,512]{1,0:T(8,128)(2,1)S(1)}, u32[]{:S(2)}, u32[]{:S(2)}) %collective-permute-start.15) | collective-permute-done | bytes 98336 | tf_op jit(solution)/shard_map/ppermute | solution.py:304
  81.8 0.0 copy-start.3
  81.8 0.0 copy-done.1
  81.8 0.0 copy-done.2
  81.8 0.6 copy-done.3
  82.4 1.9 %shard_map.90 = (bf16[96,8192]{1,0:T(8,128)(2,1)}, bf16[96,1024]{1,0:T(8,128)(2,1)}, bf16[96,1024]{1,0:T(8,128)(2,1)}) custom-call(s32[2]{0:T(128)S(1)} %pad_add_fusion.refs_0_.position_ref, bf16[96,512]{1,0:T(8,128)(2,1)} %get-tuple-element.102.refs_0_, bf16[96,512]{1,0:T(8,128)(2,1)} %copy-done.1, ...), custom_call_target="tpu_custom_call", output_to_operand_aliasing={{0}: (5, {}), {1}: (6, {}), {2}: (7, {})} | custom-call | flops 1000 | bytes 1000 | tf_op jit(solution)/shard_map/pallas_call | solution.py:255
Async XLA Ops:
  0.7 8.0 %copy-start.4 = (s32[24]{0:T(128)S(1)}, s32[24]{0:T(128)}, u32[]{:S(2)}) copy-start(s32[24]{0:T(128)} %mapping_ref.1) | copy-start | bytes 292
  4.6 33.9 %collective-permute-start.12 = (bf16[256,512]{1,0:T(8,128)(2,1)}, bf16[256,512]{1,0:T(8,128)(2,1)S(1)}, u32[]{:S(2)}, u32[]{:S(2)}) collective-permute-start(bf16[256,512]{1,0:T(8,128)(2,1)} %get-tuple-element.98), channel_id=1, source_target_pairs={{0,16},{4,20},{8,24},{12,28},{16,0},{20,4},{24,8},{28,12},{1,17},{... | collective-permute-start | bytes 786440 | tf_op jit(solution)/shard_map/ppermute | solution.py:296
  12.8 34.4 %collective-permute-start.11 = (bf16[256,768]{1,0:T(8,128)(2,1)}, bf16[256,768]{1,0:T(8,128)(2,1)S(1)}, u32[]{:S(2)}, u32[]{:S(2)}) collective-permute-start(bf16[256,768]{1,0:T(8,128)(2,1)} %get-tuple-element.97), channel_id=1, source_target_pairs={{0,16},{4,20},{8,24},{12,28},{16,0},{20,4},{24,8},{28,12},{1,17},{... | collective-permute-start | bytes 1179656 | tf_op jit(solution)/shard_map/ppermute | solution.py:296
  19.0 28.2 %copy-start.5 = (bf16[256,512]{1,0:T(8,128)(2,1)S(1)}, bf16[256,512]{1,0:T(8,128)(2,1)}, u32[]{:S(2)}) copy-start(bf16[256,512]{1,0:T(8,128)(2,1)} %get-tuple-element.94) | copy-start | bytes 786436
  19.0 41.9 %collective-permute-start.10 = (bf16[256,768]{1,0:T(8,128)(2,1)}, bf16[256,768]{1,0:T(8,128)(2,1)S(1)}, u32[]{:S(2)}, u32[]{:S(2)}) collective-permute-start(bf16[256,768]{1,0:T(8,128)(2,1)} %get-tuple-element.96), channel_id=1, source_target_pairs={{0,16},{4,20},{8,24},{12,28},{16,0},{20,4},{24,8},{28,12},{1,17},{... | collective-permute-start | bytes 1179656 | tf_op jit(solution)/shard_map/ppermute | solution.py:296
  39.8 2.0 %collective-permute-start = (bf16[96,512]{1,0:T(8,128)(2,1)}, bf16[96,512]{1,0:T(8,128)(2,1)}, u32[]{:S(2)}, u32[]{:S(2)}) collective-permute-start(bf16[96,512]{1,0:T(8,128)(2,1)} %get-tuple-element.36), channel_id=1, source_target_pairs={{0,1},{1,0},{2,3},{3,2},{4,5},{5,4},{6,7},{7,6},{8,9},{9,8},{10,11... | collective-permute-start | bytes 294920 | tf_op jit(solution)/shard_map/cond/branch_1_fun/ppermute | solution.py:304
  39.8 6.0 %collective-permute-start.1 = (bf16[96,512]{1,0:T(8,128)(2,1)}, bf16[96,512]{1,0:T(8,128)(2,1)}, u32[]{:S(2)}, u32[]{:S(2)}) collective-permute-start(bf16[96,512]{1,0:T(8,128)(2,1)} %get-tuple-element.37), channel_id=1, source_target_pairs={{0,2},{1,3},{2,0},{3,1},{4,6},{5,7},{6,4},{7,5},{8,10},{9,11},{10,... | collective-permute-start | bytes 294920 | tf_op jit(solution)/shard_map/cond/branch_1_fun/ppermute | solution.py:304
  41.7 5.5 %collective-permute-start.2 = (bf16[96,512]{1,0:T(8,128)(2,1)}, bf16[96,512]{1,0:T(8,128)(2,1)}, u32[]{:S(2)}, u32[]{:S(2)}) collective-permute-start(bf16[96,512]{1,0:T(8,128)(2,1)} %get-tuple-element.38), channel_id=1, source_target_pairs={{0,3},{1,2},{2,1},{3,0},{4,7},{5,6},{6,5},{7,4},{8,11},{9,10},{10,... | collective-permute-start | bytes 294920 | tf_op jit(solution)/shard_map/cond/branch_1_fun/ppermute | solution.py:304
  47.2 24.6 %collective-permute-start.9 = (bf16[256,512]{1,0:T(8,128)(2,1)S(1)}, bf16[256,512]{1,0:T(8,128)(2,1)S(1)}, u32[]{:S(2)}, u32[]{:S(2)}) collective-permute-start(bf16[256,512]{1,0:T(8,128)(2,1)S(1)} %copy-done.5), channel_id=1, source_target_pairs={{0,16},{4,20},{8,24},{12,28},{16,0},{20,4},{24,8},{28,12},{1,17},{... | collective-permute-start | bytes 786440 | tf_op jit(solution)/shard_map/ppermute | solution.py:296
  48.7 2.1 %collective-permute-start.3 = (bf16[96,768]{1,0:T(8,128)(2,1)}, bf16[96,768]{1,0:T(8,128)(2,1)}, u32[]{:S(2)}, u32[]{:S(2)}) collective-permute-start(bf16[96,768]{1,0:T(8,128)(2,1)} %get-tuple-element.45), channel_id=1, source_target_pairs={{0,1},{1,0},{2,3},{3,2},{4,5},{5,4},{6,7},{7,6},{8,9},{9,8},{10,11... | collective-permute-start | bytes 442376 | tf_op jit(solution)/shard_map/cond/branch_1_fun/ppermute | solution.py:304
  49.0 7.0 %collective-permute-start.4 = (bf16[96,768]{1,0:T(8,128)(2,1)}, bf16[96,768]{1,0:T(8,128)(2,1)}, u32[]{:S(2)}, u32[]{:S(2)}) collective-permute-start(bf16[96,768]{1,0:T(8,128)(2,1)} %get-tuple-element.46), channel_id=1, source_target_pairs={{0,2},{1,3},{2,0},{3,1},{4,6},{5,7},{6,4},{7,5},{8,10},{9,11},{10,... | collective-permute-start | bytes 442376 | tf_op jit(solution)/shard_map/cond/branch_1_fun/ppermute | solution.py:304
  50.8 6.9 %collective-permute-start.5 = (bf16[96,768]{1,0:T(8,128)(2,1)}, bf16[96,768]{1,0:T(8,128)(2,1)}, u32[]{:S(2)}, u32[]{:S(2)}) collective-permute-start(bf16[96,768]{1,0:T(8,128)(2,1)} %get-tuple-element.47), channel_id=1, source_target_pairs={{0,3},{1,2},{2,1},{3,0},{4,7},{5,6},{6,5},{7,4},{8,11},{9,10},{10,... | collective-permute-start | bytes 442376 | tf_op jit(solution)/shard_map/cond/branch_1_fun/ppermute | solution.py:304
  62.4 2.0 %collective-permute-start.6 = (bf16[96,768]{1,0:T(8,128)(2,1)}, bf16[96,768]{1,0:T(8,128)(2,1)}, u32[]{:S(2)}, u32[]{:S(2)}) collective-permute-start(bf16[96,768]{1,0:T(8,128)(2,1)} %get-tuple-element.54), channel_id=1, source_target_pairs={{0,1},{1,0},{2,3},{3,2},{4,5},{5,4},{6,7},{7,6},{8,9},{9,8},{10,11... | collective-permute-start | bytes 442376 | tf_op jit(solution)/shard_map/cond/branch_1_fun/ppermute | solution.py:304
  62.4 7.0 %collective-permute-start.7 = (bf16[96,768]{1,0:T(8,128)(2,1)}, bf16[96,768]{1,0:T(8,128)(2,1)}, u32[]{:S(2)}, u32[]{:S(2)}) collective-permute-start(bf16[96,768]{1,0:T(8,128)(2,1)} %get-tuple-element.55), channel_id=1, source_target_pairs={{0,2},{1,3},{2,0},{3,1},{4,6},{5,7},{6,4},{7,5},{8,10},{9,11},{10,... | collective-permute-start | bytes 442376 | tf_op jit(solution)/shard_map/cond/branch_1_fun/ppermute | solution.py:304
  64.2 7.6 %collective-permute-start.8 = (bf16[96,768]{1,0:T(8,128)(2,1)}, bf16[96,768]{1,0:T(8,128)(2,1)}, u32[]{:S(2)}, u32[]{:S(2)}) collective-permute-start(bf16[96,768]{1,0:T(8,128)(2,1)} %get-tuple-element.56), channel_id=1, source_target_pairs={{0,3},{1,2},{2,1},{3,0},{4,7},{5,6},{6,5},{7,4},{8,11},{9,10},{10,... | collective-permute-start | bytes 442376 | tf_op jit(solution)/shard_map/cond/branch_1_fun/ppermute | solution.py:304
  71.9 0.7 copy-start
  74.5 4.6 %collective-permute-start.13 = (bf16[96,512]{1,0:T(8,128)(2,1)}, bf16[96,512]{1,0:T(8,128)(2,1)S(1)}, u32[]{:S(2)}, u32[]{:S(2)}) collective-permute-start(bf16[96,512]{1,0:T(8,128)(2,1)} %get-tuple-element.103), channel_id=1, source_target_pairs={{0,1},{1,0},{2,3},{3,2},{4,5},{5,4},{6,7},{7,6},{8,9},{9,8},{10,11... | collective-permute-start | bytes 294920 | tf_op jit(solution)/shard_map/ppermute | solution.py:304
  74.7 5.5 %collective-permute-start.14 = (bf16[96,512]{1,0:T(8,128)(2,1)}, bf16[96,512]{1,0:T(8,128)(2,1)S(1)}, u32[]{:S(2)}, u32[]{:S(2)}) collective-permute-start(bf16[96,512]{1,0:T(8,128)(2,1)} %get-tuple-element.104), channel_id=1, source_target_pairs={{0,2},{1,3},{2,0},{3,1},{4,6},{5,7},{6,4},{7,5},{8,10},{9,11},{10,... | collective-permute-start | bytes 294920 | tf_op jit(solution)/shard_map/ppermute | solution.py:304
  76.4 5.3 %collective-permute-start.15 = (bf16[96,512]{1,0:T(8,128)(2,1)}, bf16[96,512]{1,0:T(8,128)(2,1)S(1)}, u32[]{:S(2)}, u32[]{:S(2)}) collective-permute-start(bf16[96,512]{1,0:T(8,128)(2,1)} %get-tuple-element.105), channel_id=1, source_target_pairs={{0,3},{1,2},{2,1},{3,0},{4,7},{5,6},{6,5},{7,4},{8,11},{9,10},{10,... | collective-permute-start | bytes 294920 | tf_op jit(solution)/shard_map/ppermute | solution.py:304
  79.1 2.7 %copy-start.1 = (bf16[96,512]{1,0:T(8,128)(2,1)}, bf16[96,512]{1,0:T(8,128)(2,1)S(1)}, u32[]{:S(2)}) copy-start(bf16[96,512]{1,0:T(8,128)(2,1)S(1)} %collective-permute-done.13.refs_1_) | copy-start | bytes 294916
  80.2 1.5 %copy-start.2 = (bf16[96,512]{1,0:T(8,128)(2,1)}, bf16[96,512]{1,0:T(8,128)(2,1)S(1)}, u32[]{:S(2)}) copy-start(bf16[96,512]{1,0:T(8,128)(2,1)S(1)} %collective-permute-done.14.refs_2_) | copy-start | bytes 294916
  81.8 0.6 copy-start.3

commit v2 on v1

--- a/solution.py
+++ b/solution.py
@@ -11,11 +11,9 @@
 HEAD_SIZE = 128
 CAP = 2
 HIDDEN = -1e30
-VMEM_LIMIT = 60 * 1024 * 1024
-KEYS_AND_VALUES = -1
+FULL_VMEM, SOME_VMEM, LITTLE_VMEM = (60 << 20, 30 << 20, 8 << 20)
 PACK = 4
 NO_COST = pl.CostEstimate(flops=1000, bytes_accessed=1000, transcendentals=0)
-PARAMS = pltpu.CompilerParams(vmem_limit_bytes=VMEM_LIMIT)
 IN_SMEM = pl.BlockSpec(memory_space=pltpu.SMEM)
 IN_VMEM = pl.BlockSpec(memory_space=pltpu.VMEM)
 ANYWHERE = pl.BlockSpec(memory_space=pl.ANY)
@@ -73,15 +71,18 @@
     return query_pieces, dscores, weights_low
 
 
-def grads_kernel(block_count, block_rows, first, last, heads, sets, *refs):
-    position_ref, starts_ref, mapping_ref, q_ref, g_ref, k_ref, v_ref, _, *refs = refs
-    if not first:
-        key_in, value_in, *refs = refs
-    outs, refs = refs[: 2 * len(sets)], refs[2 * len(sets) :]
-    if not last:
+def pairs_of(refs):
+    return list(zip(refs[::2], refs[1::2]))
+
+
+def grads_kernel(block_count, block_rows, group, first, keeps, held, heads, sets, *refs):
+    starts_ref, mapping_ref, q_ref, g_ref, k_ref, v_ref, _, *refs = refs
+    sums, refs = dict(zip(held, pairs_of(refs[: 2 * len(held)]))), refs[2 * len(held) :]
+    outs, refs = pairs_of(refs[: 2 * len(sets)]), refs[2 * len(sets) :]
+    if keeps:
         key_out, value_out, *refs = refs
     bias_ref, low_ref, key_acc, value_acc = refs
-    position = position_ref[0]
+    position = lax.axis_index("ctx")
     rows = block_count * block_rows
 
     document_row = jnp.int32(0)
@@ -96,8 +97,9 @@
         key_acc[...] = jnp.zeros_like(key_acc)
         value_acc[...] = jnp.zeros_like(value_acc)
     else:
-        key_acc[...] = key_in[...]
-        value_acc[...] = value_in[...]
+        key_acc[...] = sums[group][0][...]
+        value_acc[...] = sums[group][1][...]
+    sums[group] = (key_acc, value_acc)
 
     owned = [jnp.maximum(source, 0) for source in own_sources(mapping_ref, position, block_count)]
     moved = moved_blocks(mapping_ref, position, block_count)
@@ -113,7 +115,10 @@
                 aligned(source * block_rows, block_rows, block_rows), :
             ]
 
-    places = {unit: (outs[2 * i], outs[2 * i + 1], at) for i, units in enumerate(sets) for at, unit in enumerate(units)}
+    places = {}
+    for units, (own_ref, send_ref) in zip(sets, outs):
+        for unit in units:
+            places[unit] = (own_ref, send_ref, columns_before(units, unit) // HEAD_SIZE)
     for head in range(0, heads, PACK):
         packed = range(head, min(head + PACK, heads))
         columns = [slice(h * HEAD_SIZE, (h + 1) * HEAD_SIZE) for h in packed]
@@ -132,45 +137,57 @@
                     index * block_rows : (index + 1) * block_rows, :
                 ]
             put(*places[h])
-    if last:
-        own_ref, send_ref, at = places[KEYS_AND_VALUES]
-        low_ref[...] = (key_acc[...] * HEAD_SIZE ** (-0.5)).astype(jnp.bfloat16)
-        put(own_ref, send_ref, at)
-        low_ref[...] = value_acc[...].astype(jnp.bfloat16)
-        put(own_ref, send_ref, at + 1)
-    else:
+    for unit, (own_ref, send_ref, at) in places.items():
+        if unit < 0:
+            key_sum, value_sum = sums[group_of(unit)]
+            low_ref[...] = (key_sum[...] * HEAD_SIZE ** (-0.5)).astype(jnp.bfloat16)
+            put(own_ref, send_ref, at)
+            low_ref[...] = value_sum[...].astype(jnp.bfloat16)
+            put(own_ref, send_ref, at + 1)
+    if keeps:
         key_out[...] = key_acc[...]
         value_out[...] = value_acc[...]
 
 
-def unit_columns(units):
-    return (len(units) + units.count(KEYS_AND_VALUES)) * HEAD_SIZE
+def keys_and_values(group):
+    return -1 - group
+
+
+def group_of(unit):
+    return -1 - unit
+
+
+def columns_before(units, unit=None):
+    ahead = units if unit is None else units[: units.index(unit)]
+    return sum(HEAD_SIZE if u >= 0 else 2 * HEAD_SIZE for u in ahead)
 
 
 def grads_chunk(
-    position, starts, mapping, queries, gradient, keys, values, after, carried, start_head, heads, group, sets
+    starts, mapping, queries, gradient, keys, values, after, carried, start_head, heads, group, sets,
+    vmem=FULL_VMEM,
 ):
     rows = queries.shape[0]
     block_count = starts.shape[0]
     block_rows = rows // block_count
-    first = carried is None
-    last = any(KEYS_AND_VALUES in units for units in sets)
+    sent_groups = [group_of(u) for units in sets for u in units if u < 0]
+    held = [g for g in carried if g == group or g in sent_groups]
+    keeps = group not in sent_groups
     whole = lambda r, c: pl.BlockSpec((r, c), lambda i: (0, 0))
     cut = pl.BlockSpec((pl.Element(rows), pl.Element(heads * HEAD_SIZE)), lambda i: (0, start_head * HEAD_SIZE))
     group_spec = pl.BlockSpec((rows, HEAD_SIZE), lambda i: (0, group))
     running = jax.ShapeDtypeStruct((rows, HEAD_SIZE), jnp.float32)
     out_shape = []
     for units in sets:
-        out_shape.append(jax.ShapeDtypeStruct((rows, unit_columns(units)), jnp.bfloat16))
-        out_shape.append(jax.ShapeDtypeStruct((CAP * block_rows, unit_columns(units)), jnp.bfloat16))
-    if not last:
+        out_shape.append(jax.ShapeDtypeStruct((rows, columns_before(units)), jnp.bfloat16))
+        out_shape.append(jax.ShapeDtypeStruct((CAP * block_rows, columns_before(units)), jnp.bfloat16))
+    if keeps:
         out_shape += [running, running]
     out = pl.pallas_call(
-        functools.partial(grads_kernel, block_count, block_rows, first, last, heads, sets),
+        functools.partial(grads_kernel, block_count, block_rows, group, group not in held, keeps, held, heads, sets),
         grid=(1,),
-        in_specs=[IN_SMEM] * 3
+        in_specs=[IN_SMEM] * 2
         + [cut, cut, group_spec, group_spec, ANYWHERE]
-        + ([] if first else [whole(rows, HEAD_SIZE)] * 2),
+        + [whole(rows, HEAD_SIZE)] * (2 * len(held)),
         out_specs=[whole(*s.shape) for s in out_shape],
         out_shape=out_shape,
         scratch_shapes=[
@@ -179,11 +196,13 @@
             pltpu.VMEM((rows, HEAD_SIZE), jnp.float32),
             pltpu.VMEM((rows, HEAD_SIZE), jnp.float32),
         ],
-        compiler_params=PARAMS,
+        compiler_params=pltpu.CompilerParams(vmem_limit_bytes=vmem),
         cost_estimate=NO_COST,
-    )(position, starts, mapping, queries, gradient, keys, values, after, *(carried or ()))
-    pairs = [(out[2 * i], out[2 * i + 1]) for i in range(len(sets))]
-    return pairs, (None if last else tuple(out[2 * len(sets) :]))
+    )(starts, mapping, queries, gradient, keys, values, after, *(x for g in held for x in carried[g]))
+    carried = {g: sums for g, sums in carried.items() if g not in held}
+    if keeps:
+        carried[group] = tuple(out[2 * len(sets) :])
+    return pairs_of(out[: 2 * len(sets)]), carried
 
 
 def sort_kernel(block_count, block_rows, half_axis, peers, position_ref, mapping_ref, own_ref, arrived_ref, *refs):
@@ -220,7 +239,7 @@
         in_specs=[IN_SMEM, IN_SMEM, IN_VMEM, IN_VMEM] + [ANYWHERE] * len(after),
         out_specs=[IN_VMEM] * peers,
         out_shape=[out] * peers,
-        compiler_params=PARAMS,
+        compiler_params=pltpu.CompilerParams(vmem_limit_bytes=LITTLE_VMEM),
         cost_estimate=NO_COST,
     )(position, mapping, own, arrived, *after)
 
@@ -247,6 +266,16 @@
         copy.wait()
 
 
+def joined_parts(parts):
+    joined = []
+    for at, size, out, column in parts:
+        if joined and joined[-1][2] == out and joined[-1][0] + joined[-1][1] == at and joined[-1][3] + joined[-1][1] == column:
+            joined[-1] = (joined[-1][0], joined[-1][1] + size, out, joined[-1][3])
+        else:
+            joined.append((at, size, out, column))
+    return joined
+
+
 def place_columns(position, pieces, places, columns_here, held, peers):
     rows = pieces[0][0].shape[0]
     flat = [p for chunk in pieces for p in chunk]
@@ -259,18 +288,19 @@
         out_shape=out_shape,
         input_output_aliases={1 + len(flat) + i: i for i in range(len(held))},
         scratch_shapes=[pltpu.SemaphoreType.DMA((count,))],
-        compiler_params=PARAMS,
+        compiler_params=pltpu.CompilerParams(vmem_limit_bytes=LITTLE_VMEM),
         cost_estimate=NO_COST,
     )(position, *flat, *held)
 
 
 def plan_of(groups, repeats):
-    lead, most = max(1, repeats // 2), max(1, 3 * repeats // 4)
-    kernels = [(0, 0, lead, [list(range(lead))])]
-    kernels.append((0, lead, repeats - lead, [list(range(repeats - lead)) + [KEYS_AND_VALUES]]))
+    lead = max(1, repeats // 2)
+    heads = list(range(repeats))
+    kernels = [(0, 0, lead, [heads[:lead]]), (0, lead, repeats - lead, [heads[: repeats - lead]])]
     for group in range(1, groups):
-        heads = list(range(repeats))
-        kernels.append((group, 0, repeats, [heads[:most], heads[most:] + [KEYS_AND_VALUES]]))
+        kernels.append((group, 0, repeats, [heads[:lead], heads[lead:]]))
+    for group in range(groups):
+        kernels[-1][3].append([keys_and_values(group)])
     return kernels
 
 
@@ -285,44 +315,33 @@
     position = jnp.stack([lax.axis_index("ctx"), lax.axis_index("tensor")]).astype(jnp.int32)
     pairs = [(i, (i + half_axis) % axis_length) for i in range(axis_length)]
 
-    carried, after, sent = None, key_layout_rows, []
-    for group, start, heads, sets in plan_of(groups, repeats):
+    carried, after, sent = {}, key_layout_rows, []
+    for number, (group, start, heads, sets) in enumerate(plan_of(groups, repeats)):
         made, carried = grads_chunk(
-            position, doc_starts, block_mapping, queries, output_gradient, key_layout_rows, value_layout_rows,
-            after, carried, group * repeats + start, heads, group, sets,
+            doc_starts, block_mapping, queries, output_gradient, key_layout_rows, value_layout_rows,
+            after, carried, group * repeats + start, heads, group, sets, FULL_VMEM if number == 0 else SOME_VMEM,
         )
         after = made[0][0]
         for units, (own, send) in zip(sets, made):
-            sent.append((group, start, units, own, lax.ppermute(send, "ctx", pairs)))
+            sent.append((group * repeats + start, units, own, lax.ppermute(send, "ctx", pairs)))
 
     order, pieces, places = [after], [], []
-    for group, start, units, own, arrived in sent:
-
-        def exchange(own, arrived, *order):
-            parts = sort_rows(position, block_mapping, own, arrived, order, block_count, half_axis, peers)
-            return [parts[0]] + [
-                lax.ppermute(parts[hop], "tensor", [(i, i ^ hop) for i in range(peers)]) for hop in range(1, peers)
-            ]
-
-        def nothing(own, arrived, *order):
-            return [jnp.zeros((rows // peers, own.shape[1]), own.dtype)] * peers
-
-        if len(pieces) < len(sent) - 1:
-            got = lax.cond(block_mapping[0] >= 0, exchange, nothing, own, arrived, *order)
-        else:
-            got = exchange(own, arrived, *order)
-        order = [got[0]]
+    for start, units, own, arrived in sent:
+        parts = sort_rows(position, block_mapping, own, arrived, order, block_count, half_axis, peers)
+        got = [parts[0]] + [
+            lax.ppermute(parts[hop], "tensor", [(i, i ^ hop) for i in range(peers)]) for hop in range(1, peers)
+        ]
+        order = [got[0]] + (list(pieces[-1][1:]) if pieces else [])
         pieces.append(got)
-        parts, at = [], 0
-        queries_here = [u for u in units if u != KEYS_AND_VALUES]
-        if queries_here:
-            size = len(queries_here) * HEAD_SIZE
-            parts.append((0, size, 0, (group * repeats + start + queries_here[0]) * HEAD_SIZE))
-            at = size
-        if KEYS_AND_VALUES in units:
-            parts.append((at, HEAD_SIZE, 1, group * HEAD_SIZE))
-            parts.append((at + HEAD_SIZE, HEAD_SIZE, 2, group * HEAD_SIZE))
-        places.append(parts)
+        parts = []
+        for unit in units:
+            at = columns_before(units, unit)
+            if unit >= 0:
+                parts.append((at, HEAD_SIZE, 0, (start + unit) * HEAD_SIZE))
+            else:
+                parts.append((at, HEAD_SIZE, 1, group_of(unit) * HEAD_SIZE))
+                parts.append((at + HEAD_SIZE, HEAD_SIZE, 2, group_of(unit) * HEAD_SIZE))
+        places.append(joined_parts(parts))
     columns_here = [queries.shape[1], key_layout_rows.shape[1], value_layout_rows.shape[1]]
     held = []
     if len(pieces) > 1:

time: 84.6 us -> 77.2 us (0.913)
  waiting for transfers between devices: 42.2 us -> 27.8 us
  local copies, waits for them, and re-layouts: 1.35 us -> 8.29 us
  Pallas kernels: 24.8 us -> 19.9 us
  starting transfers between devices: 15 us -> 19.5 us
    ppermute x16 -> x24, waiting for transfers between devices: 42.2 us -> 27.8 us  [the longest x6 22.8 us: on_device(): lax.ppermute(send, 'ctx', pairs)]
    unnamed x12 -> x46, local copies, waits for them, and re-layouts: 1.35 us -> 8.29 us
    ppermute x16 -> x24, starting transfers between devices: 15 us -> 19.5 us  [the longest x18 12 us: on_device(): lax.ppermute(parts[hop], 'tensor', [(i, i ^ hop) for i in range(peers)])]
    pallas_call x3, Pallas kernels: 14.2 us -> 11.8 us  [grads_chunk(): pl.pallas_call(functools.partial(grads_kernel, block_count, block_rows, g...]
    pallas_call x2, Pallas kernels: 4.52 us -> 3.23 us  [place_columns(): pl.pallas_call(functools.partial(place_kernel, peers, columns_here, place...]
    pallas_call x4 -> x6, Pallas kernels: 6.08 us -> 4.93 us  [sort_rows(): pl.pallas_call(functools.partial(sort_kernel, block_count, rows // block_...]
  transfers between devices with their start and end apart: 16 -> 24, of which waited for: 10 -> 10; matrix products, arithmetic and copies ran while one was open for 0% -> 0% of each run, Pallas kernels for 20% -> 19%
where the time goes in v2:
time: 77.2 us; the launch traced here: 76.4 us
  waiting for transfers between devices  27.8 us (36%)
  Pallas kernels  19.9 us (26%)
  starting transfers between devices  19.5 us (25%)
  local copies, waits for them, and re-layouts  8.29 us (11%)
  between operations  0.84 us (1%)
    ppermute x6, waiting for transfers between devices, on_device(): lax.ppermute(send, 'ctx', pairs)  22.8 us
    ppermute x18, starting transfers between devices, on_device(): lax.ppermute(parts[hop], 'tensor', [(i, i ^ hop) for i in range(peers)])  12 us
    pallas_call x3, Pallas kernels, grads_chunk(): pl.pallas_call(functools.partial(grads_kernel, block_count, block_rows, g...  11.8 us
    unnamed x46, local copies, waits for them, and re-layouts  8.29 us
    ppermute x6, starting transfers between devices, on_device(): lax.ppermute(send, 'ctx', pairs)  7.54 us
    pallas_call x6, Pallas kernels, sort_rows(): pl.pallas_call(functools.partial(sort_kernel, block_count, rows // block_...  4.93 us
    ppermute x18, waiting for transfers between devices, on_device(): lax.ppermute(parts[hop], 'tensor', [(i, i ^ hop) for i in range(peers)])  4.91 us
    pallas_call x2, Pallas kernels, place_columns(): pl.pallas_call(functools.partial(place_kernel, peers, columns_here, place...  3.23 us
  transfers between devices with their start and end apart: 24, of which 10 were waited for; matrix products, arithmetic and copies ran while one was open for 0% of the time, Pallas kernels for 19%

profile of v2, /device:TPU:0, one launch (start us, length us, event | category | flops | bytes accessed | tf_op | source)
XLA Modules:
  0.0 76.4 jit_solution(6758773169895787820)
XLA Ops:
  0.6 0.0 copy-start.14
  0.6 0.0 copy-start.17
  0.7 4.0 %shard_map.85 = (bf16[384,512]{1,0:T(8,128)(2,1)}, bf16[256,512]{1,0:T(8,128)(2,1)}, f32[384,128]{1,0:T(8,128)}, f32[384,128]{1,0:T(8,128)}) custom-call(s32[3]{0:T(128)} %refs_0_.5, s32[24]{0:T(128)} %mapping_ref.11, bf16[384,2048]{1,0:T(8,128)(2,1)} %refs_2_.5, bf16[384,2048]{1,0:T(8,128)(2,1)} %refs_3_.5, bf16[384,256]{1,0:T(8,128)(2,1)} %refs_4_.5, ...), custom_call_target="tpu_custom_call" | custom-call | flops 1000 | bytes 1000 | tf_op jit(solution)/shard_map/pallas_call | solution.py:185
  4.7 4.0 %collective-permute-start.5 = (bf16[256,512]{1,0:T(8,128)(2,1)}, bf16[256,512]{1,0:T(8,128)(2,1)}, u32[]{:S(2)}, u32[]{:S(2)}) collective-permute-start(bf16[256,512]{1,0:T(8,128)(2,1)} %get-tuple-element.61), channel_id=1, source_target_pairs={{0,16},{4,20},{8,24},{12,28},{16,0},{20,4},{24,8},{28,12},{1,17},{... | collective-permute-start | bytes 786440 | tf_op jit(solution)/shard_map/ppermute | solution.py:326
  8.8 0.0 copy-start.6
  8.8 1.0 %copy-done.6 = bf16[384,512]{1,0:T(8,128)(2,1)S(1)} copy-done((bf16[384,512]{1,0:T(8,128)(2,1)S(1)}, bf16[384,512]{1,0:T(8,128)(2,1)}, u32[]{:S(2)}) %copy-start.6) | copy-done | bytes 393240
  9.8 0.9 %copy-done.10 = f32[384,128]{1,0:T(8,128)S(1)} copy-done((f32[384,128]{1,0:T(8,128)S(1)}, f32[384,128]{1,0:T(8,128)}, u32[]{:S(2)}) %copy-start.10) | copy-done | bytes 196632
  10.7 0.9 %copy-done.11 = f32[384,128]{1,0:T(8,128)S(1)} copy-done((f32[384,128]{1,0:T(8,128)S(1)}, f32[384,128]{1,0:T(8,128)}, u32[]{:S(2)}) %copy-start.11) | copy-done | bytes 196632
  11.7 2.9 %shard_map.86 = (bf16[384,512]{1,0:T(8,128)(2,1)S(1)}, bf16[256,512]{1,0:T(8,128)(2,1)}, f32[384,128]{1,0:T(8,128)S(1)}, f32[384,128]{1,0:T(8,128)S(1)}) custom-call(s32[3]{0:T(128)S(1)} %copy-done.17, s32[24]{0:T(128)S(1)} %copy-done.14, bf16[384,2048]{1,0:T(8,128)(2,1)S(1)} %copy-done, bf16[384,2048]{1,0:T(8,128)(2,1)S(1)} %copy-done.1, ...), custom_call_target="tpu_custom_call" | custom-call | flops 1000 | bytes 1000 | tf_op jit(solution)/shard_map/pallas_call | solution.py:185
  14.5 0.0 collective-permute-start.4
  14.5 4.9 %shard_map.87 = (bf16[384,512]{1,0:T(8,128)(2,1)S(1)}, bf16[256,512]{1,0:T(8,128)(2,1)}, bf16[384,512]{1,0:T(8,128)(2,1)S(1)}, bf16[256,512]{1,0:T(8,128)(2,1)},...) custom-call(s32[3]{0:T(128)S(1)} %copy-done.18, ...), custom_call_target="tpu_custom_call" | custom-call | flops 1000 | bytes 1000 | tf_op jit(solution)/shard_map/pallas_call | solution.py:185
  19.4 0.8 copy-done.8
  20.2 0.7 copy-done.12
  20.9 0.7 copy-done.19
  21.5 0.6 copy-done.21
  22.2 2.9 %collective-permute-start.3 = (bf16[256,512]{1,0:T(8,128)(2,1)}, bf16[256,512]{1,0:T(8,128)(2,1)S(1)}, u32[]{:S(2)}, u32[]{:S(2)}) collective-permute-start(bf16[256,512]{1,0:T(8,128)(2,1)} %get-tuple-element.59), channel_id=1, source_target_pairs={{0,16},{4,20},{8,24},{12,28},{16,0},{20,4},{24,8},{28,12},{1,17},{... | collective-permute-start | bytes 786440 | tf_op jit(solution)/shard_map/ppermute | solution.py:326
  25.1 0.0 collective-permute-start.2
  25.1 0.1 pad_add_fusion.position_ref
  25.2 13.5 %collective-permute-done.5.arrived_ref = bf16[256,512]{1,0:T(8,128)(2,1)} collective-permute-done((bf16[256,512]{1,0:T(8,128)(2,1)}, bf16[256,512]{1,0:T(8,128)(2,1)}, u32[]{:S(2)}, u32[]{:S(2)}) %collective-permute-start.5) | collective-permute-done | bytes 262176 | tf_op jit(solution)/shard_map/ppermute | solution.py:326
  38.7 1.0 %copy-done.7 = bf16[384,512]{1,0:T(8,128)(2,1)S(1)} copy-done((bf16[384,512]{1,0:T(8,128)(2,1)S(1)}, bf16[384,512]{1,0:T(8,128)(2,1)}, u32[]{:S(2)}) %copy-start.7) | copy-done | bytes 393240
  39.7 0.7 copy-done.16
  40.4 1.2 %shard_map.88 = (bf16[96,512]{1,0:T(8,128)(2,1)S(1)}, bf16[96,512]{1,0:T(8,128)(2,1)S(1)}, bf16[96,512]{1,0:T(8,128)(2,1)S(1)}, bf16[96,512]{1,0:T(8,128)(2,1)S(1)}) custom-call(s32[2]{0:T(128)S(1)} %pad_add_fusion.position_ref, s32[24]{0:T(128)S(1)} %copy-done.16, bf16[384,512]{1,0:T(8,128)(2,1)S(1)} %copy-done.7, ...), custom_call_target="tpu_custom_call" | custom-call | flops 1000 | bytes 1000 | tf_op jit(solution)/shard_map/pallas_call | solution.py:237
  41.5 0.1 collective-permute-start.6
  41.6 1.9 %collective-permute-start.7 = (bf16[96,512]{1,0:T(8,128)(2,1)S(1)}, bf16[96,512]{1,0:T(8,128)(2,1)S(1)}, u32[]{:S(2)}, u32[]{:S(2)}) collective-permute-start(bf16[96,512]{1,0:T(8,128)(2,1)S(1)} %get-tuple-element.65), channel_id=1, source_target_pairs={{0,2},{1,3},{2,0},{3,1},{4,6},{5,7},{6,4},{7,5},{8,10},{9,11},{10,... | collective-permute-start | bytes 294920 | tf_op jit(solution)/shard_map/ppermute | solution.py:332
  43.5 0.8 %collective-permute-done.4.arrived_ref = bf16[256,512]{1,0:T(8,128)(2,1)} collective-permute-done((bf16[256,512]{1,0:T(8,128)(2,1)}, bf16[256,512]{1,0:T(8,128)(2,1)}, u32[]{:S(2)}, u32[]{:S(2)}) %collective-permute-start.4) | collective-permute-done | bytes 262176 | tf_op jit(solution)/shard_map/ppermute | solution.py:326
  44.3 0.0 collective-permute-start.8
  44.3 1.0 %copy-done.5 = bf16[384,512]{1,0:T(8,128)(2,1)S(1)} copy-done((bf16[384,512]{1,0:T(8,128)(2,1)S(1)}, bf16[384,512]{1,0:T(8,128)(2,1)}, u32[]{:S(2)}) %copy-start.5) | copy-done | bytes 393240
  45.3 1.1 %shard_map.89 = (bf16[96,512]{1,0:T(8,128)(2,1)S(1)}, bf16[96,512]{1,0:T(8,128)(2,1)S(1)}, bf16[96,512]{1,0:T(8,128)(2,1)S(1)}, bf16[96,512]{1,0:T(8,128)(2,1)S(1)}) custom-call(s32[2]{0:T(128)S(1)} %pad_add_fusion.position_ref, s32[24]{0:T(128)S(1)} %copy-done.16, bf16[384,512]{1,0:T(8,128)(2,1)S(1)} %copy-done.5, ...), custom_call_target="tpu_custom_call" | custom-call | flops 1000 | bytes 1000 | tf_op jit(solution)/shard_map/pallas_call | solution.py:237
  46.4 3.4 %collective-permute-done.3.arrived_ref = bf16[256,512]{1,0:T(8,128)(2,1)S(1)} collective-permute-done((bf16[256,512]{1,0:T(8,128)(2,1)}, bf16[256,512]{1,0:T(8,128)(2,1)S(1)}, u32[]{:S(2)}, u32[]{:S(2)}) %collective-permute-start.3) | collective-permute-done | bytes 262176 | tf_op jit(solution)/shard_map/ppermute | solution.py:326
  49.8 0.0 collective-permute-start.9
  49.8 0.0 collective-permute-done.6.refs_1_
  49.8 1.9 %collective-permute-start.10 = (bf16[96,512]{1,0:T(8,128)(2,1)S(1)}, bf16[96,512]{1,0:T(8,128)(2,1)S(1)}, u32[]{:S(2)}, u32[]{:S(2)}) collective-permute-start(bf16[96,512]{1,0:T(8,128)(2,1)S(1)} %get-tuple-element.69), channel_id=1, source_target_pairs={{0,2},{1,3},{2,0},{3,1},{4,6},{5,7},{6,4},{7,5},{8,10},{9,11},{10,... | collective-permute-start | bytes 294920 | tf_op jit(solution)/shard_map/ppermute | solution.py:332
  51.7 0.2 collective-permute-start.11
  51.9 0.0 collective-permute-done.8.refs_3_
  51.9 0.7 shard_map.90
  52.6 2.0 %collective-permute-done.2.arrived_ref = bf16[256,512]{1,0:T(8,128)(2,1)S(1)} collective-permute-done((bf16[256,512]{1,0:T(8,128)(2,1)}, bf16[256,512]{1,0:T(8,128)(2,1)S(1)}, u32[]{:S(2)}, u32[]{:S(2)}) %collective-permute-start.2) | collective-permute-done | bytes 262176 | tf_op jit(solution)/shard_map/ppermute | solution.py:326
  54.6 0.0 collective-permute-start.12
  54.6 0.0 collective-permute-done.9.refs_1_.refs_5_
  54.6 1.6 %collective-permute-start.13 = (bf16[96,512]{1,0:T(8,128)(2,1)S(1)}, bf16[96,512]{1,0:T(8,128)(2,1)S(1)}, u32[]{:S(2)}, u32[]{:S(2)}) collective-permute-start(bf16[96,512]{1,0:T(8,128)(2,1)S(1)} %get-tuple-element.73), channel_id=1, source_target_pairs={{0,2},{1,3},{2,0},{3,1},{4,6},{5,7},{6,4},{7,5},{8,10},{9,11},{10,... | collective-permute-start | bytes 294920 | tf_op jit(solution)/shard_map/ppermute | solution.py:332
  56.2 0.3 collective-permute-start.14
  56.5 0.4 collective-permute-done.11.refs_3_.refs_7_
  56.9 0.5 collective-permute-start
  57.5 0.7 shard_map.91
  58.1 3.1 %collective-permute-done.1.arrived_ref = bf16[256,256]{1,0:T(8,128)(2,1)S(1)} collective-permute-done((bf16[256,256]{1,0:T(8,128)(2,1)S(1)}, bf16[256,256]{1,0:T(8,128)(2,1)S(1)}, u32[]{:S(2)}, u32[]{:S(2)}) %collective-permute-start.1) | collective-permute-done | bytes 131104 | tf_op jit(solution)/shard_map/ppermute | solution.py:326
  61.3 0.0 collective-permute-start.15
  61.3 0.0 collective-permute-done.12.refs_1_.refs_9_
  61.3 1.6 %collective-permute-start.16 = (bf16[96,512]{1,0:T(8,128)(2,1)S(1)}, bf16[96,512]{1,0:T(8,128)(2,1)S(1)}, u32[]{:S(2)}, u32[]{:S(2)}) collective-permute-start(bf16[96,512]{1,0:T(8,128)(2,1)S(1)} %get-tuple-element.77), channel_id=1, source_target_pairs={{0,2},{1,3},{2,0},{3,1},{4,6},{5,7},{6,4},{7,5},{8,10},{9,11},{10,... | collective-permute-start | bytes 294920 | tf_op jit(solution)/shard_map/ppermute | solution.py:332
  62.9 0.3 collective-permute-start.17
  63.1 0.0 collective-permute-done.14.refs_3_.refs_11_
  63.1 0.7 shard_map.92
  63.8 0.3 collective-permute-start.21
  64.2 0.0 collective-permute-done.arrived_ref
  64.2 1.6 %collective-permute-start.22 = (bf16[96,256]{1,0:T(8,128)(2,1)S(1)}, bf16[96,256]{1,0:T(8,128)(2,1)S(1)}, u32[]{:S(2)}, u32[]{:S(2)}) collective-permute-start(bf16[96,256]{1,0:T(8,128)(2,1)S(1)} %get-tuple-element.84), channel_id=1, source_target_pairs={{0,2},{1,3},{2,0},{3,1},{4,6},{5,7},{6,4},{7,5},{8,10},{9,11},{10,... | collective-permute-start | bytes 147464 | tf_op jit(solution)/shard_map/ppermute | solution.py:332
  65.7 0.0 collective-permute-done.15.refs_1_.refs_13_
  65.7 0.0 collective-permute-start.23
  65.8 1.1 %collective-permute-done.16.refs_2_.refs_14_ = bf16[96,512]{1,0:T(8,128)(2,1)S(1)} collective-permute-done((bf16[96,512]{1,0:T(8,128)(2,1)S(1)}, bf16[96,512]{1,0:T(8,128)(2,1)S(1)}, u32[]{:S(2)}, u32[]{:S(2)}) %collective-permute-start.16) | collective-permute-done | bytes 98336 | tf_op jit(solution)/shard_map/ppermute | solution.py:332
  66.9 1.3 %collective-permute-done.17.refs_3_.refs_15_ = bf16[96,512]{1,0:T(8,128)(2,1)S(1)} collective-permute-done((bf16[96,512]{1,0:T(8,128)(2,1)S(1)}, bf16[96,512]{1,0:T(8,128)(2,1)S(1)}, u32[]{:S(2)}, u32[]{:S(2)}) %collective-permute-start.17) | collective-permute-done | bytes 98336 | tf_op jit(solution)/shard_map/ppermute | solution.py:332
  68.2 0.7 shard_map.93
  68.9 0.7 collective-permute-start.18
  69.5 1.6 %collective-permute-start.19 = (bf16[96,256]{1,0:T(8,128)(2,1)S(1)}, bf16[96,256]{1,0:T(8,128)(2,1)S(1)}, u32[]{:S(2)}, u32[]{:S(2)}) collective-permute-start(bf16[96,256]{1,0:T(8,128)(2,1)S(1)} %get-tuple-element.81), channel_id=1, source_target_pairs={{0,2},{1,3},{2,0},{3,1},{4,6},{5,7},{6,4},{7,5},{8,10},{9,11},{10,... | collective-permute-start | bytes 147464 | tf_op jit(solution)/shard_map/ppermute | solution.py:332
  71.1 2.0 %shard_map.94 = (bf16[96,8192]{1,0:T(8,128)(2,1)}, bf16[96,1024]{1,0:T(8,128)(2,1)}, bf16[96,1024]{1,0:T(8,128)(2,1)}) custom-call(s32[2]{0:T(128)S(1)} %pad_add_fusion.position_ref, bf16[96,512]{1,0:T(8,128)(2,1)S(1)} %get-tuple-element.62.refs_0_, bf16[96,512]{1,0:T(8,128)(2,1)S(1)} %collective-permute-done.6.refs_1_, ...), custom_call_target="tpu_custom_call" | custom-call | flops 1000 | bytes 1000 | tf_op jit(solution)/shard_map/pallas_call | solution.py:284
  73.1 0.5 collective-permute-done.19.refs_2_
  73.6 1.5 %collective-permute-done.20.refs_3_ = bf16[96,256]{1,0:T(8,128)(2,1)S(1)} collective-permute-done((bf16[96,256]{1,0:T(8,128)(2,1)S(1)}, bf16[96,256]{1,0:T(8,128)(2,1)S(1)}, u32[]{:S(2)}, u32[]{:S(2)}) %collective-permute-start.20) | collective-permute-done | bytes 49184 | tf_op jit(solution)/shard_map/ppermute | solution.py:332
  75.1 1.3 %shard_map.95 = (bf16[96,8192]{1,0:T(8,128)(2,1)}, bf16[96,1024]{1,0:T(8,128)(2,1)}, bf16[96,1024]{1,0:T(8,128)(2,1)}) custom-call(s32[2]{0:T(128)S(1)} %pad_add_fusion.position_ref, bf16[96,256]{1,0:T(8,128)(2,1)S(1)} %get-tuple-element.79.refs_0_, ...), custom_call_target="tpu_custom_call", output_to_operand_aliasing={{0}: (5, {}), {1}: (6, {}), {2}: (7, {})} | custom-call | flops 1000 | bytes 1000 | tf_op jit(solution)/shard_map/pallas_call | solution.py:284
  (42 shorter events, 0.1 us)
Async XLA Ops:
  0.6 8.1 %copy-start.14 = (s32[24]{0:T(128)S(1)}, s32[24]{0:T(128)}, u32[]{:S(2)}) copy-start(s32[24]{0:T(128)} %mapping_ref.11) | copy-start | bytes 292
  0.6 8.1 %copy-start.17 = (s32[3]{0:T(128)S(1)}, s32[3]{0:T(128)}, u32[]{:S(2)}) copy-start(s32[3]{0:T(128)} %refs_0_.5) | copy-start | bytes 40
  0.7 8.1 %copy-start.1 = (bf16[384,2048]{1,0:T(8,128)(2,1)S(1)}, bf16[384,2048]{1,0:T(8,128)(2,1)}, u32[]{:S(2)}) copy-start(bf16[384,2048]{1,0:T(8,128)(2,1)} %refs_3_.5) | copy-start | bytes 4718596
  0.7 8.1 %copy-start.3 = (bf16[384,256]{1,0:T(8,128)(2,1)S(1)}, bf16[384,256]{1,0:T(8,128)(2,1)}, u32[]{:S(2)}) copy-start(bf16[384,256]{1,0:T(8,128)(2,1)} %refs_5_.5) | copy-start | bytes 589828
  0.7 8.1 %copy-start.2 = (bf16[384,256]{1,0:T(8,128)(2,1)S(1)}, bf16[384,256]{1,0:T(8,128)(2,1)}, u32[]{:S(2)}) copy-start(bf16[384,256]{1,0:T(8,128)(2,1)} %refs_4_.5) | copy-start | bytes 589828
  0.7 8.1 %copy-start = (bf16[384,2048]{1,0:T(8,128)(2,1)S(1)}, bf16[384,2048]{1,0:T(8,128)(2,1)}, u32[]{:S(2)}) copy-start(bf16[384,2048]{1,0:T(8,128)(2,1)} %refs_2_.5) | copy-start | bytes 4718596
  4.7 34.0 %collective-permute-start.5 = (bf16[256,512]{1,0:T(8,128)(2,1)}, bf16[256,512]{1,0:T(8,128)(2,1)}, u32[]{:S(2)}, u32[]{:S(2)}) collective-permute-start(bf16[256,512]{1,0:T(8,128)(2,1)} %get-tuple-element.61), channel_id=1, source_target_pairs={{0,16},{4,20},{8,24},{12,28},{16,0},{20,4},{24,8},{28,12},{1,17},{... | collective-permute-start | bytes 786440 | tf_op jit(solution)/shard_map/ppermute | solution.py:326
  8.8 1.0 %copy-start.6 = (bf16[384,512]{1,0:T(8,128)(2,1)S(1)}, bf16[384,512]{1,0:T(8,128)(2,1)}, u32[]{:S(2)}) copy-start(bf16[384,512]{1,0:T(8,128)(2,1)} %get-tuple-element.46.refs_6_.own_ref) | copy-start | bytes 1179652
  9.8 0.9 %copy-start.10 = (f32[384,128]{1,0:T(8,128)S(1)}, f32[384,128]{1,0:T(8,128)}, u32[]{:S(2)}) copy-start(f32[384,128]{1,0:T(8,128)} %get-tuple-element.47.refs_7_) | copy-start | bytes 589828
  10.7 0.9 %copy-start.11 = (f32[384,128]{1,0:T(8,128)S(1)}, f32[384,128]{1,0:T(8,128)}, u32[]{:S(2)}) copy-start(f32[384,128]{1,0:T(8,128)} %get-tuple-element.48.refs_8_) | copy-start | bytes 589828
  11.7 2.9 %copy-start.15 = (s32[24]{0:T(128)S(1)}, s32[24]{0:T(128)}, u32[]{:S(2)}) copy-start(s32[24]{0:T(128)} %mapping_ref.11) | copy-start | bytes 292
  11.7 2.9 %copy-start.18 = (s32[3]{0:T(128)S(1)}, s32[3]{0:T(128)}, u32[]{:S(2)}) copy-start(s32[3]{0:T(128)} %refs_0_.5) | copy-start | bytes 40
  14.5 4.9 %copy-start.4 = (bf16[384,512]{1,0:T(8,128)(2,1)}, bf16[384,512]{1,0:T(8,128)(2,1)S(1)}, u32[]{:S(2)}) copy-start(bf16[384,512]{1,0:T(8,128)(2,1)S(1)} %get-tuple-element.49.refs_6_.own_ref) | copy-start | bytes 1179652
  14.5 29.8 %collective-permute-start.4 = (bf16[256,512]{1,0:T(8,128)(2,1)}, bf16[256,512]{1,0:T(8,128)(2,1)}, u32[]{:S(2)}, u32[]{:S(2)}) collective-permute-start(bf16[256,512]{1,0:T(8,128)(2,1)} %get-tuple-element.60), channel_id=1, source_target_pairs={{0,16},{4,20},{8,24},{12,28},{16,0},{20,4},{24,8},{28,12},{1,17},{... | collective-permute-start | bytes 786440 | tf_op jit(solution)/shard_map/ppermute | solution.py:326
  19.4 0.8 %copy-start.8 = (bf16[384,512]{1,0:T(8,128)(2,1)}, bf16[384,512]{1,0:T(8,128)(2,1)S(1)}, u32[]{:S(2)}) copy-start(bf16[384,512]{1,0:T(8,128)(2,1)S(1)} %get-tuple-element.56.own_ref) | copy-start | bytes 1179652
  20.2 0.7 copy-start.12
  20.9 0.7 copy-start.19
  21.5 0.6 copy-start.21
  22.2 27.7 %collective-permute-start.3 = (bf16[256,512]{1,0:T(8,128)(2,1)}, bf16[256,512]{1,0:T(8,128)(2,1)S(1)}, u32[]{:S(2)}, u32[]{:S(2)}) collective-permute-start(bf16[256,512]{1,0:T(8,128)(2,1)} %get-tuple-element.59), channel_id=1, source_target_pairs={{0,16},{4,20},{8,24},{12,28},{16,0},{20,4},{24,8},{28,12},{1,17},{... | collective-permute-start | bytes 786440 | tf_op jit(solution)/shard_map/ppermute | solution.py:326
  25.1 29.5 %collective-permute-start.2 = (bf16[256,512]{1,0:T(8,128)(2,1)}, bf16[256,512]{1,0:T(8,128)(2,1)S(1)}, u32[]{:S(2)}, u32[]{:S(2)}) collective-permute-start(bf16[256,512]{1,0:T(8,128)(2,1)} %get-tuple-element.57), channel_id=1, source_target_pairs={{0,16},{4,20},{8,24},{12,28},{16,0},{20,4},{24,8},{28,12},{1,17},{... | collective-permute-start | bytes 786440 | tf_op jit(solution)/shard_map/ppermute | solution.py:326
  38.7 1.0 %copy-start.7 = (bf16[384,512]{1,0:T(8,128)(2,1)S(1)}, bf16[384,512]{1,0:T(8,128)(2,1)}, u32[]{:S(2)}) copy-start(bf16[384,512]{1,0:T(8,128)(2,1)} %get-tuple-element.46.refs_6_.own_ref) | copy-start | bytes 1179652
  39.7 0.7 copy-start.16
  40.3 11.6 %copy-start.22 = (bf16[256,256]{1,0:T(8,128)(2,1)S(1)}, bf16[256,256]{1,0:T(8,128)(2,1)}, u32[]{:S(2)}) copy-start(bf16[256,256]{1,0:T(8,128)(2,1)} %copy-done.21) | copy-start | bytes 393220
  40.3 16.6 %copy-start.20 = (bf16[256,256]{1,0:T(8,128)(2,1)S(1)}, bf16[256,256]{1,0:T(8,128)(2,1)}, u32[]{:S(2)}) copy-start(bf16[256,256]{1,0:T(8,128)(2,1)} %copy-done.19) | copy-start | bytes 393220
  40.3 17.1 %copy-start.9 = (bf16[384,512]{1,0:T(8,128)(2,1)S(1)}, bf16[384,512]{1,0:T(8,128)(2,1)}, u32[]{:S(2)}) copy-start(bf16[384,512]{1,0:T(8,128)(2,1)} %copy-done.8) | copy-start | bytes 1179652
  40.3 22.8 %copy-start.13 = (bf16[384,256]{1,0:T(8,128)(2,1)S(1)}, bf16[384,256]{1,0:T(8,128)(2,1)}, u32[]{:S(2)}) copy-start(bf16[384,256]{1,0:T(8,128)(2,1)} %copy-done.12) | copy-start | bytes 589828
  41.5 8.3 %collective-permute-start.6 = (bf16[96,512]{1,0:T(8,128)(2,1)S(1)}, bf16[96,512]{1,0:T(8,128)(2,1)S(1)}, u32[]{:S(2)}, u32[]{:S(2)}) collective-permute-start(bf16[96,512]{1,0:T(8,128)(2,1)S(1)} %get-tuple-element.64), channel_id=1, source_target_pairs={{0,1},{1,0},{2,3},{3,2},{4,5},{5,4},{6,7},{7,6},{8,9},{9,8},{10,11... | collective-permute-start | bytes 294920 | tf_op jit(solution)/shard_map/ppermute | solution.py:332
  41.6 10.1 %collective-permute-start.7 = (bf16[96,512]{1,0:T(8,128)(2,1)S(1)}, bf16[96,512]{1,0:T(8,128)(2,1)S(1)}, u32[]{:S(2)}, u32[]{:S(2)}) collective-permute-start(bf16[96,512]{1,0:T(8,128)(2,1)S(1)} %get-tuple-element.65), channel_id=1, source_target_pairs={{0,2},{1,3},{2,0},{3,1},{4,6},{5,7},{6,4},{7,5},{8,10},{9,11},{10,... | collective-permute-start | bytes 294920 | tf_op jit(solution)/shard_map/ppermute | solution.py:332
  44.3 7.6 %collective-permute-start.8 = (bf16[96,512]{1,0:T(8,128)(2,1)S(1)}, bf16[96,512]{1,0:T(8,128)(2,1)S(1)}, u32[]{:S(2)}, u32[]{:S(2)}) collective-permute-start(bf16[96,512]{1,0:T(8,128)(2,1)S(1)} %get-tuple-element.66), channel_id=1, source_target_pairs={{0,3},{1,2},{2,1},{3,0},{4,7},{5,6},{6,5},{7,4},{8,11},{9,10},{10,... | collective-permute-start | bytes 294920 | tf_op jit(solution)/shard_map/ppermute | solution.py:332
  44.3 1.0 %copy-start.5 = (bf16[384,512]{1,0:T(8,128)(2,1)S(1)}, bf16[384,512]{1,0:T(8,128)(2,1)}, u32[]{:S(2)}) copy-start(bf16[384,512]{1,0:T(8,128)(2,1)} %copy-done.4) | copy-start | bytes 1179652
  49.8 4.8 %collective-permute-start.9 = (bf16[96,512]{1,0:T(8,128)(2,1)S(1)}, bf16[96,512]{1,0:T(8,128)(2,1)S(1)}, u32[]{:S(2)}, u32[]{:S(2)}) collective-permute-start(bf16[96,512]{1,0:T(8,128)(2,1)S(1)} %get-tuple-element.68), channel_id=1, source_target_pairs={{0,1},{1,0},{2,3},{3,2},{4,5},{5,4},{6,7},{7,6},{8,9},{9,8},{10,11... | collective-permute-start | bytes 294920 | tf_op jit(solution)/shard_map/ppermute | solution.py:332
  49.8 6.4 %collective-permute-start.10 = (bf16[96,512]{1,0:T(8,128)(2,1)S(1)}, bf16[96,512]{1,0:T(8,128)(2,1)S(1)}, u32[]{:S(2)}, u32[]{:S(2)}) collective-permute-start(bf16[96,512]{1,0:T(8,128)(2,1)S(1)} %get-tuple-element.69), channel_id=1, source_target_pairs={{0,2},{1,3},{2,0},{3,1},{4,6},{5,7},{6,4},{7,5},{8,10},{9,11},{10,... | collective-permute-start | bytes 294920 | tf_op jit(solution)/shard_map/ppermute | solution.py:332
  51.7 5.2 %collective-permute-start.11 = (bf16[96,512]{1,0:T(8,128)(2,1)S(1)}, bf16[96,512]{1,0:T(8,128)(2,1)S(1)}, u32[]{:S(2)}, u32[]{:S(2)}) collective-permute-start(bf16[96,512]{1,0:T(8,128)(2,1)S(1)} %get-tuple-element.70), channel_id=1, source_target_pairs={{0,3},{1,2},{2,1},{3,0},{4,7},{5,6},{6,5},{7,4},{8,11},{9,10},{10,... | collective-permute-start | bytes 294920 | tf_op jit(solution)/shard_map/ppermute | solution.py:332
  51.9 9.4 %collective-permute-start.1 = (bf16[256,256]{1,0:T(8,128)(2,1)S(1)}, bf16[256,256]{1,0:T(8,128)(2,1)S(1)}, u32[]{:S(2)}, u32[]{:S(2)}) collective-permute-start(bf16[256,256]{1,0:T(8,128)(2,1)S(1)} %copy-done.22), channel_id=1, source_target_pairs={{0,16},{4,20},{8,24},{12,28},{16,0},{20,4},{24,8},{28,12},{1,17},{... | collective-permute-start | bytes 393224 | tf_op jit(solution)/shard_map/ppermute | solution.py:326
  54.6 6.7 %collective-permute-start.12 = (bf16[96,512]{1,0:T(8,128)(2,1)S(1)}, bf16[96,512]{1,0:T(8,128)(2,1)S(1)}, u32[]{:S(2)}, u32[]{:S(2)}) collective-permute-start(bf16[96,512]{1,0:T(8,128)(2,1)S(1)} %get-tuple-element.72), channel_id=1, source_target_pairs={{0,1},{1,0},{2,3},{3,2},{4,5},{5,4},{6,7},{7,6},{8,9},{9,8},{10,11... | collective-permute-start | bytes 294920 | tf_op jit(solution)/shard_map/ppermute | solution.py:332
  54.6 8.2 %collective-permute-start.13 = (bf16[96,512]{1,0:T(8,128)(2,1)S(1)}, bf16[96,512]{1,0:T(8,128)(2,1)S(1)}, u32[]{:S(2)}, u32[]{:S(2)}) collective-permute-start(bf16[96,512]{1,0:T(8,128)(2,1)S(1)} %get-tuple-element.73), channel_id=1, source_target_pairs={{0,2},{1,3},{2,0},{3,1},{4,6},{5,7},{6,4},{7,5},{8,10},{9,11},{10,... | collective-permute-start | bytes 294920 | tf_op jit(solution)/shard_map/ppermute | solution.py:332
  56.2 6.9 %collective-permute-start.14 = (bf16[96,512]{1,0:T(8,128)(2,1)S(1)}, bf16[96,512]{1,0:T(8,128)(2,1)S(1)}, u32[]{:S(2)}, u32[]{:S(2)}) collective-permute-start(bf16[96,512]{1,0:T(8,128)(2,1)S(1)} %get-tuple-element.74), channel_id=1, source_target_pairs={{0,3},{1,2},{2,1},{3,0},{4,7},{5,6},{6,5},{7,4},{8,11},{9,10},{10,... | collective-permute-start | bytes 294920 | tf_op jit(solution)/shard_map/ppermute | solution.py:332
  56.9 7.2 %collective-permute-start = (bf16[256,256]{1,0:T(8,128)(2,1)S(1)}, bf16[256,256]{1,0:T(8,128)(2,1)S(1)}, u32[]{:S(2)}, u32[]{:S(2)}) collective-permute-start(bf16[256,256]{1,0:T(8,128)(2,1)S(1)} %copy-done.20), channel_id=1, source_target_pairs={{0,16},{4,20},{8,24},{12,28},{16,0},{20,4},{24,8},{28,12},{1,17},{... | collective-permute-start | bytes 393224 | tf_op jit(solution)/shard_map/ppermute | solution.py:326
  61.3 4.5 %collective-permute-start.15 = (bf16[96,512]{1,0:T(8,128)(2,1)S(1)}, bf16[96,512]{1,0:T(8,128)(2,1)S(1)}, u32[]{:S(2)}, u32[]{:S(2)}) collective-permute-start(bf16[96,512]{1,0:T(8,128)(2,1)S(1)} %get-tuple-element.76), channel_id=1, source_target_pairs={{0,1},{1,0},{2,3},{3,2},{4,5},{5,4},{6,7},{7,6},{8,9},{9,8},{10,11... | collective-permute-start | bytes 294920 | tf_op jit(solution)/shard_map/ppermute | solution.py:332
  61.3 5.6 %collective-permute-start.16 = (bf16[96,512]{1,0:T(8,128)(2,1)S(1)}, bf16[96,512]{1,0:T(8,128)(2,1)S(1)}, u32[]{:S(2)}, u32[]{:S(2)}) collective-permute-start(bf16[96,512]{1,0:T(8,128)(2,1)S(1)} %get-tuple-element.77), channel_id=1, source_target_pairs={{0,2},{1,3},{2,0},{3,1},{4,6},{5,7},{6,4},{7,5},{8,10},{9,11},{10,... | collective-permute-start | bytes 294920 | tf_op jit(solution)/shard_map/ppermute | solution.py:332
  62.9 5.3 %collective-permute-start.17 = (bf16[96,512]{1,0:T(8,128)(2,1)S(1)}, bf16[96,512]{1,0:T(8,128)(2,1)S(1)}, u32[]{:S(2)}, u32[]{:S(2)}) collective-permute-start(bf16[96,512]{1,0:T(8,128)(2,1)S(1)} %get-tuple-element.78), channel_id=1, source_target_pairs={{0,3},{1,2},{2,1},{3,0},{4,7},{5,6},{6,5},{7,4},{8,11},{9,10},{10,... | collective-permute-start | bytes 294920 | tf_op jit(solution)/shard_map/ppermute | solution.py:332
  63.8 7.3 %collective-permute-start.21 = (bf16[96,256]{1,0:T(8,128)(2,1)S(1)}, bf16[96,256]{1,0:T(8,128)(2,1)S(1)}, u32[]{:S(2)}, u32[]{:S(2)}) collective-permute-start(bf16[96,256]{1,0:T(8,128)(2,1)S(1)} %get-tuple-element.83), channel_id=1, source_target_pairs={{0,1},{1,0},{2,3},{3,2},{4,5},{5,4},{6,7},{7,6},{8,9},{9,8},{10,11... | collective-permute-start | bytes 147464 | tf_op jit(solution)/shard_map/ppermute | solution.py:332
  64.2 6.9 %collective-permute-start.22 = (bf16[96,256]{1,0:T(8,128)(2,1)S(1)}, bf16[96,256]{1,0:T(8,128)(2,1)S(1)}, u32[]{:S(2)}, u32[]{:S(2)}) collective-permute-start(bf16[96,256]{1,0:T(8,128)(2,1)S(1)} %get-tuple-element.84), channel_id=1, source_target_pairs={{0,2},{1,3},{2,0},{3,1},{4,6},{5,7},{6,4},{7,5},{8,10},{9,11},{10,... | collective-permute-start | bytes 147464 | tf_op jit(solution)/shard_map/ppermute | solution.py:332
  65.7 5.4 %collective-permute-start.23 = (bf16[96,256]{1,0:T(8,128)(2,1)S(1)}, bf16[96,256]{1,0:T(8,128)(2,1)S(1)}, u32[]{:S(2)}, u32[]{:S(2)}) collective-permute-start(bf16[96,256]{1,0:T(8,128)(2,1)S(1)} %get-tuple-element.85), channel_id=1, source_target_pairs={{0,3},{1,2},{2,1},{3,0},{4,7},{5,6},{6,5},{7,4},{8,11},{9,10},{10,... | collective-permute-start | bytes 147464 | tf_op jit(solution)/shard_map/ppermute | solution.py:332
  68.9 4.2 %collective-permute-start.18 = (bf16[96,256]{1,0:T(8,128)(2,1)S(1)}, bf16[96,256]{1,0:T(8,128)(2,1)S(1)}, u32[]{:S(2)}, u32[]{:S(2)}) collective-permute-start(bf16[96,256]{1,0:T(8,128)(2,1)S(1)} %get-tuple-element.80), channel_id=1, source_target_pairs={{0,1},{1,0},{2,3},{3,2},{4,5},{5,4},{6,7},{7,6},{8,9},{9,8},{10,11... | collective-permute-start | bytes 147464 | tf_op jit(solution)/shard_map/ppermute | solution.py:332
  69.5 4.1 %collective-permute-start.19 = (bf16[96,256]{1,0:T(8,128)(2,1)S(1)}, bf16[96,256]{1,0:T(8,128)(2,1)S(1)}, u32[]{:S(2)}, u32[]{:S(2)}) collective-permute-start(bf16[96,256]{1,0:T(8,128)(2,1)S(1)} %get-tuple-element.81), channel_id=1, source_target_pairs={{0,2},{1,3},{2,0},{3,1},{4,6},{5,7},{6,4},{7,5},{8,10},{9,11},{10,... | collective-permute-start | bytes 147464 | tf_op jit(solution)/shard_map/ppermute | solution.py:332
  71.1 4.0 %collective-permute-start.20 = (bf16[96,256]{1,0:T(8,128)(2,1)S(1)}, bf16[96,256]{1,0:T(8,128)(2,1)S(1)}, u32[]{:S(2)}, u32[]{:S(2)}) collective-permute-start(bf16[96,256]{1,0:T(8,128)(2,1)S(1)} %get-tuple-element.82), channel_id=1, source_target_pairs={{0,3},{1,2},{2,1},{3,0},{4,7},{5,6},{6,5},{7,4},{8,11},{9,10},{10,... | collective-permute-start | bytes 147464 | tf_op jit(solution)/shard_map/ppermute | solution.py:332

commit v3 on v2

--- a/solution.py
+++ b/solution.py
@@ -11,6 +11,7 @@
 HEAD_SIZE = 128
 CAP = 2
 HIDDEN = -1e30
+AT_ONCE = ()
 FULL_VMEM, SOME_VMEM, LITTLE_VMEM = (60 << 20, 30 << 20, 8 << 20)
 PACK = 4
 NO_COST = pl.CostEstimate(flops=1000, bytes_accessed=1000, transcendentals=0)
@@ -205,8 +206,8 @@
     return pairs_of(out[: 2 * len(sets)]), carried
 
 
-def sort_kernel(block_count, block_rows, half_axis, peers, position_ref, mapping_ref, own_ref, arrived_ref, *refs):
-    outs = refs[-peers:]
+def sort_kernel(block_count, block_rows, half_axis, peers, in_order, position_ref, mapping_ref, own_ref, arrived_ref, *refs):
+    outs = [refs[-1].at[p] for p in range(peers)] if in_order else refs[-peers:]
     at, peer = position_ref[0], position_ref[1]
     partner = lax.rem(at + half_axis, 2 * half_axis)
     arrived_slot = [jnp.int32(-1)] * block_count
@@ -217,42 +218,46 @@
     share = block_count * block_rows // peers
     step = math.gcd(share, block_rows)
     for hop, out_ref in enumerate(outs):
-        to_peer = jnp.bitwise_xor(peer, hop)
+        to_peer = hop if in_order else jnp.bitwise_xor(peer, hop)
         for piece in range(share // step):
             row = to_peer * share + piece * step
-            block = lax.div(row, block_rows)
+            block = lax.div(jnp.int32(row), jnp.int32(block_rows))
             slot = jnp.int32(-1)
             for b in range(block_count):
                 slot = jnp.where(block == b, arrived_slot[b], slot)
             from_own = own_ref[aligned(row, step, step), :]
             from_pair = arrived_ref[
-                aligned(jnp.maximum(slot, 0) * block_rows + lax.rem(row, block_rows), step, step), :
+                aligned(jnp.maximum(slot, 0) * block_rows + lax.rem(jnp.int32(row), jnp.int32(block_rows)), step, step), :
             ]
             out_ref[piece * step : (piece + 1) * step, :] = jnp.where(slot >= 0, from_pair, from_own)
 
 
-def sort_rows(position, mapping, own, arrived, after, block_count, half_axis, peers):
+def sort_rows(position, mapping, own, arrived, after, block_count, half_axis, peers, in_order):
     rows, columns = own.shape
-    out = jax.ShapeDtypeStruct((rows // peers, columns), own.dtype)
+    if in_order:
+        out = [jax.ShapeDtypeStruct((peers, rows // peers, columns), own.dtype)]
+    else:
+        out = [jax.ShapeDtypeStruct((rows // peers, columns), own.dtype)] * peers
     return pl.pallas_call(
-        functools.partial(sort_kernel, block_count, rows // block_count, half_axis, peers),
+        functools.partial(sort_kernel, block_count, rows // block_count, half_axis, peers, in_order),
         in_specs=[IN_SMEM, IN_SMEM, IN_VMEM, IN_VMEM] + [ANYWHERE] * len(after),
-        out_specs=[IN_VMEM] * peers,
-        out_shape=[out] * peers,
+        out_specs=[IN_VMEM] * len(out),
+        out_shape=out,
         compiler_params=pltpu.CompilerParams(vmem_limit_bytes=LITTLE_VMEM),
         cost_estimate=NO_COST,
     )(position, mapping, own, arrived, *after)
 
 
 def place_kernel(peers, columns_here, places, held, position_ref, *refs):
-    pieces = refs[: peers * len(places)]
+    pieces = list(refs)
     outs, sem = refs[-len(columns_here) - 1 : -1], refs[-1]
     peer = position_ref[1]
     copies = []
-    for index, parts in enumerate(places):
+    for in_order, parts in places:
+        chunk = pieces.pop(0) if in_order else None
         for hop in range(peers):
-            from_peer = jnp.bitwise_xor(peer, hop)
-            piece = pieces[index * peers + hop]
+            from_peer = hop if in_order else jnp.bitwise_xor(peer, hop)
+            piece = chunk.at[hop] if in_order else pieces.pop(0)
             for at, size, out, column in parts:
                 copies.append(
                     pltpu.make_async_copy(
@@ -266,6 +271,83 @@
         copy.wait()
 
 
+def spread_kernel(block_count, block_rows, half_axis, peers, position_ref, mapping_ref, own_ref, send_ref, out_ref):
+    at = position_ref[0]
+    partner = lax.rem(at + half_axis, 2 * half_axis)
+    send_slot = [jnp.int32(0)] * block_count
+    for index, block in enumerate(moved_blocks(mapping_ref, at, block_count)):
+        target = mapping_ref[at * block_count + block] - partner * block_count
+        for slot in range(block_count):
+            send_slot[slot] = jnp.where(target == slot, index, send_slot[slot])
+    share = block_count * block_rows // peers
+    step = math.gcd(share, block_rows)
+    for peer in range(peers):
+        out_ref[peer, 0] = own_ref[peer * share : (peer + 1) * share, :]
+        for piece in range(share // step):
+            row = peer * share + piece * step
+            at_send = send_slot[row // block_rows] * block_rows + row % block_rows
+            out_ref[peer, 1, piece * step : (piece + 1) * step, :] = send_ref[aligned(at_send, step, step), :]
+
+
+def spread_rows(position, mapping, own, send, half_axis, block_count, peers):
+    rows, columns = own.shape
+    return pl.pallas_call(
+        functools.partial(spread_kernel, block_count, rows // block_count, half_axis, peers),
+        in_specs=[IN_SMEM, IN_SMEM, IN_VMEM, IN_VMEM],
+        out_specs=IN_VMEM,
+        out_shape=jax.ShapeDtypeStruct((peers, 2, rows // peers, columns), own.dtype),
+        compiler_params=pltpu.CompilerParams(vmem_limit_bytes=LITTLE_VMEM),
+        cost_estimate=NO_COST,
+    )(position, mapping, own, send)
+
+
+def place_last_kernel(block_count, block_rows, peers, columns_here, parts, *refs):
+    position_ref, mapping_ref, spread_ref, arrived_ref, *refs = refs
+    outs, merged_ref, sem = refs[-len(columns_here) - 2 : -2], refs[-2], refs[-1]
+    here = own_sources(mapping_ref, position_ref[0], block_count)
+    share = block_count * block_rows // peers
+    step = math.gcd(share, block_rows)
+    for piece in range(share // step):
+        block = lax.div(position_ref[1] * share + piece * step, block_rows)
+        source = jnp.int32(-1)
+        for slot in range(block_count):
+            source = jnp.where(block == slot, here[slot], source)
+        rows = slice(piece * step, (piece + 1) * step)
+        for peer in range(peers):
+            merged_ref[peer, rows, :] = jnp.where(source >= 0, spread_ref[peer, 0, rows, :], arrived_ref[peer, rows, :])
+    copies = []
+    for peer in range(peers):
+        for at, size, out, column in parts:
+            start = peer * columns_here[out] + column
+            copies.append(
+                pltpu.make_async_copy(
+                    merged_ref.at[peer, :, at : at + size], outs[out].at[:, start : start + size], sem.at[len(copies)]
+                )
+            )
+            copies[-1].start()
+    for copy in copies:
+        copy.wait()
+
+
+def place_last(position, mapping, spread, arrived, parts, columns_here, held, block_count):
+    peers, _, share, columns = spread.shape
+    return pl.pallas_call(
+        functools.partial(
+            place_last_kernel, block_count, share * peers // block_count, peers, columns_here, parts
+        ),
+        in_specs=[IN_SMEM, IN_SMEM, IN_VMEM, IN_VMEM] + [ANYWHERE] * len(held),
+        out_specs=[ANYWHERE] * len(held),
+        out_shape=[jax.ShapeDtypeStruct(h.shape, h.dtype) for h in held],
+        input_output_aliases={4 + i: i for i in range(len(held))},
+        scratch_shapes=[
+            pltpu.VMEM((peers, share, columns), spread.dtype),
+            pltpu.SemaphoreType.DMA((peers * len(parts),)),
+        ],
+        compiler_params=pltpu.CompilerParams(vmem_limit_bytes=LITTLE_VMEM),
+        cost_estimate=NO_COST,
+    )(position, mapping, spread, arrived, *held)
+
+
 def joined_parts(parts):
     joined = []
     for at, size, out, column in parts:
@@ -277,10 +359,10 @@
 
 
 def place_columns(position, pieces, places, columns_here, held, peers):
-    rows = pieces[0][0].shape[0]
+    rows, dtype = pieces[0][0].shape[-2], pieces[0][0].dtype
     flat = [p for chunk in pieces for p in chunk]
-    count = peers * sum(len(parts) for parts in places)
-    out_shape = [jax.ShapeDtypeStruct((rows, peers * c), pieces[0][0].dtype) for c in columns_here]
+    count = peers * sum(len(parts) for _, parts in places)
+    out_shape = [jax.ShapeDtypeStruct((rows, peers * c), dtype) for c in columns_here]
     return pl.pallas_call(
         functools.partial(place_kernel, peers, columns_here, places, len(held)),
         in_specs=[IN_SMEM] + [IN_VMEM] * len(flat) + [ANYWHERE] * len(held),
@@ -294,13 +376,14 @@
 
 
 def plan_of(groups, repeats):
-    lead = max(1, repeats // 2)
+    lead, cut = max(1, 5 * repeats // 8), max(1, 4 * repeats // 8)
     heads = list(range(repeats))
     kernels = [(0, 0, lead, [heads[:lead]]), (0, lead, repeats - lead, [heads[: repeats - lead]])]
     for group in range(1, groups):
-        kernels.append((group, 0, repeats, [heads[:lead], heads[lead:]]))
-    for group in range(groups):
-        kernels[-1][3].append([keys_and_values(group)])
+        kernels.append((group, 0, repeats, [heads[:cut], heads[cut:]]))
+    for group in range(groups - 1):
+        kernels[group + 1][3][-1].append(keys_and_values(group))
+    kernels[-1][3].append([keys_and_values(groups - 1)])
     return kernels
 
 
@@ -323,16 +406,15 @@
         )
         after = made[0][0]
         for units, (own, send) in zip(sets, made):
-            sent.append((group * repeats + start, units, own, lax.ppermute(send, "ctx", pairs)))
-
-    order, pieces, places = [after], [], []
-    for start, units, own, arrived in sent:
-        parts = sort_rows(position, block_mapping, own, arrived, order, block_count, half_axis, peers)
-        got = [parts[0]] + [
-            lax.ppermute(parts[hop], "tensor", [(i, i ^ hop) for i in range(peers)]) for hop in range(1, peers)
-        ]
-        order = [got[0]] + (list(pieces[-1][1:]) if pieces else [])
-        pieces.append(got)
+            sent.append((group * repeats + start, units, own, send))
+
+    *sent, (_, last_units, own, send) = sent
+    sent = [(start, units, own, lax.ppermute(send, "ctx", pairs)) for start, units, own, send in sent]
+    spread = spread_rows(position, block_mapping, own, send, half_axis, block_count, peers)
+    spread = lax.all_to_all(spread, "tensor", split_axis=0, concat_axis=0, tiled=True)
+    last_arrived = lax.ppermute(spread[:, 1], "ctx", pairs)
+
+    def parts_of(start, units):
         parts = []
         for unit in units:
             at = columns_before(units, unit)
@@ -341,12 +423,27 @@
             else:
                 parts.append((at, HEAD_SIZE, 1, group_of(unit) * HEAD_SIZE))
                 parts.append((at + HEAD_SIZE, HEAD_SIZE, 2, group_of(unit) * HEAD_SIZE))
-        places.append(joined_parts(parts))
+        return joined_parts(parts)
+
+    order, pieces, places = [after], [], []
+    for index, (start, units, own, arrived) in enumerate(sent):
+        at_once = index in AT_ONCE
+        got = sort_rows(position, block_mapping, own, arrived, order, block_count, half_axis, peers, at_once)
+        if at_once:
+            got = [lax.all_to_all(got[0], "tensor", split_axis=0, concat_axis=0, tiled=True)]
+        else:
+            got = [got[0]] + [
+                lax.ppermute(got[hop], "tensor", [(i, i ^ hop) for i in range(peers)]) for hop in range(1, peers)
+            ]
+        order = [got[0], got[1]] + (list(pieces[-1][2:]) if pieces else [])
+        pieces.append(got)
+        places.append((at_once, parts_of(start, units)))
     columns_here = [queries.shape[1], key_layout_rows.shape[1], value_layout_rows.shape[1]]
-    held = []
-    if len(pieces) > 1:
-        held = place_columns(position, pieces[:-1], places[:-1], columns_here, [], peers)
-    return tuple(place_columns(position, pieces[-1:], places[-1:], columns_here, held, peers))
+    held = place_columns(position, pieces, places, columns_here, [], peers)
+    parts = parts_of(0, last_units)
+    return tuple(
+        place_last(position, block_mapping, spread, last_arrived, parts, columns_here, held, block_count)
+    )
 
 
 def solution(mesh):

time: 77.2 us -> 75.7 us (0.981)
  waiting for transfers between devices: 27.8 us -> 25.1 us
  Pallas kernels: 19.9 us -> 21.1 us
    ppermute x6 -> x4, waiting for transfers between devices: 22.8 us -> 19.3 us  [on_device(): lax.ppermute(send, 'ctx', pairs)]
    all_to_all x0 -> x1, starting transfers between devices: none -> 3.46 us  [on_device(): lax.all_to_all(spread, 'tensor', split_axis=0, concat_axis=0, tiled=True)]
    ppermute x18 -> x13, starting transfers between devices: 12 us -> 9.26 us  [the longest x12 9.25 us: on_device(): lax.ppermute(got[hop], 'tensor', [(i, i ^ hop) for i in range(peers)])]
    pallas_call x0 -> x2, Pallas kernels: none -> 2.63 us  [the longest x1 1.31 us: spread_rows(): pl.pallas_call(functools.partial(spread_kernel, block_count, rows // bloc...]
    pallas_call x6 -> x4, Pallas kernels: 4.93 us -> 3.58 us  [sort_rows(): pl.pallas_call(functools.partial(sort_kernel, block_count, rows // block_...]
    pallas_call x2 -> x1, Pallas kernels: 3.23 us -> 1.94 us  [place_columns(): pl.pallas_call(functools.partial(place_kernel, peers, columns_here, place...]
    pallas_call x3, Pallas kernels: 11.8 us -> 12.9 us  [grads_chunk(): pl.pallas_call(functools.partial(grads_kernel, block_count, block_rows, g...]
    ppermute x18 -> x13, waiting for transfers between devices: 4.91 us -> 5.87 us  [the longest x12 4.59 us: on_device(): lax.ppermute(got[hop], 'tensor', [(i, i ^ hop) for i in range(peers)])]
  transfers between devices with their start and end apart: 24 -> 18, of which waited for: 10 -> 7; matrix products, arithmetic and copies ran while one was open for 0% -> 0% of each run, Pallas kernels for 19% -> 19%
where the time goes in v3:
time: 75.7 us; the launch traced here: 75.3 us
  waiting for transfers between devices  25.1 us (33%)
  Pallas kernels  21.1 us (28%)
  starting transfers between devices  19.8 us (26%)
  local copies, waits for them, and re-layouts  8.35 us (11%)
  between operations  0.83 us (1%)
    ppermute x4, waiting for transfers between devices, on_device(): lax.ppermute(send, 'ctx', pairs)  19.3 us
    pallas_call x3, Pallas kernels, grads_chunk(): pl.pallas_call(functools.partial(grads_kernel, block_count, block_rows, g...  12.9 us
    ppermute x12, starting transfers between devices, on_device(): lax.ppermute(got[hop], 'tensor', [(i, i ^ hop) for i in range(peers)])  9.25 us
    unnamed x38, local copies, waits for them, and re-layouts  8.33 us
    ppermute x4, starting transfers between devices, on_device(): lax.ppermute(send, 'ctx', pairs)  7.1 us
    ppermute x12, waiting for transfers between devices, on_device(): lax.ppermute(got[hop], 'tensor', [(i, i ^ hop) for i in range(peers)])  4.59 us
    pallas_call x4, Pallas kernels, sort_rows(): pl.pallas_call(functools.partial(sort_kernel, block_count, rows // block_...  3.58 us
    all_to_all x1, starting transfers between devices, on_device(): lax.all_to_all(spread, 'tensor', split_axis=0, concat_axis=0, tiled=True)  3.46 us
  transfers between devices with their start and end apart: 18, of which 7 were waited for; matrix products, arithmetic and copies ran while one was open for 0% of the time, Pallas kernels for 19%

profile of v3, /device:TPU:0, one launch (start us, length us, event | category | flops | bytes accessed | tf_op | source)
XLA Modules:
  0.0 75.3 jit_solution(16566498077722677110)
XLA Ops:
  0.6 0.0 copy-start.16
  0.6 0.0 copy-start.17
  0.7 0.0 copy-start.1
  0.7 0.0 copy-start.5
  0.7 5.3 %shard_map.85 = (bf16[384,640]{1,0:T(8,128)(2,1)}, bf16[256,640]{1,0:T(8,128)(2,1)}, f32[384,128]{1,0:T(8,128)}, f32[384,128]{1,0:T(8,128)}) custom-call(s32[3]{0:T(128)} %refs_0_.5, s32[24]{0:T(128)} %refs_1_.7, bf16[384,2048]{1,0:T(8,128)(2,1)} %refs_2_.5, bf16[384,2048]{1,0:T(8,128)(2,1)} %refs_3_.5, bf16[384,256]{1,0:T(8,128)(2,1)} %refs_4_.5, ...), custom_call_target="tpu_custom_call" | custom-call | flops 1000 | bytes 1000 | tf_op jit(solution)/shard_map/pallas_call | solution.py:186
  6.0 4.0 %collective-permute-start.1 = (bf16[256,640]{1,0:T(8,128)(2,1)}, bf16[256,640]{1,0:T(8,128)(2,1)}, u32[]{:S(2)}, u32[]{:S(2)}) collective-permute-start(bf16[256,640]{1,0:T(8,128)(2,1)} %get-tuple-element.40), channel_id=1, source_target_pairs={{0,16},{4,20},{8,24},{12,28},{16,0},{20,4},{24,8},{28,12},{1,17},{... | collective-permute-start | bytes 983048 | tf_op jit(solution)/shard_map/ppermute | solution.py:412
  10.0 0.0 copy-done.1
  10.0 0.0 copy-start.3
  10.1 1.0 %copy-done.3 = bf16[384,640]{1,0:T(8,128)(2,1)S(1)} copy-done((bf16[384,640]{1,0:T(8,128)(2,1)S(1)}, bf16[384,640]{1,0:T(8,128)(2,1)}, u32[]{:S(2)}) %copy-start.3) | copy-done | bytes 491544
  11.1 0.9 %copy-done.10 = f32[384,128]{1,0:T(8,128)S(1)} copy-done((f32[384,128]{1,0:T(8,128)S(1)}, f32[384,128]{1,0:T(8,128)}, u32[]{:S(2)}) %copy-start.10) | copy-done | bytes 196632
  12.0 0.9 %copy-done.11 = f32[384,128]{1,0:T(8,128)S(1)} copy-done((f32[384,128]{1,0:T(8,128)S(1)}, f32[384,128]{1,0:T(8,128)}, u32[]{:S(2)}) %copy-start.11) | copy-done | bytes 196632
  12.9 3.0 %shard_map.86 = (bf16[384,640]{1,0:T(8,128)(2,1)S(1)}, bf16[256,640]{1,0:T(8,128)(2,1)}) custom-call(s32[3]{0:T(128)S(1)} %copy-done.17, s32[24]{0:T(128)S(1)} %copy-done.16, bf16[384,2048]{1,0:T(8,128)(2,1)S(1)} %copy-done, bf16[384,2048]{1,0:T(8,128)(2,1)S(1)} %copy-done.1, bf16[384,256]{1,0:T(8,128)(2,1)S(1)} %copy-done.2, ...), custom_call_target="tpu_custom_call" | custom-call | flops 1000 | bytes 1000 | tf_op jit(solution)/shard_map/pallas_call | solution.py:186
  15.9 0.0 collective-permute-start.5
  15.9 4.7 %shard_map.87 = (bf16[384,512]{1,0:T(8,128)(2,1)S(1)}, bf16[256,512]{1,0:T(8,128)(2,1)S(1)}, bf16[384,512]{1,0:T(8,128)(2,1)S(1)}, bf16[256,512]{1,0:T(8,128)(2,...) custom-call(s32[3]{0:T(128)S(1)} %copy-done.17, s32[24]{0:T(128)S(1)} %copy-done.16, ...), custom_call_target="tpu_custom_call" | custom-call | flops 1000 | bytes 1000 | tf_op jit(solution)/shard_map/pallas_call | solution.py:186
  20.6 0.8 %copy-done.6 = bf16[384,512]{1,0:T(8,128)(2,1)} copy-done((bf16[384,512]{1,0:T(8,128)(2,1)}, bf16[384,512]{1,0:T(8,128)(2,1)S(1)}, u32[]{:S(2)}) %copy-start.6) | copy-done | bytes 393240
  21.4 0.7 copy-done.8
  22.1 0.7 copy-done.12
  22.8 0.7 copy-done.14
  23.5 0.7 copy-done.18
  24.1 0.1 pad_add_fusion.position_ref.refs_0_
  24.2 1.0 %copy-done.13 = bf16[384,256]{1,0:T(8,128)(2,1)S(1)} copy-done((bf16[384,256]{1,0:T(8,128)(2,1)S(1)}, bf16[384,256]{1,0:T(8,128)(2,1)}, u32[]{:S(2)}) %copy-start.13) | copy-done | bytes 196632
  25.2 0.9 %copy-done.15 = bf16[256,256]{1,0:T(8,128)(2,1)S(1)} copy-done((bf16[256,256]{1,0:T(8,128)(2,1)S(1)}, bf16[256,256]{1,0:T(8,128)(2,1)}, u32[]{:S(2)}) %copy-start.15) | copy-done | bytes 131096
  26.1 1.3 %shard_map.88 = bf16[4,2,96,256]{3,2,1,0:T(8,128)(2,1)} custom-call(s32[2]{0:T(128)S(1)} %pad_add_fusion.position_ref.refs_0_, s32[24]{0:T(128)S(1)} %copy-done.16, bf16[384,256]{1,0:T(8,128)(2,1)S(1)} %copy-done.13, bf16[256,256]{1,0:T(8,128)(2,1)S(1)} %copy-done.15), custom_call_target="tpu_custom_call" | custom-call | flops 1000 | bytes 1000 | tf_op jit(solution)/shard_map/pallas_call | solution.py:294
  27.4 3.5 %all-to-all-start = ((bf16[4,2,96,256]{3,2,1,0:T(8,128)(2,1)}), bf16[4,2,96,256]{3,2,1,0:T(8,128)(2,1)S(1)}, u32[]{:S(2)}, u32[]{:S(2)}) async-start(bf16[4,2,96,256]{3,2,1,0:T(8,128)(2,1)} %shard_map.88), calls=%async_computation | async-start | bytes 786432 | tf_op jit(solution)/shard_map/all_to_all | solution.py:414
  30.9 3.0 %collective-permute-start.9 = (bf16[256,512]{1,0:T(8,128)(2,1)}, bf16[256,512]{1,0:T(8,128)(2,1)S(1)}, u32[]{:S(2)}, u32[]{:S(2)}) collective-permute-start(bf16[256,512]{1,0:T(8,128)(2,1)} %copy-done.18), channel_id=1, source_target_pairs={{0,16},{4,20},{8,24},{12,28},{16,0},{20,4},{24,8},{28,12},{1,17},{... | collective-permute-start | bytes 786440 | tf_op jit(solution)/shard_map/ppermute | solution.py:412
  33.9 0.0 collective-permute-done.1.arrived_ref
  33.9 1.1 %shard_map.89 = (bf16[96,640]{1,0:T(8,128)(2,1)S(1)}, bf16[96,640]{1,0:T(8,128)(2,1)S(1)}, bf16[96,640]{1,0:T(8,128)(2,1)S(1)}, bf16[96,640]{1,0:T(8,128)(2,1)S(1)}) custom-call(s32[2]{0:T(128)S(1)} %pad_add_fusion.position_ref.refs_0_, s32[24]{0:T(128)S(1)} %copy-done.16, bf16[384,640]{1,0:T(8,128)(2,1)S(1)} %copy-done.4, ...), custom_call_target="tpu_custom_call" | custom-call | flops 1000 | bytes 1000 | tf_op jit(solution)/shard_map/pallas_call | solution.py:241
  35.0 0.2 collective-permute-start.2
  35.2 1.9 %collective-permute-start.3 = (bf16[96,640]{1,0:T(8,128)(2,1)S(1)}, bf16[96,640]{1,0:T(8,128)(2,1)S(1)}, u32[]{:S(2)}, u32[]{:S(2)}) collective-permute-start(bf16[96,640]{1,0:T(8,128)(2,1)S(1)} %get-tuple-element.44), channel_id=1, source_target_pairs={{0,2},{1,3},{2,0},{3,1},{4,6},{5,7},{6,4},{7,5},{8,10},{9,11},{10,... | collective-permute-start | bytes 368648 | tf_op jit(solution)/shard_map/ppermute | solution.py:436
  37.1 0.1 collective-permute-start.4
  37.2 8.4 %collective-permute-done.5.arrived_ref = bf16[256,640]{1,0:T(8,128)(2,1)} collective-permute-done((bf16[256,640]{1,0:T(8,128)(2,1)}, bf16[256,640]{1,0:T(8,128)(2,1)}, u32[]{:S(2)}, u32[]{:S(2)}) %collective-permute-start.5) | collective-permute-done | bytes 327712 | tf_op jit(solution)/shard_map/ppermute | solution.py:412
  45.5 0.0 collective-permute-done.2.refs_1_
  45.5 1.1 %shard_map.90 = (bf16[96,640]{1,0:T(8,128)(2,1)S(1)}, bf16[96,640]{1,0:T(8,128)(2,1)S(1)}, bf16[96,640]{1,0:T(8,128)(2,1)S(1)}, bf16[96,640]{1,0:T(8,128)(2,1)S(1)}) custom-call(s32[2]{0:T(128)S(1)} %pad_add_fusion.position_ref.refs_0_, s32[24]{0:T(128)S(1)} %copy-done.16, bf16[384,640]{1,0:T(8,128)(2,1)S(1)} %get-tuple-element.37.refs_6_.own_ref, ...), custom_call_target="tpu_custom_call" | custom-call | flops 1000 | bytes 1000 | tf_op jit(solution)/shard_map/pallas_call | solution.py:241
  46.7 0.1 collective-permute-start.6
  46.8 0.1 collective-permute-start.13
  46.8 3.4 %collective-permute-done.9.arrived_ref = bf16[256,512]{1,0:T(8,128)(2,1)S(1)} collective-permute-done((bf16[256,512]{1,0:T(8,128)(2,1)}, bf16[256,512]{1,0:T(8,128)(2,1)S(1)}, u32[]{:S(2)}, u32[]{:S(2)}) %collective-permute-start.9) | collective-permute-done | bytes 262176 | tf_op jit(solution)/shard_map/ppermute | solution.py:412
  50.2 1.6 %collective-permute-start.7 = (bf16[96,640]{1,0:T(8,128)(2,1)S(1)}, bf16[96,640]{1,0:T(8,128)(2,1)S(1)}, u32[]{:S(2)}, u32[]{:S(2)}) collective-permute-start(bf16[96,640]{1,0:T(8,128)(2,1)S(1)} %get-tuple-element.49), channel_id=1, source_target_pairs={{0,2},{1,3},{2,0},{3,1},{4,6},{5,7},{6,4},{7,5},{8,10},{9,11},{10,... | collective-permute-start | bytes 368648 | tf_op jit(solution)/shard_map/ppermute | solution.py:436
  51.8 0.0 collective-permute-done.3.refs_2_
  51.8 0.0 collective-permute-start.8
  51.8 0.0 collective-permute-done.4.refs_3_
  51.8 0.0 collective-permute-done.6.refs_1_.refs_5_
  51.8 0.7 shard_map.91
  52.5 0.6 collective-permute-start.10
  53.1 1.6 %collective-permute-start.11 = (bf16[96,512]{1,0:T(8,128)(2,1)S(1)}, bf16[96,512]{1,0:T(8,128)(2,1)S(1)}, u32[]{:S(2)}, u32[]{:S(2)}) collective-permute-start(bf16[96,512]{1,0:T(8,128)(2,1)S(1)} %get-tuple-element.54), channel_id=1, source_target_pairs={{0,2},{1,3},{2,0},{3,1},{4,6},{5,7},{6,4},{7,5},{8,10},{9,11},{10,... | collective-permute-start | bytes 294920 | tf_op jit(solution)/shard_map/ppermute | solution.py:436
  54.7 0.0 all-to-all-done.refs_2_
  54.7 7.5 %collective-permute-done.13.arrived_ref = bf16[256,512]{1,0:T(8,128)(2,1)S(1)} collective-permute-done((bf16[256,512]{1,0:T(8,128)(2,1)}, bf16[256,512]{1,0:T(8,128)(2,1)S(1)}, u32[]{:S(2)}, u32[]{:S(2)}) %collective-permute-start.13) | collective-permute-done | bytes 262176 | tf_op jit(solution)/shard_map/ppermute | solution.py:412
  62.2 0.0 collective-permute-start
  62.2 0.0 collective-permute-done.7.refs_2_.refs_6_
  62.2 1.3 %collective-permute-start.12 = (bf16[96,512]{1,0:T(8,128)(2,1)S(1)}, bf16[96,512]{1,0:T(8,128)(2,1)S(1)}, u32[]{:S(2)}, u32[]{:S(2)}) collective-permute-start(bf16[96,512]{1,0:T(8,128)(2,1)S(1)} %get-tuple-element.55), channel_id=1, source_target_pairs={{0,3},{1,2},{2,1},{3,0},{4,7},{5,6},{6,5},{7,4},{8,11},{9,10},{10,... | collective-permute-start | bytes 294920 | tf_op jit(solution)/shard_map/ppermute | solution.py:436
  63.5 0.0 collective-permute-done.8.refs_3_.refs_7_
  63.6 0.0 collective-permute-done.10.refs_1_.refs_9_
  63.6 0.0 copy-done.9
  63.6 0.7 shard_map.92
  64.2 0.5 collective-permute-start.14
  64.8 0.4 collective-permute-start.15
  65.1 0.0 collective-permute-done.11.refs_10_
  65.1 1.1 %collective-permute-start.16 = (bf16[96,512]{1,0:T(8,128)(2,1)S(1)}, bf16[96,512]{1,0:T(8,128)(2,1)S(1)}, u32[]{:S(2)}, u32[]{:S(2)}) collective-permute-start(bf16[96,512]{1,0:T(8,128)(2,1)S(1)} %get-tuple-element.61), channel_id=1, source_target_pairs={{0,3},{1,2},{2,1},{3,0},{4,7},{5,6},{6,5},{7,4},{8,11},{9,10},{10,... | collective-permute-start | bytes 294920 | tf_op jit(solution)/shard_map/ppermute | solution.py:436
  66.2 0.9 %collective-permute-done.12.refs_11_ = bf16[96,512]{1,0:T(8,128)(2,1)S(1)} collective-permute-done((bf16[96,512]{1,0:T(8,128)(2,1)S(1)}, bf16[96,512]{1,0:T(8,128)(2,1)S(1)}, u32[]{:S(2)}, u32[]{:S(2)}) %collective-permute-start.12) | collective-permute-done | bytes 98336 | tf_op jit(solution)/shard_map/ppermute | solution.py:436
  67.1 0.0 collective-permute-done.14.refs_13_
  67.1 3.3 %collective-permute-done.15.refs_14_ = bf16[96,512]{1,0:T(8,128)(2,1)S(1)} collective-permute-done((bf16[96,512]{1,0:T(8,128)(2,1)S(1)}, bf16[96,512]{1,0:T(8,128)(2,1)S(1)}, u32[]{:S(2)}, u32[]{:S(2)}) %collective-permute-start.15) | collective-permute-done | bytes 98336 | tf_op jit(solution)/shard_map/ppermute | solution.py:436
  70.4 0.4 collective-permute-done.16.refs_15_
  70.8 1.9 %shard_map.93 = (bf16[96,8192]{1,0:T(8,128)(2,1)}, bf16[96,1024]{1,0:T(8,128)(2,1)}, bf16[96,1024]{1,0:T(8,128)(2,1)}) custom-call(s32[2]{0:T(128)S(1)} %pad_add_fusion.position_ref.refs_0_, bf16[96,640]{1,0:T(8,128)(2,1)S(1)} %get-tuple-element.42.refs_0_, bf16[96,640]{1,0:T(8,128)(2,1)S(1)} %collective-permute-done.2.refs_1_, ...), custom_call_target="tpu_custom_call" | custom-call | flops 1000 | bytes 1000 | tf_op jit(solution)/shard_map/pallas_call | solution.py:366
  72.7 1.3 %collective-permute-done.refs_3_ = bf16[4,96,256]{2,1,0:T(8,128)(2,1)S(1)} collective-permute-done((bf16[4,96,256]{2,1,0:T(8,128)(2,1)S(1)}, bf16[4,96,256]{2,1,0:T(8,128)(2,1)S(1)}, u32[]{:S(2)}, u32[]{:S(2)}) %collective-permute-start) | collective-permute-done | bytes 196640 | tf_op jit(solution)/shard_map/ppermute | solution.py:415
  74.0 1.3 %shard_map.94 = (bf16[96,8192]{1,0:T(8,128)(2,1)}, bf16[96,1024]{1,0:T(8,128)(2,1)}, bf16[96,1024]{1,0:T(8,128)(2,1)}) custom-call(s32[2]{0:T(128)S(1)} %pad_add_fusion.position_ref.refs_0_, s32[24]{0:T(128)S(1)} %copy-done.16, bf16[4,2,96,256]{3,2,1,0:T(8,128)(2,1)S(1)} %all-to-all-done.refs_2_, ...), custom_call_target="tpu_custom_call", output_to_operand_aliasing={{0}: (4, {}), {1}: (5, {}), {2}: (6, {})} | custom-call | flops 1000 | bytes 1000 | tf_op jit(solution)/shard_map/pallas_call | solution.py:334
  (22 shorter events, 0.1 us)
Async XLA Ops:
  0.6 9.4 %copy-start.16 = (s32[24]{0:T(128)S(1)}, s32[24]{0:T(128)}, u32[]{:S(2)}) copy-start(s32[24]{0:T(128)} %refs_1_.7) | copy-start | bytes 292
  0.6 9.4 %copy-start.17 = (s32[3]{0:T(128)S(1)}, s32[3]{0:T(128)}, u32[]{:S(2)}) copy-start(s32[3]{0:T(128)} %refs_0_.5) | copy-start | bytes 40
  0.7 9.4 %copy-start.1 = (bf16[384,2048]{1,0:T(8,128)(2,1)S(1)}, bf16[384,2048]{1,0:T(8,128)(2,1)}, u32[]{:S(2)}) copy-start(bf16[384,2048]{1,0:T(8,128)(2,1)} %refs_3_.5) | copy-start | bytes 4718596
  0.7 9.4 %copy-start.5 = (bf16[384,256]{1,0:T(8,128)(2,1)S(1)}, bf16[384,256]{1,0:T(8,128)(2,1)}, u32[]{:S(2)}) copy-start(bf16[384,256]{1,0:T(8,128)(2,1)} %refs_5_.5) | copy-start | bytes 589828
  0.7 9.4 %copy-start.2 = (bf16[384,256]{1,0:T(8,128)(2,1)S(1)}, bf16[384,256]{1,0:T(8,128)(2,1)}, u32[]{:S(2)}) copy-start(bf16[384,256]{1,0:T(8,128)(2,1)} %refs_4_.5) | copy-start | bytes 589828
  0.7 9.4 %copy-start = (bf16[384,2048]{1,0:T(8,128)(2,1)S(1)}, bf16[384,2048]{1,0:T(8,128)(2,1)}, u32[]{:S(2)}) copy-start(bf16[384,2048]{1,0:T(8,128)(2,1)} %refs_2_.5) | copy-start | bytes 4718596
  6.0 27.9 %collective-permute-start.1 = (bf16[256,640]{1,0:T(8,128)(2,1)}, bf16[256,640]{1,0:T(8,128)(2,1)}, u32[]{:S(2)}, u32[]{:S(2)}) collective-permute-start(bf16[256,640]{1,0:T(8,128)(2,1)} %get-tuple-element.40), channel_id=1, source_target_pairs={{0,16},{4,20},{8,24},{12,28},{16,0},{20,4},{24,8},{28,12},{1,17},{... | collective-permute-start | bytes 983048 | tf_op jit(solution)/shard_map/ppermute | solution.py:412
  10.0 1.0 %copy-start.3 = (bf16[384,640]{1,0:T(8,128)(2,1)S(1)}, bf16[384,640]{1,0:T(8,128)(2,1)}, u32[]{:S(2)}) copy-start(bf16[384,640]{1,0:T(8,128)(2,1)} %get-tuple-element.34.refs_6_.own_ref) | copy-start | bytes 1474564
  11.1 0.9 %copy-start.10 = (f32[384,128]{1,0:T(8,128)S(1)}, f32[384,128]{1,0:T(8,128)}, u32[]{:S(2)}) copy-start(f32[384,128]{1,0:T(8,128)} %get-tuple-element.35.refs_7_) | copy-start | bytes 589828
  12.0 0.9 %copy-start.11 = (f32[384,128]{1,0:T(8,128)S(1)}, f32[384,128]{1,0:T(8,128)}, u32[]{:S(2)}) copy-start(f32[384,128]{1,0:T(8,128)} %get-tuple-element.36.refs_8_) | copy-start | bytes 589828
  15.9 29.6 %collective-permute-start.5 = (bf16[256,640]{1,0:T(8,128)(2,1)}, bf16[256,640]{1,0:T(8,128)(2,1)}, u32[]{:S(2)}, u32[]{:S(2)}) collective-permute-start(bf16[256,640]{1,0:T(8,128)(2,1)} %get-tuple-element.46), channel_id=1, source_target_pairs={{0,16},{4,20},{8,24},{12,28},{16,0},{20,4},{24,8},{28,12},{1,17},{... | collective-permute-start | bytes 983048 | tf_op jit(solution)/shard_map/ppermute | solution.py:412
  20.6 0.8 %copy-start.6 = (bf16[384,512]{1,0:T(8,128)(2,1)}, bf16[384,512]{1,0:T(8,128)(2,1)S(1)}, u32[]{:S(2)}) copy-start(bf16[384,512]{1,0:T(8,128)(2,1)S(1)} %get-tuple-element.41.refs_0_.own_ref) | copy-start | bytes 1179652
  21.4 0.7 copy-start.8
  22.1 0.7 copy-start.12
  22.8 0.7 copy-start.14
  23.5 0.7 copy-start.18
  24.1 9.7 %copy-start.4 = (bf16[384,640]{1,0:T(8,128)(2,1)S(1)}, bf16[384,640]{1,0:T(8,128)(2,1)}, u32[]{:S(2)}) copy-start(bf16[384,640]{1,0:T(8,128)(2,1)} %get-tuple-element.34.refs_6_.own_ref) | copy-start | bytes 1474564
  24.1 9.7 %copy-start.7 = (bf16[384,512]{1,0:T(8,128)(2,1)S(1)}, bf16[384,512]{1,0:T(8,128)(2,1)}, u32[]{:S(2)}) copy-start(bf16[384,512]{1,0:T(8,128)(2,1)} %copy-done.6) | copy-start | bytes 1179652
  24.2 1.0 %copy-start.13 = (bf16[384,256]{1,0:T(8,128)(2,1)S(1)}, bf16[384,256]{1,0:T(8,128)(2,1)}, u32[]{:S(2)}) copy-start(bf16[384,256]{1,0:T(8,128)(2,1)} %copy-done.12) | copy-start | bytes 589828
  25.2 0.9 %copy-start.15 = (bf16[256,256]{1,0:T(8,128)(2,1)S(1)}, bf16[256,256]{1,0:T(8,128)(2,1)}, u32[]{:S(2)}) copy-start(bf16[256,256]{1,0:T(8,128)(2,1)} %copy-done.14) | copy-start | bytes 393220
  27.4 27.3 %all-to-all-start = ((bf16[4,2,96,256]{3,2,1,0:T(8,128)(2,1)}), bf16[4,2,96,256]{3,2,1,0:T(8,128)(2,1)S(1)}, u32[]{:S(2)}, u32[]{:S(2)}) async-start(bf16[4,2,96,256]{3,2,1,0:T(8,128)(2,1)} %shard_map.88), calls=%async_computation | async-start | bytes 786432 | tf_op jit(solution)/shard_map/all_to_all | solution.py:414
  30.9 19.3 %collective-permute-start.9 = (bf16[256,512]{1,0:T(8,128)(2,1)}, bf16[256,512]{1,0:T(8,128)(2,1)S(1)}, u32[]{:S(2)}, u32[]{:S(2)}) collective-permute-start(bf16[256,512]{1,0:T(8,128)(2,1)} %copy-done.18), channel_id=1, source_target_pairs={{0,16},{4,20},{8,24},{12,28},{16,0},{20,4},{24,8},{28,12},{1,17},{... | collective-permute-start | bytes 786440 | tf_op jit(solution)/shard_map/ppermute | solution.py:412
  35.0 28.5 %copy-start.9 = (bf16[384,512]{1,0:T(8,128)(2,1)S(1)}, bf16[384,512]{1,0:T(8,128)(2,1)}, u32[]{:S(2)}) copy-start(bf16[384,512]{1,0:T(8,128)(2,1)} %copy-done.8) | copy-start | bytes 1179652
  35.0 10.5 %collective-permute-start.2 = (bf16[96,640]{1,0:T(8,128)(2,1)S(1)}, bf16[96,640]{1,0:T(8,128)(2,1)S(1)}, u32[]{:S(2)}, u32[]{:S(2)}) collective-permute-start(bf16[96,640]{1,0:T(8,128)(2,1)S(1)} %get-tuple-element.43), channel_id=1, source_target_pairs={{0,1},{1,0},{2,3},{3,2},{4,5},{5,4},{6,7},{7,6},{8,9},{9,8},{10,11... | collective-permute-start | bytes 368648 | tf_op jit(solution)/shard_map/ppermute | solution.py:436
  35.2 16.6 %collective-permute-start.3 = (bf16[96,640]{1,0:T(8,128)(2,1)S(1)}, bf16[96,640]{1,0:T(8,128)(2,1)S(1)}, u32[]{:S(2)}, u32[]{:S(2)}) collective-permute-start(bf16[96,640]{1,0:T(8,128)(2,1)S(1)} %get-tuple-element.44), channel_id=1, source_target_pairs={{0,2},{1,3},{2,0},{3,1},{4,6},{5,7},{6,4},{7,5},{8,10},{9,11},{10,... | collective-permute-start | bytes 368648 | tf_op jit(solution)/shard_map/ppermute | solution.py:436
  37.1 14.7 %collective-permute-start.4 = (bf16[96,640]{1,0:T(8,128)(2,1)S(1)}, bf16[96,640]{1,0:T(8,128)(2,1)S(1)}, u32[]{:S(2)}, u32[]{:S(2)}) collective-permute-start(bf16[96,640]{1,0:T(8,128)(2,1)S(1)} %get-tuple-element.45), channel_id=1, source_target_pairs={{0,3},{1,2},{2,1},{3,0},{4,7},{5,6},{6,5},{7,4},{8,11},{9,10},{10,... | collective-permute-start | bytes 368648 | tf_op jit(solution)/shard_map/ppermute | solution.py:436
  46.7 5.1 %collective-permute-start.6 = (bf16[96,640]{1,0:T(8,128)(2,1)S(1)}, bf16[96,640]{1,0:T(8,128)(2,1)S(1)}, u32[]{:S(2)}, u32[]{:S(2)}) collective-permute-start(bf16[96,640]{1,0:T(8,128)(2,1)S(1)} %get-tuple-element.48), channel_id=1, source_target_pairs={{0,1},{1,0},{2,3},{3,2},{4,5},{5,4},{6,7},{7,6},{8,9},{9,8},{10,11... | collective-permute-start | bytes 368648 | tf_op jit(solution)/shard_map/ppermute | solution.py:436
  46.8 15.4 %collective-permute-start.13 = (bf16[256,512]{1,0:T(8,128)(2,1)}, bf16[256,512]{1,0:T(8,128)(2,1)S(1)}, u32[]{:S(2)}, u32[]{:S(2)}) collective-permute-start(bf16[256,512]{1,0:T(8,128)(2,1)} %get-tuple-element.57), channel_id=1, source_target_pairs={{0,16},{4,20},{8,24},{12,28},{16,0},{20,4},{24,8},{28,12},{1,17},{... | collective-permute-start | bytes 786440 | tf_op jit(solution)/shard_map/ppermute | solution.py:412
  50.2 12.0 %collective-permute-start.7 = (bf16[96,640]{1,0:T(8,128)(2,1)S(1)}, bf16[96,640]{1,0:T(8,128)(2,1)S(1)}, u32[]{:S(2)}, u32[]{:S(2)}) collective-permute-start(bf16[96,640]{1,0:T(8,128)(2,1)S(1)} %get-tuple-element.49), channel_id=1, source_target_pairs={{0,2},{1,3},{2,0},{3,1},{4,6},{5,7},{6,4},{7,5},{8,10},{9,11},{10,... | collective-permute-start | bytes 368648 | tf_op jit(solution)/shard_map/ppermute | solution.py:436
  51.8 11.7 %collective-permute-start.8 = (bf16[96,640]{1,0:T(8,128)(2,1)S(1)}, bf16[96,640]{1,0:T(8,128)(2,1)S(1)}, u32[]{:S(2)}, u32[]{:S(2)}) collective-permute-start(bf16[96,640]{1,0:T(8,128)(2,1)S(1)} %get-tuple-element.50), channel_id=1, source_target_pairs={{0,3},{1,2},{2,1},{3,0},{4,7},{5,6},{6,5},{7,4},{8,11},{9,10},{10,... | collective-permute-start | bytes 368648 | tf_op jit(solution)/shard_map/ppermute | solution.py:436
  52.5 11.1 %collective-permute-start.10 = (bf16[96,512]{1,0:T(8,128)(2,1)S(1)}, bf16[96,512]{1,0:T(8,128)(2,1)S(1)}, u32[]{:S(2)}, u32[]{:S(2)}) collective-permute-start(bf16[96,512]{1,0:T(8,128)(2,1)S(1)} %get-tuple-element.53), channel_id=1, source_target_pairs={{0,1},{1,0},{2,3},{3,2},{4,5},{5,4},{6,7},{7,6},{8,9},{9,8},{10,11... | collective-permute-start | bytes 294920 | tf_op jit(solution)/shard_map/ppermute | solution.py:436
  53.1 12.0 %collective-permute-start.11 = (bf16[96,512]{1,0:T(8,128)(2,1)S(1)}, bf16[96,512]{1,0:T(8,128)(2,1)S(1)}, u32[]{:S(2)}, u32[]{:S(2)}) collective-permute-start(bf16[96,512]{1,0:T(8,128)(2,1)S(1)} %get-tuple-element.54), channel_id=1, source_target_pairs={{0,2},{1,3},{2,0},{3,1},{4,6},{5,7},{6,4},{7,5},{8,10},{9,11},{10,... | collective-permute-start | bytes 294920 | tf_op jit(solution)/shard_map/ppermute | solution.py:436
  62.2 11.8 %collective-permute-start = (bf16[4,96,256]{2,1,0:T(8,128)(2,1)S(1)}, bf16[4,96,256]{2,1,0:T(8,128)(2,1)S(1)}, u32[]{:S(2)}, u32[]{:S(2)}) collective-permute-start(bf16[4,96,256]{2,1,0:T(8,128)(2,1)S(1)} %slice_bitcast_fusion), channel_id=1, source_target_pairs={{0,16},{4,20},{8,24},{12,28},{16,0},{20,4},{24,8},{28,12},{1,17},{... | collective-permute-start | bytes 589832 | tf_op jit(solution)/shard_map/ppermute | solution.py:415
  62.2 4.9 %collective-permute-start.12 = (bf16[96,512]{1,0:T(8,128)(2,1)S(1)}, bf16[96,512]{1,0:T(8,128)(2,1)S(1)}, u32[]{:S(2)}, u32[]{:S(2)}) collective-permute-start(bf16[96,512]{1,0:T(8,128)(2,1)S(1)} %get-tuple-element.55), channel_id=1, source_target_pairs={{0,3},{1,2},{2,1},{3,0},{4,7},{5,6},{6,5},{7,4},{8,11},{9,10},{10,... | collective-permute-start | bytes 294920 | tf_op jit(solution)/shard_map/ppermute | solution.py:436
  64.2 2.8 %collective-permute-start.14 = (bf16[96,512]{1,0:T(8,128)(2,1)S(1)}, bf16[96,512]{1,0:T(8,128)(2,1)S(1)}, u32[]{:S(2)}, u32[]{:S(2)}) collective-permute-start(bf16[96,512]{1,0:T(8,128)(2,1)S(1)} %get-tuple-element.59), channel_id=1, source_target_pairs={{0,1},{1,0},{2,3},{3,2},{4,5},{5,4},{6,7},{7,6},{8,9},{9,8},{10,11... | collective-permute-start | bytes 294920 | tf_op jit(solution)/shard_map/ppermute | solution.py:436
  64.8 5.7 %collective-permute-start.15 = (bf16[96,512]{1,0:T(8,128)(2,1)S(1)}, bf16[96,512]{1,0:T(8,128)(2,1)S(1)}, u32[]{:S(2)}, u32[]{:S(2)}) collective-permute-start(bf16[96,512]{1,0:T(8,128)(2,1)S(1)} %get-tuple-element.60), channel_id=1, source_target_pairs={{0,2},{1,3},{2,0},{3,1},{4,6},{5,7},{6,4},{7,5},{8,10},{9,11},{10,... | collective-permute-start | bytes 294920 | tf_op jit(solution)/shard_map/ppermute | solution.py:436
  65.1 5.6 %collective-permute-start.16 = (bf16[96,512]{1,0:T(8,128)(2,1)S(1)}, bf16[96,512]{1,0:T(8,128)(2,1)S(1)}, u32[]{:S(2)}, u32[]{:S(2)}) collective-permute-start(bf16[96,512]{1,0:T(8,128)(2,1)S(1)} %get-tuple-element.61), channel_id=1, source_target_pairs={{0,3},{1,2},{2,1},{3,0},{4,7},{5,6},{6,5},{7,4},{8,11},{9,10},{10,... | collective-permute-start | bytes 294920 | tf_op jit(solution)/shard_map/ppermute | solution.py:436

commit v4 on v3

--- a/solution.py
+++ b/solution.py
@@ -11,7 +11,6 @@
 HEAD_SIZE = 128
 CAP = 2
 HIDDEN = -1e30
-AT_ONCE = ()
 FULL_VMEM, SOME_VMEM, LITTLE_VMEM = (60 << 20, 30 << 20, 8 << 20)
 PACK = 4
 NO_COST = pl.CostEstimate(flops=1000, bytes_accessed=1000, transcendentals=0)
@@ -206,8 +205,8 @@
     return pairs_of(out[: 2 * len(sets)]), carried
 
 
-def sort_kernel(block_count, block_rows, half_axis, peers, in_order, position_ref, mapping_ref, own_ref, arrived_ref, *refs):
-    outs = [refs[-1].at[p] for p in range(peers)] if in_order else refs[-peers:]
+def sort_kernel(block_count, block_rows, half_axis, peers, widths, position_ref, mapping_ref, *refs):
+    sources, outs = pairs_of(refs[: 2 * len(widths)]), refs[-peers:]
     at, peer = position_ref[0], position_ref[1]
     partner = lax.rem(at + half_axis, 2 * half_axis)
     arrived_slot = [jnp.int32(-1)] * block_count
@@ -218,34 +217,36 @@
     share = block_count * block_rows // peers
     step = math.gcd(share, block_rows)
     for hop, out_ref in enumerate(outs):
-        to_peer = hop if in_order else jnp.bitwise_xor(peer, hop)
+        to_peer = jnp.bitwise_xor(peer, hop)
         for piece in range(share // step):
             row = to_peer * share + piece * step
-            block = lax.div(jnp.int32(row), jnp.int32(block_rows))
+            block = lax.div(row, block_rows)
             slot = jnp.int32(-1)
             for b in range(block_count):
                 slot = jnp.where(block == b, arrived_slot[b], slot)
-            from_own = own_ref[aligned(row, step, step), :]
-            from_pair = arrived_ref[
-                aligned(jnp.maximum(slot, 0) * block_rows + lax.rem(jnp.int32(row), jnp.int32(block_rows)), step, step), :
-            ]
-            out_ref[piece * step : (piece + 1) * step, :] = jnp.where(slot >= 0, from_pair, from_own)
-
-
-def sort_rows(position, mapping, own, arrived, after, block_count, half_axis, peers, in_order):
-    rows, columns = own.shape
-    if in_order:
-        out = [jax.ShapeDtypeStruct((peers, rows // peers, columns), own.dtype)]
-    else:
-        out = [jax.ShapeDtypeStruct((rows // peers, columns), own.dtype)] * peers
+            at_pair = jnp.maximum(slot, 0) * block_rows + lax.rem(row, block_rows)
+            column = 0
+            for (own_ref, arrived_ref), width in zip(sources, widths):
+                from_own = own_ref[aligned(row, step, step), :]
+                from_pair = arrived_ref[aligned(at_pair, step, step), :]
+                out_ref[piece * step : (piece + 1) * step, column : column + width] = jnp.where(
+                    slot >= 0, from_pair, from_own
+                )
+                column += width
+
+
+def sort_rows(position, mapping, sources, after, block_count, half_axis, peers):
+    rows = sources[0][0].shape[0]
+    widths = [own.shape[1] for own, _ in sources]
+    out = jax.ShapeDtypeStruct((rows // peers, sum(widths)), sources[0][0].dtype)
     return pl.pallas_call(
-        functools.partial(sort_kernel, block_count, rows // block_count, half_axis, peers, in_order),
-        in_specs=[IN_SMEM, IN_SMEM, IN_VMEM, IN_VMEM] + [ANYWHERE] * len(after),
-        out_specs=[IN_VMEM] * len(out),
-        out_shape=out,
+        functools.partial(sort_kernel, block_count, rows // block_count, half_axis, peers, widths),
+        in_specs=[IN_SMEM, IN_SMEM] + [IN_VMEM] * (2 * len(sources)) + [ANYWHERE] * len(after),
+        out_specs=[IN_VMEM] * peers,
+        out_shape=[out] * peers,
         compiler_params=pltpu.CompilerParams(vmem_limit_bytes=LITTLE_VMEM),
         cost_estimate=NO_COST,
-    )(position, mapping, own, arrived, *after)
+    )(position, mapping, *(x for source in sources for x in source), *after)
 
 
 def place_kernel(peers, columns_here, places, held, position_ref, *refs):
@@ -253,11 +254,10 @@
     outs, sem = refs[-len(columns_here) - 1 : -1], refs[-1]
     peer = position_ref[1]
     copies = []
-    for in_order, parts in places:
-        chunk = pieces.pop(0) if in_order else None
+    for parts in places:
         for hop in range(peers):
-            from_peer = hop if in_order else jnp.bitwise_xor(peer, hop)
-            piece = chunk.at[hop] if in_order else pieces.pop(0)
+            from_peer = jnp.bitwise_xor(peer, hop)
+            piece = pieces.pop(0)
             for at, size, out, column in parts:
                 copies.append(
                     pltpu.make_async_copy(
@@ -271,7 +271,7 @@
         copy.wait()
 
 
-def spread_kernel(block_count, block_rows, half_axis, peers, position_ref, mapping_ref, own_ref, send_ref, out_ref):
+def spread_kernel(block_count, block_rows, half_axis, peers, position_ref, mapping_ref, own_ref, send_ref, _, out_ref):
     at = position_ref[0]
     partner = lax.rem(at + half_axis, 2 * half_axis)
     send_slot = [jnp.int32(0)] * block_count
@@ -289,21 +289,31 @@
             out_ref[peer, 1, piece * step : (piece + 1) * step, :] = send_ref[aligned(at_send, step, step), :]
 
 
-def spread_rows(position, mapping, own, send, half_axis, block_count, peers):
+def spread_rows(position, mapping, own, send, after, half_axis, block_count, peers):
     rows, columns = own.shape
     return pl.pallas_call(
         functools.partial(spread_kernel, block_count, rows // block_count, half_axis, peers),
-        in_specs=[IN_SMEM, IN_SMEM, IN_VMEM, IN_VMEM],
+        in_specs=[IN_SMEM, IN_SMEM, IN_VMEM, IN_VMEM, ANYWHERE],
         out_specs=IN_VMEM,
         out_shape=jax.ShapeDtypeStruct((peers, 2, rows // peers, columns), own.dtype),
         compiler_params=pltpu.CompilerParams(vmem_limit_bytes=LITTLE_VMEM),
         cost_estimate=NO_COST,
-    )(position, mapping, own, send)
-
-
-def place_last_kernel(block_count, block_rows, peers, columns_here, parts, *refs):
+    )(position, mapping, own, send, after)
+
+
+def place_last_kernel(block_count, block_rows, peers, columns_here, parts, piece_parts, *refs):
     position_ref, mapping_ref, spread_ref, arrived_ref, *refs = refs
+    pieces = refs[:peers]
     outs, merged_ref, sem = refs[-len(columns_here) - 2 : -2], refs[-2], refs[-1]
+    copies = []
+    for hop, piece in enumerate(pieces):
+        from_peer = jnp.bitwise_xor(position_ref[1], hop)
+        for at, size, out, column in piece_parts:
+            start = aligned(from_peer * columns_here[out] + column, size, HEAD_SIZE)
+            copies.append(
+                pltpu.make_async_copy(piece.at[:, at : at + size], outs[out].at[:, start], sem.at[len(copies)])
+            )
+            copies[-1].start()
     here = own_sources(mapping_ref, position_ref[0], block_count)
     share = block_count * block_rows // peers
     step = math.gcd(share, block_rows)
@@ -315,7 +325,6 @@
         rows = slice(piece * step, (piece + 1) * step)
         for peer in range(peers):
             merged_ref[peer, rows, :] = jnp.where(source >= 0, spread_ref[peer, 0, rows, :], arrived_ref[peer, rows, :])
-    copies = []
     for peer in range(peers):
         for at, size, out, column in parts:
             start = peer * columns_here[out] + column
@@ -329,23 +338,23 @@
         copy.wait()
 
 
-def place_last(position, mapping, spread, arrived, parts, columns_here, held, block_count):
+def place_last(position, mapping, spread, arrived, parts, pieces, piece_parts, columns_here, held, block_count):
     peers, _, share, columns = spread.shape
     return pl.pallas_call(
         functools.partial(
-            place_last_kernel, block_count, share * peers // block_count, peers, columns_here, parts
+            place_last_kernel, block_count, share * peers // block_count, peers, columns_here, parts, piece_parts
         ),
-        in_specs=[IN_SMEM, IN_SMEM, IN_VMEM, IN_VMEM] + [ANYWHERE] * len(held),
+        in_specs=[IN_SMEM, IN_SMEM] + [IN_VMEM] * (2 + peers) + [ANYWHERE] * len(held),
         out_specs=[ANYWHERE] * len(held),
         out_shape=[jax.ShapeDtypeStruct(h.shape, h.dtype) for h in held],
-        input_output_aliases={4 + i: i for i in range(len(held))},
+        input_output_aliases={4 + peers + i: i for i in range(len(held))},
         scratch_shapes=[
             pltpu.VMEM((peers, share, columns), spread.dtype),
-            pltpu.SemaphoreType.DMA((peers * len(parts),)),
+            pltpu.SemaphoreType.DMA((peers * (len(parts) + len(piece_parts)),)),
         ],
         compiler_params=pltpu.CompilerParams(vmem_limit_bytes=LITTLE_VMEM),
         cost_estimate=NO_COST,
-    )(position, mapping, spread, arrived, *held)
+    )(position, mapping, spread, arrived, *pieces, *held)
 
 
 def joined_parts(parts):
@@ -361,7 +370,7 @@
 def place_columns(position, pieces, places, columns_here, held, peers):
     rows, dtype = pieces[0][0].shape[-2], pieces[0][0].dtype
     flat = [p for chunk in pieces for p in chunk]
-    count = peers * sum(len(parts) for _, parts in places)
+    count = peers * sum(len(parts) for parts in places)
     out_shape = [jax.ShapeDtypeStruct((rows, peers * c), dtype) for c in columns_here]
     return pl.pallas_call(
         functools.partial(place_kernel, peers, columns_here, places, len(held)),
@@ -376,15 +385,18 @@
 
 
 def plan_of(groups, repeats):
-    lead, cut = max(1, 5 * repeats // 8), max(1, 4 * repeats // 8)
+    lead, cut = max(1, 4 * repeats // 8), max(1, 4 * repeats // 8)
     heads = list(range(repeats))
     kernels = [(0, 0, lead, [heads[:lead]]), (0, lead, repeats - lead, [heads[: repeats - lead]])]
     for group in range(1, groups):
         kernels.append((group, 0, repeats, [heads[:cut], heads[cut:]]))
     for group in range(groups - 1):
-        kernels[group + 1][3][-1].append(keys_and_values(group))
+        kernels[group + 2][3][0].append(keys_and_values(group))
     kernels[-1][3].append([keys_and_values(groups - 1)])
     return kernels
+
+
+TOGETHER = 1
 
 
 def on_device(queries, key_layout_rows, value_layout_rows, output_gradient, doc_starts, block_mapping):
@@ -398,19 +410,20 @@
     position = jnp.stack([lax.axis_index("ctx"), lax.axis_index("tensor")]).astype(jnp.int32)
     pairs = [(i, (i + half_axis) % axis_length) for i in range(axis_length)]
 
-    carried, after, sent = {}, key_layout_rows, []
-    for number, (group, start, heads, sets) in enumerate(plan_of(groups, repeats)):
+    carried, after, sent, landed = {}, key_layout_rows, [], []
+    kernels = plan_of(groups, repeats)
+    for number, (group, start, heads, sets) in enumerate(kernels):
         made, carried = grads_chunk(
             doc_starts, block_mapping, queries, output_gradient, key_layout_rows, value_layout_rows,
             after, carried, group * repeats + start, heads, group, sets, FULL_VMEM if number == 0 else SOME_VMEM,
         )
         after = made[0][0]
         for units, (own, send) in zip(sets, made):
-            sent.append((group * repeats + start, units, own, send))
-
-    *sent, (_, last_units, own, send) = sent
-    sent = [(start, units, own, lax.ppermute(send, "ctx", pairs)) for start, units, own, send in sent]
-    spread = spread_rows(position, block_mapping, own, send, half_axis, block_count, peers)
+            sent.append((group * repeats + start, units, own))
+            if number < len(kernels) - 1 or len(sent) < sum(len(k[3]) for k in kernels):
+                landed.append(lax.ppermute(send, "ctx", pairs))
+    _, last_units, own = sent[-1]
+    spread = spread_rows(position, block_mapping, own, send, landed[0], half_axis, block_count, peers)
     spread = lax.all_to_all(spread, "tensor", split_axis=0, concat_axis=0, tiled=True)
     last_arrived = lax.ppermute(spread[:, 1], "ctx", pairs)
 
@@ -426,23 +439,28 @@
         return joined_parts(parts)
 
     order, pieces, places = [after], [], []
-    for index, (start, units, own, arrived) in enumerate(sent):
-        at_once = index in AT_ONCE
-        got = sort_rows(position, block_mapping, own, arrived, order, block_count, half_axis, peers, at_once)
-        if at_once:
-            got = [lax.all_to_all(got[0], "tensor", split_axis=0, concat_axis=0, tiled=True)]
-        else:
-            got = [got[0]] + [
-                lax.ppermute(got[hop], "tensor", [(i, i ^ hop) for i in range(peers)]) for hop in range(1, peers)
-            ]
+    chunks = list(zip(sent, landed))
+    for chunk in [chunks[:TOGETHER]] + [[c] for c in chunks[TOGETHER:]]:
+        sources = [(own, arrived) for (_, _, own), arrived in chunk]
+        parts = sort_rows(position, block_mapping, sources, order, block_count, half_axis, peers)
+        got = [parts[0]] + [
+            lax.ppermute(parts[hop], "tensor", [(i, i ^ hop) for i in range(peers)]) for hop in range(1, peers)
+        ]
         order = [got[0], got[1]] + (list(pieces[-1][2:]) if pieces else [])
         pieces.append(got)
-        places.append((at_once, parts_of(start, units)))
+        places.append([])
+        before = 0
+        for (start, units, own), _ in chunk:
+            places[-1] += [(before + at, size, out, column) for at, size, out, column in parts_of(start, units)]
+            before += own.shape[1]
+        places[-1] = joined_parts(places[-1])
     columns_here = [queries.shape[1], key_layout_rows.shape[1], value_layout_rows.shape[1]]
-    held = place_columns(position, pieces, places, columns_here, [], peers)
+    held = place_columns(position, pieces[:-1], places[:-1], columns_here, [], peers)
     parts = parts_of(0, last_units)
     return tuple(
-        place_last(position, block_mapping, spread, last_arrived, parts, columns_here, held, block_count)
+        place_last(
+            position, block_mapping, spread, last_arrived, parts, pieces[-1], places[-1], columns_here, held, block_count
+        )
     )
 
 

time: 75.7 us -> 73.7 us (0.974)
  waiting for transfers between devices: 25.1 us -> 21.8 us
  local copies, waits for them, and re-layouts: 8.35 us -> 10.1 us
  starting transfers between devices: 19.8 us -> 18.8 us
    ppermute x16, waiting for transfers between devices: 23.9 us -> 20.9 us  [the longest x4 14.2 us: on_device(): landed.append(lax.ppermute(send, 'ctx', pairs))]
    unnamed x38 -> x44, local copies, waits for them, and re-layouts: 8.33 us -> 10.1 us
    pallas_call x4, Pallas kernels: 3.58 us -> 4.84 us  [sort_rows(): pl.pallas_call(functools.partial(sort_kernel, block_count, rows // block_...]
    pallas_call x3, Pallas kernels: 12.9 us -> 11.8 us  [grads_chunk(): pl.pallas_call(functools.partial(grads_kernel, block_count, block_rows, g...]
    ppermute x16, starting transfers between devices: 16.4 us -> 15.3 us  [the longest x12 8.38 us: on_device(): lax.ppermute(parts[hop], 'tensor', [(i, i ^ hop) for i in range(peers)])]
  transfers between devices with their start and end apart: 18 -> 18, of which waited for: 7 -> 10; matrix products, arithmetic and copies ran while one was open for 0% -> 0% of each run, Pallas kernels for 19% -> 22%
where the time goes in v4:
time: 73.7 us; the launch traced here: 72.9 us
  waiting for transfers between devices  21.8 us (30%)
  Pallas kernels  21.2 us (29%)
  starting transfers between devices  18.8 us (26%)
  local copies, waits for them, and re-layouts  10.1 us (14%)
  between operations  0.8 us (1%)
    ppermute x4, waiting for transfers between devices, on_device(): landed.append(lax.ppermute(send, 'ctx', pairs))  14.2 us
    pallas_call x3, Pallas kernels, grads_chunk(): pl.pallas_call(functools.partial(grads_kernel, block_count, block_rows, g...  11.8 us
    unnamed x44, local copies, waits for them, and re-layouts  10.1 us
    ppermute x12, starting transfers between devices, on_device(): lax.ppermute(parts[hop], 'tensor', [(i, i ^ hop) for i in range(peers)])  8.38 us
    ppermute x4, starting transfers between devices, on_device(): landed.append(lax.ppermute(send, 'ctx', pairs))  6.96 us
    ppermute x12, waiting for transfers between devices, on_device(): lax.ppermute(parts[hop], 'tensor', [(i, i ^ hop) for i in range(peers)])  6.68 us
    pallas_call x4, Pallas kernels, sort_rows(): pl.pallas_call(functools.partial(sort_kernel, block_count, rows // block_...  4.84 us
    all_to_all x1, starting transfers between devices, on_device(): lax.all_to_all(spread, 'tensor', split_axis=0, concat_axis=0, tiled=True)  3.46 us
  transfers between devices with their start and end apart: 18, of which 10 were waited for; matrix products, arithmetic and copies ran while one was open for 0% of the time, Pallas kernels for 22%

profile of v4, /device:TPU:0, one launch (start us, length us, event | category | flops | bytes accessed | tf_op | source)
XLA Modules:
  0.0 72.9 jit_solution(12497465815068184406)
XLA Ops:
  0.7 4.0 %shard_map.85 = (bf16[384,512]{1,0:T(8,128)(2,1)}, bf16[256,512]{1,0:T(8,128)(2,1)}, f32[384,128]{1,0:T(8,128)}, f32[384,128]{1,0:T(8,128)}) custom-call(s32[3]{0:T(128)} %refs_0_.5, s32[24]{0:T(128)} %refs_1_.7, bf16[384,2048]{1,0:T(8,128)(2,1)} %refs_2_.5, bf16[384,2048]{1,0:T(8,128)(2,1)} %refs_3_.5, bf16[384,256]{1,0:T(8,128)(2,1)} %refs_4_.5, ...), custom_call_target="tpu_custom_call" | custom-call | flops 1000 | bytes 1000 | tf_op jit(solution)/shard_map/pallas_call | solution.py:185
  4.7 4.0 %collective-permute-start = (bf16[256,512]{1,0:T(8,128)(2,1)}, bf16[256,512]{1,0:T(8,128)(2,1)}, u32[]{:S(2)}, u32[]{:S(2)}) collective-permute-start(bf16[256,512]{1,0:T(8,128)(2,1)} %get-tuple-element.44), channel_id=1, source_target_pairs={{0,16},{4,20},{8,24},{12,28},{16,0},{20,4},{24,8},{28,12},{1,17},{... | collective-permute-start | bytes 786440 | tf_op jit(solution)/shard_map/ppermute | solution.py:424
  8.7 0.0 copy-done.1
  8.8 0.0 copy-start.6
  8.8 1.0 %copy-done.6 = bf16[384,512]{1,0:T(8,128)(2,1)S(1)} copy-done((bf16[384,512]{1,0:T(8,128)(2,1)S(1)}, bf16[384,512]{1,0:T(8,128)(2,1)}, u32[]{:S(2)}) %copy-start.6) | copy-done | bytes 393240
  9.8 0.9 %copy-done.10 = f32[384,128]{1,0:T(8,128)S(1)} copy-done((f32[384,128]{1,0:T(8,128)S(1)}, f32[384,128]{1,0:T(8,128)}, u32[]{:S(2)}) %copy-start.10) | copy-done | bytes 196632
  10.7 0.9 %copy-done.11 = f32[384,128]{1,0:T(8,128)S(1)} copy-done((f32[384,128]{1,0:T(8,128)S(1)}, f32[384,128]{1,0:T(8,128)}, u32[]{:S(2)}) %copy-start.11) | copy-done | bytes 196632
  11.6 0.7 copy-done.16
  12.3 0.7 copy-done.20
  12.9 2.9 %shard_map.86 = (bf16[384,512]{1,0:T(8,128)(2,1)S(1)}, bf16[256,512]{1,0:T(8,128)(2,1)}, f32[384,128]{1,0:T(8,128)S(1)}, f32[384,128]{1,0:T(8,128)S(1)}) custom-call(s32[3]{0:T(128)S(1)} %copy-done.20, s32[24]{0:T(128)S(1)} %copy-done.16, bf16[384,2048]{1,0:T(8,128)(2,1)S(1)} %copy-done, bf16[384,2048]{1,0:T(8,128)(2,1)S(1)} %copy-done.1, ...), custom_call_target="tpu_custom_call" | custom-call | flops 1000 | bytes 1000 | tf_op jit(solution)/shard_map/pallas_call | solution.py:185
  15.8 0.0 collective-permute-start.4
  15.8 4.9 %shard_map.87 = (bf16[384,768]{1,0:T(8,128)(2,1)S(1)}, bf16[256,768]{1,0:T(8,128)(2,1)}, bf16[384,512]{1,0:T(8,128)(2,1)S(1)}, bf16[256,512]{1,0:T(8,128)(2,1)S(...) custom-call(s32[3]{0:T(128)S(1)} %copy-done.20, s32[24]{0:T(128)S(1)} %copy-done.16, ...), custom_call_target="tpu_custom_call" | custom-call | flops 1000 | bytes 1000 | tf_op jit(solution)/shard_map/pallas_call | solution.py:185
  20.7 0.7 %copy-done.8 = bf16[384,512]{1,0:T(8,128)(2,1)} copy-done((bf16[384,512]{1,0:T(8,128)(2,1)}, bf16[384,512]{1,0:T(8,128)(2,1)S(1)}, u32[]{:S(2)}) %copy-start.8) | copy-done | bytes 393240
  21.4 0.7 copy-done.12
  22.1 0.7 copy-done.14
  22.8 0.7 copy-done.21
  23.5 2.9 %collective-permute-start.3 = (bf16[256,768]{1,0:T(8,128)(2,1)}, bf16[256,768]{1,0:T(8,128)(2,1)S(1)}, u32[]{:S(2)}, u32[]{:S(2)}) collective-permute-start(bf16[256,768]{1,0:T(8,128)(2,1)} %get-tuple-element.48), channel_id=1, source_target_pairs={{0,16},{4,20},{8,24},{12,28},{16,0},{20,4},{24,8},{28,12},{1,17},{... | collective-permute-start | bytes 1179656 | tf_op jit(solution)/shard_map/ppermute | solution.py:424
  26.4 0.1 pad_add_fusion.position_ref.refs_0_
  26.5 1.0 %collective-permute-done._.refs_1_ = bf16[256,512]{1,0:T(8,128)(2,1)} collective-permute-done((bf16[256,512]{1,0:T(8,128)(2,1)}, bf16[256,512]{1,0:T(8,128)(2,1)}, u32[]{:S(2)}, u32[]{:S(2)}) %collective-permute-start) | collective-permute-done | bytes 262176 | tf_op jit(solution)/shard_map/ppermute | solution.py:424
  27.4 0.9 %copy-done.13 = bf16[384,256]{1,0:T(8,128)(2,1)S(1)} copy-done((bf16[384,256]{1,0:T(8,128)(2,1)S(1)}, bf16[384,256]{1,0:T(8,128)(2,1)}, u32[]{:S(2)}) %copy-start.13) | copy-done | bytes 196632
  28.4 0.9 %copy-done.15 = bf16[256,256]{1,0:T(8,128)(2,1)S(1)} copy-done((bf16[256,256]{1,0:T(8,128)(2,1)S(1)}, bf16[256,256]{1,0:T(8,128)(2,1)}, u32[]{:S(2)}) %copy-start.15) | copy-done | bytes 131096
  29.3 0.7 copy-done.17
  29.9 1.4 %shard_map.88 = bf16[4,2,96,256]{3,2,1,0:T(8,128)(2,1)} custom-call(s32[2]{0:T(128)S(1)} %pad_add_fusion.position_ref.refs_0_, s32[24]{0:T(128)S(1)} %copy-done.17, bf16[384,256]{1,0:T(8,128)(2,1)S(1)} %copy-done.13, bf16[256,256]{1,0:T(8,128)(2,1)S(1)} %copy-done.15, bf16[256,512]{1,0:T(8,128)(2,1)} %collective-permute-done._.refs_1_), custom_call_target="tpu_custom_call" | custom-call | flops 1000 | bytes 1000 | tf_op jit(solution)/shard_map/pallas_call | solution.py:294
  31.3 3.5 %all-to-all-start = ((bf16[4,2,96,256]{3,2,1,0:T(8,128)(2,1)}), bf16[4,2,96,256]{3,2,1,0:T(8,128)(2,1)S(1)}, u32[]{:S(2)}, u32[]{:S(2)}) async-start(bf16[4,2,96,256]{3,2,1,0:T(8,128)(2,1)} %shard_map.88), calls=%async_computation | async-start | bytes 786432 | tf_op jit(solution)/shard_map/all_to_all | solution.py:427
  34.8 0.0 copy-start.18
  34.8 0.6 copy-done.18
  35.4 1.1 %shard_map.89 = (bf16[96,512]{1,0:T(8,128)(2,1)S(1)}, bf16[96,512]{1,0:T(8,128)(2,1)S(1)}, bf16[96,512]{1,0:T(8,128)(2,1)S(1)}, bf16[96,512]{1,0:T(8,128)(2,1)S(1)}) custom-call(s32[2]{0:T(128)S(1)} %pad_add_fusion.position_ref.refs_0_, s32[24]{0:T(128)S(1)} %copy-done.18, bf16[384,512]{1,0:T(8,128)(2,1)S(1)} %copy-done.7, ...), custom_call_target="tpu_custom_call" | custom-call | flops 1000 | bytes 1000 | tf_op jit(solution)/shard_map/pallas_call | solution.py:242
  36.5 0.0 copy-start.19
  36.5 0.5 collective-permute-start.5
  37.1 1.7 %collective-permute-start.7 = (bf16[96,512]{1,0:T(8,128)(2,1)S(1)}, bf16[96,512]{1,0:T(8,128)(2,1)S(1)}, u32[]{:S(2)}, u32[]{:S(2)}) collective-permute-start(bf16[96,512]{1,0:T(8,128)(2,1)S(1)} %get-tuple-element.54), channel_id=1, source_target_pairs={{0,2},{1,3},{2,0},{3,1},{4,6},{5,7},{6,4},{7,5},{8,10},{9,11},{10,... | collective-permute-start | bytes 294920 | tf_op jit(solution)/shard_map/ppermute | solution.py:447
  38.7 0.0 collective-permute-start.8
  38.7 2.7 %collective-permute-done.4.refs_1_ = bf16[256,512]{1,0:T(8,128)(2,1)} collective-permute-done((bf16[256,512]{1,0:T(8,128)(2,1)}, bf16[256,512]{1,0:T(8,128)(2,1)}, u32[]{:S(2)}, u32[]{:S(2)}) %collective-permute-start.4) | collective-permute-done | bytes 262176 | tf_op jit(solution)/shard_map/ppermute | solution.py:424
  41.5 0.0 collective-permute-done.5.refs_3_.refs_1_
  41.5 1.8 %shard_map.90 = (bf16[96,512]{1,0:T(8,128)(2,1)S(1)}, bf16[96,512]{1,0:T(8,128)(2,1)S(1)}, bf16[96,512]{1,0:T(8,128)(2,1)}, bf16[96,512]{1,0:T(8,128)(2,1)}) custom-call(s32[2]{0:T(128)S(1)} %pad_add_fusion.position_ref.refs_0_, s32[24]{0:T(128)S(1)} %copy-done.18, bf16[384,512]{1,0:T(8,128)(2,1)S(1)} %copy-done.5, ...), custom_call_target="tpu_custom_call" | custom-call | flops 1000 | bytes 1000 | tf_op jit(solution)/shard_map/pallas_call | solution.py:242
  43.2 0.0 collective-permute-start.6
  43.2 0.0 collective-permute-start.2
  43.2 1.5 %collective-permute-done.7.refs_4_.refs_2_ = bf16[96,512]{1,0:T(8,128)(2,1)S(1)} collective-permute-done((bf16[96,512]{1,0:T(8,128)(2,1)S(1)}, bf16[96,512]{1,0:T(8,128)(2,1)S(1)}, u32[]{:S(2)}, u32[]{:S(2)}) %collective-permute-start.7) | collective-permute-done | bytes 98336 | tf_op jit(solution)/shard_map/ppermute | solution.py:447
  44.7 0.5 collective-permute-start.10
  45.2 0.7 collective-permute-done.8.refs_5_.refs_3_
  45.9 0.6 collective-permute-start.11
  46.4 9.0 %collective-permute-done.3.refs_1_ = bf16[256,768]{1,0:T(8,128)(2,1)S(1)} collective-permute-done((bf16[256,768]{1,0:T(8,128)(2,1)}, bf16[256,768]{1,0:T(8,128)(2,1)S(1)}, u32[]{:S(2)}, u32[]{:S(2)}) %collective-permute-start.3) | collective-permute-done | bytes 393248 | tf_op jit(solution)/shard_map/ppermute | solution.py:424
  55.4 0.0 collective-permute-done.6.refs_3_.refs_5_
  55.4 1.3 %shard_map.91 = (bf16[96,768]{1,0:T(8,128)(2,1)S(1)}, bf16[96,768]{1,0:T(8,128)(2,1)}, bf16[96,768]{1,0:T(8,128)(2,1)S(1)}, bf16[96,768]{1,0:T(8,128)(2,1)S(1)}) custom-call(s32[2]{0:T(128)S(1)} %pad_add_fusion.position_ref.refs_0_, s32[24]{0:T(128)S(1)} %copy-done.18, bf16[384,768]{1,0:T(8,128)(2,1)S(1)} %get-tuple-element.47.refs_2_.refs_0_, ...), custom_call_target="tpu_custom_call" | custom-call | flops 1000 | bytes 1000 | tf_op jit(solution)/shard_map/pallas_call | solution.py:242
  56.7 0.0 collective-permute-start.9
  56.7 1.9 %collective-permute-start.15 = (bf16[96,768]{1,0:T(8,128)(2,1)S(1)}, bf16[96,768]{1,0:T(8,128)(2,1)S(1)}, u32[]{:S(2)}, u32[]{:S(2)}) collective-permute-start(bf16[96,768]{1,0:T(8,128)(2,1)S(1)} %get-tuple-element.64), channel_id=1, source_target_pairs={{0,2},{1,3},{2,0},{3,1},{4,6},{5,7},{6,4},{7,5},{8,10},{9,11},{10,... | collective-permute-start | bytes 442376 | tf_op jit(solution)/shard_map/ppermute | solution.py:447
  58.6 0.0 all-to-all-done.refs_2_
  58.6 1.6 %collective-permute-done.2.refs_1_ = bf16[256,512]{1,0:T(8,128)(2,1)S(1)} collective-permute-done((bf16[256,512]{1,0:T(8,128)(2,1)}, bf16[256,512]{1,0:T(8,128)(2,1)S(1)}, u32[]{:S(2)}, u32[]{:S(2)}) %collective-permute-start.2) | collective-permute-done | bytes 262176 | tf_op jit(solution)/shard_map/ppermute | solution.py:424
  60.2 0.0 collective-permute-start.1
  60.2 0.0 collective-permute-done.10.refs_4_.refs_6_
  60.2 0.2 collective-permute-start.16
  60.4 0.0 collective-permute-done.11.refs_5_.refs_7_
  60.4 0.0 collective-permute-done.9.refs_3_.refs_9_
  60.4 0.7 shard_map.92
  61.1 1.6 %collective-permute-start.12 = (bf16[96,512]{1,0:T(8,128)(2,1)S(1)}, bf16[96,512]{1,0:T(8,128)(2,1)S(1)}, u32[]{:S(2)}, u32[]{:S(2)}) collective-permute-start(bf16[96,512]{1,0:T(8,128)(2,1)S(1)} %get-tuple-element.61), channel_id=1, source_target_pairs={{0,1},{1,0},{2,3},{3,2},{4,5},{5,4},{6,7},{7,6},{8,9},{9,8},{10,11... | collective-permute-start | bytes 294920 | tf_op jit(solution)/shard_map/ppermute | solution.py:447
  62.7 0.5 collective-permute-start.13
  63.1 0.0 collective-permute-done.15.refs_10_
  63.1 1.1 %collective-permute-start.14 = (bf16[96,512]{1,0:T(8,128)(2,1)S(1)}, bf16[96,512]{1,0:T(8,128)(2,1)S(1)}, u32[]{:S(2)}, u32[]{:S(2)}) collective-permute-start(bf16[96,512]{1,0:T(8,128)(2,1)S(1)} %get-tuple-element.63), channel_id=1, source_target_pairs={{0,3},{1,2},{2,1},{3,0},{4,7},{5,6},{6,5},{7,4},{8,11},{9,10},{10,... | collective-permute-start | bytes 294920 | tf_op jit(solution)/shard_map/ppermute | solution.py:447
  64.2 2.0 %collective-permute-done.16.refs_11_ = bf16[96,768]{1,0:T(8,128)(2,1)S(1)} collective-permute-done((bf16[96,768]{1,0:T(8,128)(2,1)S(1)}, bf16[96,768]{1,0:T(8,128)(2,1)S(1)}, u32[]{:S(2)}, u32[]{:S(2)}) %collective-permute-start.16) | collective-permute-done | bytes 147488 | tf_op jit(solution)/shard_map/ppermute | solution.py:447
  66.2 1.8 %shard_map.93 = (bf16[96,8192]{1,0:T(8,128)(2,1)}, bf16[96,1024]{1,0:T(8,128)(2,1)}, bf16[96,1024]{1,0:T(8,128)(2,1)}) custom-call(s32[2]{0:T(128)S(1)} %pad_add_fusion.position_ref.refs_0_, bf16[96,512]{1,0:T(8,128)(2,1)S(1)} %get-tuple-element.50.refs_2_.refs_0_, bf16[96,512]{1,0:T(8,128)(2,1)S(1)} %collective-permute-done.5.refs_3_.refs_1_, ...), custom_call_target="tpu_custom_call" | custom-call | flops 1000 | bytes 1000 | tf_op jit(solution)/shard_map/pallas_call | solution.py:375
  68.0 0.0 collective-permute-done.12.refs_5_
  68.0 0.6 collective-permute-done.13.refs_6_
  68.6 1.9 %collective-permute-done.14.refs_7_ = bf16[96,512]{1,0:T(8,128)(2,1)S(1)} collective-permute-done((bf16[96,512]{1,0:T(8,128)(2,1)S(1)}, bf16[96,512]{1,0:T(8,128)(2,1)S(1)}, u32[]{:S(2)}, u32[]{:S(2)}) %collective-permute-start.14) | collective-permute-done | bytes 98336 | tf_op jit(solution)/shard_map/ppermute | solution.py:447
  70.5 1.0 %collective-permute-done.1.refs_3_ = bf16[4,96,256]{2,1,0:T(8,128)(2,1)S(1)} collective-permute-done((bf16[4,96,256]{2,1,0:T(8,128)(2,1)S(1)}, bf16[4,96,256]{2,1,0:T(8,128)(2,1)S(1)}, u32[]{:S(2)}, u32[]{:S(2)}) %collective-permute-start.1) | collective-permute-done | bytes 196640 | tf_op jit(solution)/shard_map/ppermute | solution.py:428
  71.4 1.4 %shard_map.94 = (bf16[96,8192]{1,0:T(8,128)(2,1)}, bf16[96,1024]{1,0:T(8,128)(2,1)}, bf16[96,1024]{1,0:T(8,128)(2,1)}) custom-call(s32[2]{0:T(128)S(1)} %pad_add_fusion.position_ref.refs_0_, s32[24]{0:T(128)S(1)} %copy-done.19, bf16[4,2,96,256]{3,2,1,0:T(8,128)(2,1)S(1)} %all-to-all-done.refs_2_, ...), custom_call_target="tpu_custom_call", output_to_operand_aliasing={{0}: (8, {}), {1}: (9, {}), {2}: (10, {})} | custom-call | flops 1000 | bytes 1000 | tf_op jit(solution)/shard_map/pallas_call | solution.py:343
  (28 shorter events, 0.1 us)
Async XLA Ops:
  0.6 8.1 %copy-start.1 = (bf16[384,2048]{1,0:T(8,128)(2,1)S(1)}, bf16[384,2048]{1,0:T(8,128)(2,1)}, u32[]{:S(2)}) copy-start(bf16[384,2048]{1,0:T(8,128)(2,1)} %refs_3_.5) | copy-start | bytes 4718596
  0.6 8.1 %copy-start.3 = (bf16[384,256]{1,0:T(8,128)(2,1)S(1)}, bf16[384,256]{1,0:T(8,128)(2,1)}, u32[]{:S(2)}) copy-start(bf16[384,256]{1,0:T(8,128)(2,1)} %refs_5_.5) | copy-start | bytes 589828
  0.7 8.1 %copy-start.2 = (bf16[384,256]{1,0:T(8,128)(2,1)S(1)}, bf16[384,256]{1,0:T(8,128)(2,1)}, u32[]{:S(2)}) copy-start(bf16[384,256]{1,0:T(8,128)(2,1)} %refs_4_.5) | copy-start | bytes 589828
  0.7 8.1 %copy-start = (bf16[384,2048]{1,0:T(8,128)(2,1)S(1)}, bf16[384,2048]{1,0:T(8,128)(2,1)}, u32[]{:S(2)}) copy-start(bf16[384,2048]{1,0:T(8,128)(2,1)} %refs_2_.5) | copy-start | bytes 4718596
  4.7 22.7 %collective-permute-start = (bf16[256,512]{1,0:T(8,128)(2,1)}, bf16[256,512]{1,0:T(8,128)(2,1)}, u32[]{:S(2)}, u32[]{:S(2)}) collective-permute-start(bf16[256,512]{1,0:T(8,128)(2,1)} %get-tuple-element.44), channel_id=1, source_target_pairs={{0,16},{4,20},{8,24},{12,28},{16,0},{20,4},{24,8},{28,12},{1,17},{... | collective-permute-start | bytes 786440 | tf_op jit(solution)/shard_map/ppermute | solution.py:424
  8.8 1.0 %copy-start.6 = (bf16[384,512]{1,0:T(8,128)(2,1)S(1)}, bf16[384,512]{1,0:T(8,128)(2,1)}, u32[]{:S(2)}) copy-start(bf16[384,512]{1,0:T(8,128)(2,1)} %get-tuple-element.36.refs_6_.refs_0_) | copy-start | bytes 1179652
  9.8 0.9 %copy-start.10 = (f32[384,128]{1,0:T(8,128)S(1)}, f32[384,128]{1,0:T(8,128)}, u32[]{:S(2)}) copy-start(f32[384,128]{1,0:T(8,128)} %get-tuple-element.37.refs_7_) | copy-start | bytes 589828
  10.7 0.9 %copy-start.11 = (f32[384,128]{1,0:T(8,128)S(1)}, f32[384,128]{1,0:T(8,128)}, u32[]{:S(2)}) copy-start(f32[384,128]{1,0:T(8,128)} %get-tuple-element.38.refs_8_) | copy-start | bytes 589828
  11.6 0.7 copy-start.16
  12.3 0.7 copy-start.20
  15.8 4.9 %copy-start.4 = (bf16[384,512]{1,0:T(8,128)(2,1)}, bf16[384,512]{1,0:T(8,128)(2,1)S(1)}, u32[]{:S(2)}) copy-start(bf16[384,512]{1,0:T(8,128)(2,1)S(1)} %get-tuple-element.39.refs_6_.refs_0_) | copy-start | bytes 1179652
  15.8 25.7 %collective-permute-start.4 = (bf16[256,512]{1,0:T(8,128)(2,1)}, bf16[256,512]{1,0:T(8,128)(2,1)}, u32[]{:S(2)}, u32[]{:S(2)}) collective-permute-start(bf16[256,512]{1,0:T(8,128)(2,1)} %get-tuple-element.49), channel_id=1, source_target_pairs={{0,16},{4,20},{8,24},{12,28},{16,0},{20,4},{24,8},{28,12},{1,17},{... | collective-permute-start | bytes 786440 | tf_op jit(solution)/shard_map/ppermute | solution.py:424
  20.7 0.7 %copy-start.8 = (bf16[384,512]{1,0:T(8,128)(2,1)}, bf16[384,512]{1,0:T(8,128)(2,1)S(1)}, u32[]{:S(2)}) copy-start(bf16[384,512]{1,0:T(8,128)(2,1)S(1)} %get-tuple-element.45.refs_0_) | copy-start | bytes 1179652
  21.4 0.7 copy-start.12
  22.1 0.7 copy-start.14
  22.8 0.7 %copy-start.21 = (bf16[256,512]{1,0:T(8,128)(2,1)}, bf16[256,512]{1,0:T(8,128)(2,1)S(1)}, u32[]{:S(2)}) copy-start(bf16[256,512]{1,0:T(8,128)(2,1)S(1)} %get-tuple-element.46) | copy-start | bytes 786436
  22.8 12.0 %copy-start.7 = (bf16[384,512]{1,0:T(8,128)(2,1)S(1)}, bf16[384,512]{1,0:T(8,128)(2,1)}, u32[]{:S(2)}) copy-start(bf16[384,512]{1,0:T(8,128)(2,1)} %get-tuple-element.36.refs_6_.refs_0_) | copy-start | bytes 1179652
  23.5 18.0 %copy-start.5 = (bf16[384,512]{1,0:T(8,128)(2,1)S(1)}, bf16[384,512]{1,0:T(8,128)(2,1)}, u32[]{:S(2)}) copy-start(bf16[384,512]{1,0:T(8,128)(2,1)} %copy-done.4) | copy-start | bytes 1179652
  23.5 31.9 %collective-permute-start.3 = (bf16[256,768]{1,0:T(8,128)(2,1)}, bf16[256,768]{1,0:T(8,128)(2,1)S(1)}, u32[]{:S(2)}, u32[]{:S(2)}) collective-permute-start(bf16[256,768]{1,0:T(8,128)(2,1)} %get-tuple-element.48), channel_id=1, source_target_pairs={{0,16},{4,20},{8,24},{12,28},{16,0},{20,4},{24,8},{28,12},{1,17},{... | collective-permute-start | bytes 1179656 | tf_op jit(solution)/shard_map/ppermute | solution.py:424
  27.4 0.9 %copy-start.13 = (bf16[384,256]{1,0:T(8,128)(2,1)S(1)}, bf16[384,256]{1,0:T(8,128)(2,1)}, u32[]{:S(2)}) copy-start(bf16[384,256]{1,0:T(8,128)(2,1)} %copy-done.12) | copy-start | bytes 589828
  28.4 0.9 %copy-start.15 = (bf16[256,256]{1,0:T(8,128)(2,1)S(1)}, bf16[256,256]{1,0:T(8,128)(2,1)}, u32[]{:S(2)}) copy-start(bf16[256,256]{1,0:T(8,128)(2,1)} %copy-done.14) | copy-start | bytes 393220
  29.3 0.7 copy-start.17
  31.3 27.3 %all-to-all-start = ((bf16[4,2,96,256]{3,2,1,0:T(8,128)(2,1)}), bf16[4,2,96,256]{3,2,1,0:T(8,128)(2,1)S(1)}, u32[]{:S(2)}, u32[]{:S(2)}) async-start(bf16[4,2,96,256]{3,2,1,0:T(8,128)(2,1)} %shard_map.88), calls=%async_computation | async-start | bytes 786432 | tf_op jit(solution)/shard_map/all_to_all | solution.py:427
  34.8 0.7 copy-start.18
  36.5 23.9 %copy-start.9 = (bf16[384,512]{1,0:T(8,128)(2,1)S(1)}, bf16[384,512]{1,0:T(8,128)(2,1)}, u32[]{:S(2)}) copy-start(bf16[384,512]{1,0:T(8,128)(2,1)} %copy-done.8) | copy-start | bytes 1179652
  36.5 23.9 %copy-start.19 = (s32[24]{0:T(128)S(1)}, s32[24]{0:T(128)}, u32[]{:S(2)}) copy-start(s32[24]{0:T(128)} %refs_1_.7) | copy-start | bytes 292
  36.5 4.9 %collective-permute-start.5 = (bf16[96,512]{1,0:T(8,128)(2,1)S(1)}, bf16[96,512]{1,0:T(8,128)(2,1)S(1)}, u32[]{:S(2)}, u32[]{:S(2)}) collective-permute-start(bf16[96,512]{1,0:T(8,128)(2,1)S(1)} %get-tuple-element.51), channel_id=1, source_target_pairs={{0,1},{1,0},{2,3},{3,2},{4,5},{5,4},{6,7},{7,6},{8,9},{9,8},{10,11... | collective-permute-start | bytes 294920 | tf_op jit(solution)/shard_map/ppermute | solution.py:447
  37.1 7.7 %collective-permute-start.7 = (bf16[96,512]{1,0:T(8,128)(2,1)S(1)}, bf16[96,512]{1,0:T(8,128)(2,1)S(1)}, u32[]{:S(2)}, u32[]{:S(2)}) collective-permute-start(bf16[96,512]{1,0:T(8,128)(2,1)S(1)} %get-tuple-element.54), channel_id=1, source_target_pairs={{0,2},{1,3},{2,0},{3,1},{4,6},{5,7},{6,4},{7,5},{8,10},{9,11},{10,... | collective-permute-start | bytes 294920 | tf_op jit(solution)/shard_map/ppermute | solution.py:447
  38.7 7.1 %collective-permute-start.8 = (bf16[96,512]{1,0:T(8,128)(2,1)S(1)}, bf16[96,512]{1,0:T(8,128)(2,1)S(1)}, u32[]{:S(2)}, u32[]{:S(2)}) collective-permute-start(bf16[96,512]{1,0:T(8,128)(2,1)S(1)} %get-tuple-element.55), channel_id=1, source_target_pairs={{0,3},{1,2},{2,1},{3,0},{4,7},{5,6},{6,5},{7,4},{8,11},{9,10},{10,... | collective-permute-start | bytes 294920 | tf_op jit(solution)/shard_map/ppermute | solution.py:447
  43.2 12.2 %collective-permute-start.6 = (bf16[96,512]{1,0:T(8,128)(2,1)S(1)}, bf16[96,512]{1,0:T(8,128)(2,1)S(1)}, u32[]{:S(2)}, u32[]{:S(2)}) collective-permute-start(bf16[96,512]{1,0:T(8,128)(2,1)S(1)} %get-tuple-element.53), channel_id=1, source_target_pairs={{0,1},{1,0},{2,3},{3,2},{4,5},{5,4},{6,7},{7,6},{8,9},{9,8},{10,11... | collective-permute-start | bytes 294920 | tf_op jit(solution)/shard_map/ppermute | solution.py:447
  43.2 17.0 %collective-permute-start.2 = (bf16[256,512]{1,0:T(8,128)(2,1)}, bf16[256,512]{1,0:T(8,128)(2,1)S(1)}, u32[]{:S(2)}, u32[]{:S(2)}) collective-permute-start(bf16[256,512]{1,0:T(8,128)(2,1)} %copy-done.21), channel_id=1, source_target_pairs={{0,16},{4,20},{8,24},{12,28},{16,0},{20,4},{24,8},{28,12},{1,17},{... | collective-permute-start | bytes 786440 | tf_op jit(solution)/shard_map/ppermute | solution.py:424
  44.7 15.5 %collective-permute-start.10 = (bf16[96,512]{1,0:T(8,128)(2,1)}, bf16[96,512]{1,0:T(8,128)(2,1)S(1)}, u32[]{:S(2)}, u32[]{:S(2)}) collective-permute-start(bf16[96,512]{1,0:T(8,128)(2,1)} %get-tuple-element.58), channel_id=1, source_target_pairs={{0,2},{1,3},{2,0},{3,1},{4,6},{5,7},{6,4},{7,5},{8,10},{9,11},{10,... | collective-permute-start | bytes 294920 | tf_op jit(solution)/shard_map/ppermute | solution.py:447
  45.9 14.5 %collective-permute-start.11 = (bf16[96,512]{1,0:T(8,128)(2,1)}, bf16[96,512]{1,0:T(8,128)(2,1)S(1)}, u32[]{:S(2)}, u32[]{:S(2)}) collective-permute-start(bf16[96,512]{1,0:T(8,128)(2,1)} %get-tuple-element.59), channel_id=1, source_target_pairs={{0,3},{1,2},{2,1},{3,0},{4,7},{5,6},{6,5},{7,4},{8,11},{9,10},{10,... | collective-permute-start | bytes 294920 | tf_op jit(solution)/shard_map/ppermute | solution.py:447
  56.7 3.6 %collective-permute-start.9 = (bf16[96,768]{1,0:T(8,128)(2,1)}, bf16[96,768]{1,0:T(8,128)(2,1)S(1)}, u32[]{:S(2)}, u32[]{:S(2)}) collective-permute-start(bf16[96,768]{1,0:T(8,128)(2,1)} %get-tuple-element.57), channel_id=1, source_target_pairs={{0,1},{1,0},{2,3},{3,2},{4,5},{5,4},{6,7},{7,6},{8,9},{9,8},{10,11... | collective-permute-start | bytes 442376 | tf_op jit(solution)/shard_map/ppermute | solution.py:447
  56.7 6.4 %collective-permute-start.15 = (bf16[96,768]{1,0:T(8,128)(2,1)S(1)}, bf16[96,768]{1,0:T(8,128)(2,1)S(1)}, u32[]{:S(2)}, u32[]{:S(2)}) collective-permute-start(bf16[96,768]{1,0:T(8,128)(2,1)S(1)} %get-tuple-element.64), channel_id=1, source_target_pairs={{0,2},{1,3},{2,0},{3,1},{4,6},{5,7},{6,4},{7,5},{8,10},{9,11},{10,... | collective-permute-start | bytes 442376 | tf_op jit(solution)/shard_map/ppermute | solution.py:447
  60.2 11.2 %collective-permute-start.1 = (bf16[4,96,256]{2,1,0:T(8,128)(2,1)S(1)}, bf16[4,96,256]{2,1,0:T(8,128)(2,1)S(1)}, u32[]{:S(2)}, u32[]{:S(2)}) collective-permute-start(bf16[4,96,256]{2,1,0:T(8,128)(2,1)S(1)} %slice_bitcast_fusion), channel_id=1, source_target_pairs={{0,16},{4,20},{8,24},{12,28},{16,0},{20,4},{24,8},{28,12},{1,17},{... | collective-permute-start | bytes 589832 | tf_op jit(solution)/shard_map/ppermute | solution.py:428
  60.2 6.0 %collective-permute-start.16 = (bf16[96,768]{1,0:T(8,128)(2,1)S(1)}, bf16[96,768]{1,0:T(8,128)(2,1)S(1)}, u32[]{:S(2)}, u32[]{:S(2)}) collective-permute-start(bf16[96,768]{1,0:T(8,128)(2,1)S(1)} %get-tuple-element.65), channel_id=1, source_target_pairs={{0,3},{1,2},{2,1},{3,0},{4,7},{5,6},{6,5},{7,4},{8,11},{9,10},{10,... | collective-permute-start | bytes 442376 | tf_op jit(solution)/shard_map/ppermute | solution.py:447
  61.1 7.0 %collective-permute-start.12 = (bf16[96,512]{1,0:T(8,128)(2,1)S(1)}, bf16[96,512]{1,0:T(8,128)(2,1)S(1)}, u32[]{:S(2)}, u32[]{:S(2)}) collective-permute-start(bf16[96,512]{1,0:T(8,128)(2,1)S(1)} %get-tuple-element.61), channel_id=1, source_target_pairs={{0,1},{1,0},{2,3},{3,2},{4,5},{5,4},{6,7},{7,6},{8,9},{9,8},{10,11... | collective-permute-start | bytes 294920 | tf_op jit(solution)/shard_map/ppermute | solution.py:447
  62.7 5.9 %collective-permute-start.13 = (bf16[96,512]{1,0:T(8,128)(2,1)S(1)}, bf16[96,512]{1,0:T(8,128)(2,1)S(1)}, u32[]{:S(2)}, u32[]{:S(2)}) collective-permute-start(bf16[96,512]{1,0:T(8,128)(2,1)S(1)} %get-tuple-element.62), channel_id=1, source_target_pairs={{0,2},{1,3},{2,0},{3,1},{4,6},{5,7},{6,4},{7,5},{8,10},{9,11},{10,... | collective-permute-start | bytes 294920 | tf_op jit(solution)/shard_map/ppermute | solution.py:447
  63.1 7.3 %collective-permute-start.14 = (bf16[96,512]{1,0:T(8,128)(2,1)S(1)}, bf16[96,512]{1,0:T(8,128)(2,1)S(1)}, u32[]{:S(2)}, u32[]{:S(2)}) collective-permute-start(bf16[96,512]{1,0:T(8,128)(2,1)S(1)} %get-tuple-element.63), channel_id=1, source_target_pairs={{0,3},{1,2},{2,1},{3,0},{4,7},{5,6},{6,5},{7,4},{8,11},{9,10},{10,... | collective-permute-start | bytes 294920 | tf_op jit(solution)/shard_map/ppermute | solution.py:447

commit v5 on v4

--- a/solution.py
+++ b/solution.py
@@ -415,7 +415,7 @@
     for number, (group, start, heads, sets) in enumerate(kernels):
         made, carried = grads_chunk(
             doc_starts, block_mapping, queries, output_gradient, key_layout_rows, value_layout_rows,
-            after, carried, group * repeats + start, heads, group, sets, FULL_VMEM if number == 0 else SOME_VMEM,
+            after, carried, group * repeats + start, heads, group, sets, FULL_VMEM if number < 2 else SOME_VMEM,
         )
         after = made[0][0]
         for units, (own, send) in zip(sets, made):
@@ -442,6 +442,8 @@
     chunks = list(zip(sent, landed))
     for chunk in [chunks[:TOGETHER]] + [[c] for c in chunks[TOGETHER:]]:
         sources = [(own, arrived) for (_, _, own), arrived in chunk]
+        if len(pieces) == 2:
+            order = order + [spread]
         parts = sort_rows(position, block_mapping, sources, order, block_count, half_axis, peers)
         got = [parts[0]] + [
             lax.ppermute(parts[hop], "tensor", [(i, i ^ hop) for i in range(peers)]) for hop in range(1, peers)

time: 73.7 us -> 73.6 us (level)
    ppermute x1, waiting for transfers between devices: 0.96 us -> 3.37 us  [on_device(): last_arrived = lax.ppermute(spread[:, 1], 'ctx', pairs)]
    ppermute x4, waiting for transfers between devices: 14.2 us -> 12.8 us  [on_device(): landed.append(lax.ppermute(send, 'ctx', pairs))]
    pallas_call x4, Pallas kernels: 4.84 us -> 3.52 us  [sort_rows(): pl.pallas_call(functools.partial(sort_kernel, block_count, rows // block_...]
    pallas_call x3, Pallas kernels: 11.8 us -> 12.9 us  [grads_chunk(): pl.pallas_call(functools.partial(grads_kernel, block_count, block_rows, g...]
    ppermute x12, waiting for transfers between devices: 6.68 us -> 5.74 us  [on_device(): lax.ppermute(parts[hop], 'tensor', [(i, i ^ hop) for i in range(peers)])]
  transfers between devices with their start and end apart: 18 -> 18, of which waited for: 10 -> 7; matrix products, arithmetic and copies ran while one was open for 0% -> 0% of each run, Pallas kernels for 22% -> 22%
where the time goes in v5:
time: 73.6 us; the launch traced here: 72.7 us
  waiting for transfers between devices  21.9 us (30%)
  Pallas kernels  21 us (29%)
  starting transfers between devices  18.7 us (25%)
  local copies, waits for them, and re-layouts  10.1 us (14%)
  between operations  0.8 us (1%)
    pallas_call x3, Pallas kernels, grads_chunk(): pl.pallas_call(functools.partial(grads_kernel, block_count, block_rows, g...  12.9 us
    ppermute x4, waiting for transfers between devices, on_device(): landed.append(lax.ppermute(send, 'ctx', pairs))  12.8 us
    unnamed x44, local copies, waits for them, and re-layouts  10.1 us
    ppermute x12, starting transfers between devices, on_device(): lax.ppermute(parts[hop], 'tensor', [(i, i ^ hop) for i in range(peers)])  8.11 us
    ppermute x4, starting transfers between devices, on_device(): landed.append(lax.ppermute(send, 'ctx', pairs))  7.04 us
    ppermute x12, waiting for transfers between devices, on_device(): lax.ppermute(parts[hop], 'tensor', [(i, i ^ hop) for i in range(peers)])  5.74 us
    all_to_all x1, starting transfers between devices, on_device(): lax.all_to_all(spread, 'tensor', split_axis=0, concat_axis=0, tiled=True)  3.59 us
    pallas_call x4, Pallas kernels, sort_rows(): pl.pallas_call(functools.partial(sort_kernel, block_count, rows // block_...  3.52 us
  transfers between devices with their start and end apart: 18, of which 7 were waited for; matrix products, arithmetic and copies ran while one was open for 0% of the time, Pallas kernels for 22%

profile of v5, /device:TPU:0, one launch (start us, length us, event | category | flops | bytes accessed | tf_op | source)
XLA Modules:
  0.0 72.7 jit_solution(11093186370698017213)
XLA Ops:
  0.6 3.9 %shard_map.85 = (bf16[384,512]{1,0:T(8,128)(2,1)}, bf16[256,512]{1,0:T(8,128)(2,1)}, f32[384,128]{1,0:T(8,128)}, f32[384,128]{1,0:T(8,128)}) custom-call(s32[3]{0:T(128)} %refs_0_.5, s32[24]{0:T(128)} %refs_1_.7, bf16[384,2048]{1,0:T(8,128)(2,1)} %refs_2_.5, bf16[384,2048]{1,0:T(8,128)(2,1)} %refs_3_.5, bf16[384,256]{1,0:T(8,128)(2,1)} %refs_4_.5, ...), custom_call_target="tpu_custom_call" | custom-call | flops 1000 | bytes 1000 | tf_op jit(solution)/shard_map/pallas_call | solution.py:185
  4.5 4.0 %collective-permute-start = (bf16[256,512]{1,0:T(8,128)(2,1)}, bf16[256,512]{1,0:T(8,128)(2,1)}, u32[]{:S(2)}, u32[]{:S(2)}) collective-permute-start(bf16[256,512]{1,0:T(8,128)(2,1)} %get-tuple-element.44), channel_id=1, source_target_pairs={{0,16},{4,20},{8,24},{12,28},{16,0},{20,4},{24,8},{28,12},{1,17},{... | collective-permute-start | bytes 786440 | tf_op jit(solution)/shard_map/ppermute | solution.py:424
  8.6 4.2 %shard_map.86 = (bf16[384,512]{1,0:T(8,128)(2,1)}, bf16[256,512]{1,0:T(8,128)(2,1)}, f32[384,128]{1,0:T(8,128)}, f32[384,128]{1,0:T(8,128)}) custom-call(s32[3]{0:T(128)} %refs_0_.5, s32[24]{0:T(128)} %refs_1_.7, bf16[384,2048]{1,0:T(8,128)(2,1)} %refs_2_.5, bf16[384,2048]{1,0:T(8,128)(2,1)} %refs_3_.5, bf16[384,256]{1,0:T(8,128)(2,1)} %refs_4_.5, ...), custom_call_target="tpu_custom_call" | custom-call | flops 1000 | bytes 1000 | tf_op jit(solution)/shard_map/pallas_call | solution.py:185
  12.8 0.0 collective-permute-start.4
  12.8 0.0 copy-done
  12.8 1.0 %copy-done.4 = bf16[384,512]{1,0:T(8,128)(2,1)S(1)} copy-done((bf16[384,512]{1,0:T(8,128)(2,1)S(1)}, bf16[384,512]{1,0:T(8,128)(2,1)}, u32[]{:S(2)}) %copy-start.4) | copy-done | bytes 393240
  13.8 0.9 %copy-done.9 = f32[384,128]{1,0:T(8,128)S(1)} copy-done((f32[384,128]{1,0:T(8,128)S(1)}, f32[384,128]{1,0:T(8,128)}, u32[]{:S(2)}) %copy-start.9) | copy-done | bytes 196632
  14.7 0.9 %copy-done.10 = f32[384,128]{1,0:T(8,128)S(1)} copy-done((f32[384,128]{1,0:T(8,128)S(1)}, f32[384,128]{1,0:T(8,128)}, u32[]{:S(2)}) %copy-start.10) | copy-done | bytes 196632
  15.7 0.7 copy-done.15
  16.3 0.7 copy-done.19
  17.0 4.8 %shard_map.87 = (bf16[384,768]{1,0:T(8,128)(2,1)S(1)}, bf16[256,768]{1,0:T(8,128)(2,1)}, bf16[384,512]{1,0:T(8,128)(2,1)S(1)}, bf16[256,512]{1,0:T(8,128)(2,1)S(...) custom-call(s32[3]{0:T(128)S(1)} %copy-done.19, s32[24]{0:T(128)S(1)} %copy-done.15, ...), custom_call_target="tpu_custom_call" | custom-call | flops 1000 | bytes 1000 | tf_op jit(solution)/shard_map/pallas_call | solution.py:185
  21.8 0.8 %copy-done.7 = bf16[384,512]{1,0:T(8,128)(2,1)} copy-done((bf16[384,512]{1,0:T(8,128)(2,1)}, bf16[384,512]{1,0:T(8,128)(2,1)S(1)}, u32[]{:S(2)}) %copy-start.7) | copy-done | bytes 393240
  22.6 0.7 copy-done.11
  23.3 0.7 copy-done.13
  23.9 0.7 copy-done.20
  24.6 2.9 %collective-permute-start.3 = (bf16[256,768]{1,0:T(8,128)(2,1)}, bf16[256,768]{1,0:T(8,128)(2,1)S(1)}, u32[]{:S(2)}, u32[]{:S(2)}) collective-permute-start(bf16[256,768]{1,0:T(8,128)(2,1)} %get-tuple-element.48), channel_id=1, source_target_pairs={{0,16},{4,20},{8,24},{12,28},{16,0},{20,4},{24,8},{28,12},{1,17},{... | collective-permute-start | bytes 1179656 | tf_op jit(solution)/shard_map/ppermute | solution.py:424
  27.5 0.1 pad_add_fusion.position_ref.refs_0_
  27.6 0.0 collective-permute-done._.refs_1_
  27.6 0.9 %copy-done.12 = bf16[384,256]{1,0:T(8,128)(2,1)S(1)} copy-done((bf16[384,256]{1,0:T(8,128)(2,1)S(1)}, bf16[384,256]{1,0:T(8,128)(2,1)}, u32[]{:S(2)}) %copy-start.12) | copy-done | bytes 196632
  28.5 0.9 %copy-done.14 = bf16[256,256]{1,0:T(8,128)(2,1)S(1)} copy-done((bf16[256,256]{1,0:T(8,128)(2,1)S(1)}, bf16[256,256]{1,0:T(8,128)(2,1)}, u32[]{:S(2)}) %copy-start.14) | copy-done | bytes 131096
  29.5 0.7 copy-done.16
  30.1 1.4 %shard_map.88 = bf16[4,2,96,256]{3,2,1,0:T(8,128)(2,1)} custom-call(s32[2]{0:T(128)S(1)} %pad_add_fusion.position_ref.refs_0_, s32[24]{0:T(128)S(1)} %copy-done.16, bf16[384,256]{1,0:T(8,128)(2,1)S(1)} %copy-done.12, bf16[256,256]{1,0:T(8,128)(2,1)S(1)} %copy-done.14, bf16[256,512]{1,0:T(8,128)(2,1)} %collective-permute-done._.refs_1_), custom_call_target="tpu_custom_call" | custom-call | flops 1000 | bytes 1000 | tf_op jit(solution)/shard_map/pallas_call | solution.py:294
  31.5 3.6 %all-to-all-start = ((bf16[4,2,96,256]{3,2,1,0:T(8,128)(2,1)}), bf16[4,2,96,256]{3,2,1,0:T(8,128)(2,1)S(1)}, u32[]{:S(2)}, u32[]{:S(2)}) async-start(bf16[4,2,96,256]{3,2,1,0:T(8,128)(2,1)} %shard_map.88), calls=%async_computation | async-start | bytes 786432 | tf_op jit(solution)/shard_map/all_to_all | solution.py:427
  35.1 0.0 copy-start.17
  35.1 0.6 copy-done.17
  35.7 1.1 %shard_map.89 = (bf16[96,512]{1,0:T(8,128)(2,1)S(1)}, bf16[96,512]{1,0:T(8,128)(2,1)S(1)}, bf16[96,512]{1,0:T(8,128)(2,1)S(1)}, bf16[96,512]{1,0:T(8,128)(2,1)S(1)}) custom-call(s32[2]{0:T(128)S(1)} %pad_add_fusion.position_ref.refs_0_, s32[24]{0:T(128)S(1)} %copy-done.17, bf16[384,512]{1,0:T(8,128)(2,1)S(1)} %copy-done.6, ...), custom_call_target="tpu_custom_call" | custom-call | flops 1000 | bytes 1000 | tf_op jit(solution)/shard_map/pallas_call | solution.py:242
  36.8 0.0 copy-start.8
  36.8 0.5 collective-permute-start.5
  37.4 1.7 %collective-permute-start.7 = (bf16[96,512]{1,0:T(8,128)(2,1)S(1)}, bf16[96,512]{1,0:T(8,128)(2,1)S(1)}, u32[]{:S(2)}, u32[]{:S(2)}) collective-permute-start(bf16[96,512]{1,0:T(8,128)(2,1)S(1)} %get-tuple-element.54), channel_id=1, source_target_pairs={{0,2},{1,3},{2,0},{3,1},{4,6},{5,7},{6,4},{7,5},{8,10},{9,11},{10,... | collective-permute-start | bytes 294920 | tf_op jit(solution)/shard_map/ppermute | solution.py:449
  39.1 0.0 collective-permute-start.8
  39.1 2.2 %collective-permute-done.4.refs_1_ = bf16[256,512]{1,0:T(8,128)(2,1)} collective-permute-done((bf16[256,512]{1,0:T(8,128)(2,1)}, bf16[256,512]{1,0:T(8,128)(2,1)}, u32[]{:S(2)}, u32[]{:S(2)}) %collective-permute-start.4) | collective-permute-done | bytes 262176 | tf_op jit(solution)/shard_map/ppermute | solution.py:424
  41.3 0.0 collective-permute-done.5.refs_3_.refs_1_
  41.3 1.1 %shard_map.90 = (bf16[96,512]{1,0:T(8,128)(2,1)S(1)}, bf16[96,512]{1,0:T(8,128)(2,1)S(1)}, bf16[96,512]{1,0:T(8,128)(2,1)S(1)}, bf16[96,512]{1,0:T(8,128)(2,1)S(1)}) custom-call(s32[2]{0:T(128)S(1)} %pad_add_fusion.position_ref.refs_0_, s32[24]{0:T(128)S(1)} %copy-done.17, bf16[384,512]{1,0:T(8,128)(2,1)S(1)} %copy-done.5, ...), custom_call_target="tpu_custom_call" | custom-call | flops 1000 | bytes 1000 | tf_op jit(solution)/shard_map/pallas_call | solution.py:242
  42.4 0.1 collective-permute-start.6
  42.5 0.1 collective-permute-start.2
  42.6 2.5 %collective-permute-done.7.refs_4_.refs_2_ = bf16[96,512]{1,0:T(8,128)(2,1)S(1)} collective-permute-done((bf16[96,512]{1,0:T(8,128)(2,1)S(1)}, bf16[96,512]{1,0:T(8,128)(2,1)S(1)}, u32[]{:S(2)}, u32[]{:S(2)}) %collective-permute-start.7) | collective-permute-done | bytes 98336 | tf_op jit(solution)/shard_map/ppermute | solution.py:449
  45.1 0.1 collective-permute-start.10
  45.1 1.1 %collective-permute-done.8.refs_5_.refs_3_ = bf16[96,512]{1,0:T(8,128)(2,1)S(1)} collective-permute-done((bf16[96,512]{1,0:T(8,128)(2,1)S(1)}, bf16[96,512]{1,0:T(8,128)(2,1)S(1)}, u32[]{:S(2)}, u32[]{:S(2)}) %collective-permute-start.8) | collective-permute-done | bytes 98336 | tf_op jit(solution)/shard_map/ppermute | solution.py:449
  46.2 0.6 collective-permute-start.11
  46.8 8.5 %collective-permute-done.3.refs_1_ = bf16[256,768]{1,0:T(8,128)(2,1)S(1)} collective-permute-done((bf16[256,768]{1,0:T(8,128)(2,1)}, bf16[256,768]{1,0:T(8,128)(2,1)S(1)}, u32[]{:S(2)}, u32[]{:S(2)}) %collective-permute-start.3) | collective-permute-done | bytes 393248 | tf_op jit(solution)/shard_map/ppermute | solution.py:424
  55.2 0.0 collective-permute-done.6.refs_3_.refs_5_
  55.2 0.0 all-to-all-done.refs_6_.refs_2_
  55.2 0.7 shard_map.91
  55.9 0.1 collective-permute-start.9
  56.0 1.9 %collective-permute-start.15 = (bf16[96,768]{1,0:T(8,128)(2,1)S(1)}, bf16[96,768]{1,0:T(8,128)(2,1)S(1)}, u32[]{:S(2)}, u32[]{:S(2)}) collective-permute-start(bf16[96,768]{1,0:T(8,128)(2,1)S(1)} %get-tuple-element.64), channel_id=1, source_target_pairs={{0,2},{1,3},{2,0},{3,1},{4,6},{5,7},{6,4},{7,5},{8,10},{9,11},{10,... | collective-permute-start | bytes 442376 | tf_op jit(solution)/shard_map/ppermute | solution.py:449
  58.0 2.1 %collective-permute-done.2.refs_1_ = bf16[256,512]{1,0:T(8,128)(2,1)S(1)} collective-permute-done((bf16[256,512]{1,0:T(8,128)(2,1)S(1)}, bf16[256,512]{1,0:T(8,128)(2,1)S(1)}, u32[]{:S(2)}, u32[]{:S(2)}) %collective-permute-start.2) | collective-permute-done | bytes 262176 | tf_op jit(solution)/shard_map/ppermute | solution.py:424
  60.0 0.0 collective-permute-start.1
  60.0 0.0 collective-permute-done.10.refs_4_.refs_6_
  60.0 0.1 collective-permute-start.16
  60.2 0.0 collective-permute-done.11.refs_5_.refs_7_
  60.2 0.0 collective-permute-done.9.refs_3_.refs_9_
  60.2 0.0 copy-done.8
  60.2 0.7 shard_map.92
  60.9 1.6 %collective-permute-start.12 = (bf16[96,512]{1,0:T(8,128)(2,1)S(1)}, bf16[96,512]{1,0:T(8,128)(2,1)S(1)}, u32[]{:S(2)}, u32[]{:S(2)}) collective-permute-start(bf16[96,512]{1,0:T(8,128)(2,1)S(1)} %get-tuple-element.61), channel_id=1, source_target_pairs={{0,1},{1,0},{2,3},{3,2},{4,5},{5,4},{6,7},{7,6},{8,9},{9,8},{10,11... | collective-permute-start | bytes 294920 | tf_op jit(solution)/shard_map/ppermute | solution.py:449
  62.5 0.5 collective-permute-start.13
  62.9 0.0 collective-permute-done.15.refs_10_
  62.9 1.0 %collective-permute-start.14 = (bf16[96,512]{1,0:T(8,128)(2,1)S(1)}, bf16[96,512]{1,0:T(8,128)(2,1)S(1)}, u32[]{:S(2)}, u32[]{:S(2)}) collective-permute-start(bf16[96,512]{1,0:T(8,128)(2,1)S(1)} %get-tuple-element.63), channel_id=1, source_target_pairs={{0,3},{1,2},{2,1},{3,0},{4,7},{5,6},{6,5},{7,4},{8,11},{9,10},{10,... | collective-permute-start | bytes 294920 | tf_op jit(solution)/shard_map/ppermute | solution.py:449
  63.9 2.2 %collective-permute-done.16.refs_11_ = bf16[96,768]{1,0:T(8,128)(2,1)S(1)} collective-permute-done((bf16[96,768]{1,0:T(8,128)(2,1)S(1)}, bf16[96,768]{1,0:T(8,128)(2,1)S(1)}, u32[]{:S(2)}, u32[]{:S(2)}) %collective-permute-start.16) | collective-permute-done | bytes 147488 | tf_op jit(solution)/shard_map/ppermute | solution.py:449
  66.0 1.8 %shard_map.93 = (bf16[96,8192]{1,0:T(8,128)(2,1)}, bf16[96,1024]{1,0:T(8,128)(2,1)}, bf16[96,1024]{1,0:T(8,128)(2,1)}) custom-call(s32[2]{0:T(128)S(1)} %pad_add_fusion.position_ref.refs_0_, bf16[96,512]{1,0:T(8,128)(2,1)S(1)} %get-tuple-element.50.refs_2_.refs_0_, bf16[96,512]{1,0:T(8,128)(2,1)S(1)} %collective-permute-done.5.refs_3_.refs_1_, ...), custom_call_target="tpu_custom_call" | custom-call | flops 1000 | bytes 1000 | tf_op jit(solution)/shard_map/pallas_call | solution.py:375
  67.8 3.4 %collective-permute-done.1.refs_3_ = bf16[4,96,256]{2,1,0:T(8,128)(2,1)S(1)} collective-permute-done((bf16[4,96,256]{2,1,0:T(8,128)(2,1)S(1)}, bf16[4,96,256]{2,1,0:T(8,128)(2,1)S(1)}, u32[]{:S(2)}, u32[]{:S(2)}) %collective-permute-start.1) | collective-permute-done | bytes 196640 | tf_op jit(solution)/shard_map/ppermute | solution.py:428
  71.2 0.0 collective-permute-done.12.refs_5_
  71.2 0.0 collective-permute-done.13.refs_6_
  71.2 0.0 collective-permute-done.14.refs_7_
  71.2 1.5 %shard_map.94 = (bf16[96,8192]{1,0:T(8,128)(2,1)}, bf16[96,1024]{1,0:T(8,128)(2,1)}, bf16[96,1024]{1,0:T(8,128)(2,1)}) custom-call(s32[2]{0:T(128)S(1)} %pad_add_fusion.position_ref.refs_0_, s32[24]{0:T(128)S(1)} %copy-done.18, bf16[4,2,96,256]{3,2,1,0:T(8,128)(2,1)S(1)} %all-to-all-done.refs_6_.refs_2_, ...), custom_call_target="tpu_custom_call", output_to_operand_aliasing={{0}: (8, {}), {1}: (9, {}), {2}: (10, {})} | custom-call | flops 1000 | bytes 1000 | tf_op jit(solution)/shard_map/pallas_call | solution.py:343
  (28 shorter events, 0.1 us)
Async XLA Ops:
  4.5 23.1 %collective-permute-start = (bf16[256,512]{1,0:T(8,128)(2,1)}, bf16[256,512]{1,0:T(8,128)(2,1)}, u32[]{:S(2)}, u32[]{:S(2)}) collective-permute-start(bf16[256,512]{1,0:T(8,128)(2,1)} %get-tuple-element.44), channel_id=1, source_target_pairs={{0,16},{4,20},{8,24},{12,28},{16,0},{20,4},{24,8},{28,12},{1,17},{... | collective-permute-start | bytes 786440 | tf_op jit(solution)/shard_map/ppermute | solution.py:424
  8.6 4.2 %copy-start = (bf16[384,2048]{1,0:T(8,128)(2,1)S(1)}, bf16[384,2048]{1,0:T(8,128)(2,1)}, u32[]{:S(2)}) copy-start(bf16[384,2048]{1,0:T(8,128)(2,1)} %refs_2_.5) | copy-start | bytes 4718596
  8.6 4.2 %copy-start.1 = (bf16[384,2048]{1,0:T(8,128)(2,1)S(1)}, bf16[384,2048]{1,0:T(8,128)(2,1)}, u32[]{:S(2)}) copy-start(bf16[384,2048]{1,0:T(8,128)(2,1)} %refs_3_.5) | copy-start | bytes 4718596
  8.6 4.2 %copy-start.2 = (bf16[384,256]{1,0:T(8,128)(2,1)S(1)}, bf16[384,256]{1,0:T(8,128)(2,1)}, u32[]{:S(2)}) copy-start(bf16[384,256]{1,0:T(8,128)(2,1)} %refs_4_.5) | copy-start | bytes 589828
  8.6 4.2 %copy-start.3 = (bf16[384,256]{1,0:T(8,128)(2,1)S(1)}, bf16[384,256]{1,0:T(8,128)(2,1)}, u32[]{:S(2)}) copy-start(bf16[384,256]{1,0:T(8,128)(2,1)} %refs_5_.5) | copy-start | bytes 589828
  12.8 28.5 %collective-permute-start.4 = (bf16[256,512]{1,0:T(8,128)(2,1)}, bf16[256,512]{1,0:T(8,128)(2,1)}, u32[]{:S(2)}, u32[]{:S(2)}) collective-permute-start(bf16[256,512]{1,0:T(8,128)(2,1)} %get-tuple-element.49), channel_id=1, source_target_pairs={{0,16},{4,20},{8,24},{12,28},{16,0},{20,4},{24,8},{28,12},{1,17},{... | collective-permute-start | bytes 786440 | tf_op jit(solution)/shard_map/ppermute | solution.py:424
  12.8 1.0 %copy-start.4 = (bf16[384,512]{1,0:T(8,128)(2,1)S(1)}, bf16[384,512]{1,0:T(8,128)(2,1)}, u32[]{:S(2)}) copy-start(bf16[384,512]{1,0:T(8,128)(2,1)} %get-tuple-element.39.refs_6_.refs_0_) | copy-start | bytes 1179652
  13.8 0.9 %copy-start.9 = (f32[384,128]{1,0:T(8,128)S(1)}, f32[384,128]{1,0:T(8,128)}, u32[]{:S(2)}) copy-start(f32[384,128]{1,0:T(8,128)} %get-tuple-element.40.refs_7_) | copy-start | bytes 589828
  14.7 0.9 %copy-start.10 = (f32[384,128]{1,0:T(8,128)S(1)}, f32[384,128]{1,0:T(8,128)}, u32[]{:S(2)}) copy-start(f32[384,128]{1,0:T(8,128)} %get-tuple-element.41.refs_8_) | copy-start | bytes 589828
  15.7 0.7 copy-start.15
  16.3 0.7 copy-start.19
  21.8 0.8 %copy-start.7 = (bf16[384,512]{1,0:T(8,128)(2,1)}, bf16[384,512]{1,0:T(8,128)(2,1)S(1)}, u32[]{:S(2)}) copy-start(bf16[384,512]{1,0:T(8,128)(2,1)S(1)} %get-tuple-element.45.refs_0_) | copy-start | bytes 1179652
  22.6 0.7 copy-start.11
  23.3 0.7 copy-start.13
  23.9 0.7 copy-start.20
  24.6 10.4 %copy-start.6 = (bf16[384,512]{1,0:T(8,128)(2,1)S(1)}, bf16[384,512]{1,0:T(8,128)(2,1)}, u32[]{:S(2)}) copy-start(bf16[384,512]{1,0:T(8,128)(2,1)} %get-tuple-element.36.refs_6_.refs_0_) | copy-start | bytes 1179652
  24.6 16.7 %copy-start.5 = (bf16[384,512]{1,0:T(8,128)(2,1)S(1)}, bf16[384,512]{1,0:T(8,128)(2,1)}, u32[]{:S(2)}) copy-start(bf16[384,512]{1,0:T(8,128)(2,1)} %get-tuple-element.39.refs_6_.refs_0_) | copy-start | bytes 1179652
  24.6 30.6 %collective-permute-start.3 = (bf16[256,768]{1,0:T(8,128)(2,1)}, bf16[256,768]{1,0:T(8,128)(2,1)S(1)}, u32[]{:S(2)}, u32[]{:S(2)}) collective-permute-start(bf16[256,768]{1,0:T(8,128)(2,1)} %get-tuple-element.48), channel_id=1, source_target_pairs={{0,16},{4,20},{8,24},{12,28},{16,0},{20,4},{24,8},{28,12},{1,17},{... | collective-permute-start | bytes 1179656 | tf_op jit(solution)/shard_map/ppermute | solution.py:424
  27.6 0.9 %copy-start.12 = (bf16[384,256]{1,0:T(8,128)(2,1)S(1)}, bf16[384,256]{1,0:T(8,128)(2,1)}, u32[]{:S(2)}) copy-start(bf16[384,256]{1,0:T(8,128)(2,1)} %copy-done.11) | copy-start | bytes 589828
  28.5 0.9 %copy-start.14 = (bf16[256,256]{1,0:T(8,128)(2,1)S(1)}, bf16[256,256]{1,0:T(8,128)(2,1)}, u32[]{:S(2)}) copy-start(bf16[256,256]{1,0:T(8,128)(2,1)} %copy-done.13) | copy-start | bytes 393220
  29.4 0.7 copy-start.16
  31.5 11.0 %copy-start.21 = (bf16[256,512]{1,0:T(8,128)(2,1)S(1)}, bf16[256,512]{1,0:T(8,128)(2,1)}, u32[]{:S(2)}) copy-start(bf16[256,512]{1,0:T(8,128)(2,1)} %copy-done.20) | copy-start | bytes 786436
  31.5 23.8 %copy-start.18 = (s32[24]{0:T(128)S(1)}, s32[24]{0:T(128)}, u32[]{:S(2)}) copy-start(s32[24]{0:T(128)} %refs_1_.7) | copy-start | bytes 292
  31.5 23.8 %all-to-all-start = ((bf16[4,2,96,256]{3,2,1,0:T(8,128)(2,1)}), bf16[4,2,96,256]{3,2,1,0:T(8,128)(2,1)S(1)}, u32[]{:S(2)}, u32[]{:S(2)}) async-start(bf16[4,2,96,256]{3,2,1,0:T(8,128)(2,1)} %shard_map.88), calls=%async_computation | async-start | bytes 786432 | tf_op jit(solution)/shard_map/all_to_all | solution.py:427
  35.1 0.7 copy-start.17
  36.8 23.3 %copy-start.8 = (bf16[384,512]{1,0:T(8,128)(2,1)S(1)}, bf16[384,512]{1,0:T(8,128)(2,1)}, u32[]{:S(2)}) copy-start(bf16[384,512]{1,0:T(8,128)(2,1)} %copy-done.7) | copy-start | bytes 1179652
  36.8 4.5 %collective-permute-start.5 = (bf16[96,512]{1,0:T(8,128)(2,1)S(1)}, bf16[96,512]{1,0:T(8,128)(2,1)S(1)}, u32[]{:S(2)}, u32[]{:S(2)}) collective-permute-start(bf16[96,512]{1,0:T(8,128)(2,1)S(1)} %get-tuple-element.51), channel_id=1, source_target_pairs={{0,1},{1,0},{2,3},{3,2},{4,5},{5,4},{6,7},{7,6},{8,9},{9,8},{10,11... | collective-permute-start | bytes 294920 | tf_op jit(solution)/shard_map/ppermute | solution.py:449
  37.4 7.7 %collective-permute-start.7 = (bf16[96,512]{1,0:T(8,128)(2,1)S(1)}, bf16[96,512]{1,0:T(8,128)(2,1)S(1)}, u32[]{:S(2)}, u32[]{:S(2)}) collective-permute-start(bf16[96,512]{1,0:T(8,128)(2,1)S(1)} %get-tuple-element.54), channel_id=1, source_target_pairs={{0,2},{1,3},{2,0},{3,1},{4,6},{5,7},{6,4},{7,5},{8,10},{9,11},{10,... | collective-permute-start | bytes 294920 | tf_op jit(solution)/shard_map/ppermute | solution.py:449
  39.1 7.2 %collective-permute-start.8 = (bf16[96,512]{1,0:T(8,128)(2,1)S(1)}, bf16[96,512]{1,0:T(8,128)(2,1)S(1)}, u32[]{:S(2)}, u32[]{:S(2)}) collective-permute-start(bf16[96,512]{1,0:T(8,128)(2,1)S(1)} %get-tuple-element.55), channel_id=1, source_target_pairs={{0,3},{1,2},{2,1},{3,0},{4,7},{5,6},{6,5},{7,4},{8,11},{9,10},{10,... | collective-permute-start | bytes 294920 | tf_op jit(solution)/shard_map/ppermute | solution.py:449
  42.4 12.8 %collective-permute-start.6 = (bf16[96,512]{1,0:T(8,128)(2,1)S(1)}, bf16[96,512]{1,0:T(8,128)(2,1)S(1)}, u32[]{:S(2)}, u32[]{:S(2)}) collective-permute-start(bf16[96,512]{1,0:T(8,128)(2,1)S(1)} %get-tuple-element.53), channel_id=1, source_target_pairs={{0,1},{1,0},{2,3},{3,2},{4,5},{5,4},{6,7},{7,6},{8,9},{9,8},{10,11... | collective-permute-start | bytes 294920 | tf_op jit(solution)/shard_map/ppermute | solution.py:449
  42.5 17.5 %collective-permute-start.2 = (bf16[256,512]{1,0:T(8,128)(2,1)S(1)}, bf16[256,512]{1,0:T(8,128)(2,1)S(1)}, u32[]{:S(2)}, u32[]{:S(2)}) collective-permute-start(bf16[256,512]{1,0:T(8,128)(2,1)S(1)} %copy-done.21), channel_id=1, source_target_pairs={{0,16},{4,20},{8,24},{12,28},{16,0},{20,4},{24,8},{28,12},{1,17},{... | collective-permute-start | bytes 786440 | tf_op jit(solution)/shard_map/ppermute | solution.py:424
  45.1 15.0 %collective-permute-start.10 = (bf16[96,512]{1,0:T(8,128)(2,1)S(1)}, bf16[96,512]{1,0:T(8,128)(2,1)S(1)}, u32[]{:S(2)}, u32[]{:S(2)}) collective-permute-start(bf16[96,512]{1,0:T(8,128)(2,1)S(1)} %get-tuple-element.58), channel_id=1, source_target_pairs={{0,2},{1,3},{2,0},{3,1},{4,6},{5,7},{6,4},{7,5},{8,10},{9,11},{10,... | collective-permute-start | bytes 294920 | tf_op jit(solution)/shard_map/ppermute | solution.py:449
  46.2 14.0 %collective-permute-start.11 = (bf16[96,512]{1,0:T(8,128)(2,1)S(1)}, bf16[96,512]{1,0:T(8,128)(2,1)S(1)}, u32[]{:S(2)}, u32[]{:S(2)}) collective-permute-start(bf16[96,512]{1,0:T(8,128)(2,1)S(1)} %get-tuple-element.59), channel_id=1, source_target_pairs={{0,3},{1,2},{2,1},{3,0},{4,7},{5,6},{6,5},{7,4},{8,11},{9,10},{10,... | collective-permute-start | bytes 294920 | tf_op jit(solution)/shard_map/ppermute | solution.py:449
  55.9 4.2 %collective-permute-start.9 = (bf16[96,768]{1,0:T(8,128)(2,1)S(1)}, bf16[96,768]{1,0:T(8,128)(2,1)S(1)}, u32[]{:S(2)}, u32[]{:S(2)}) collective-permute-start(bf16[96,768]{1,0:T(8,128)(2,1)S(1)} %get-tuple-element.57), channel_id=1, source_target_pairs={{0,1},{1,0},{2,3},{3,2},{4,5},{5,4},{6,7},{7,6},{8,9},{9,8},{10,11... | collective-permute-start | bytes 442376 | tf_op jit(solution)/shard_map/ppermute | solution.py:449
  56.0 6.9 %collective-permute-start.15 = (bf16[96,768]{1,0:T(8,128)(2,1)S(1)}, bf16[96,768]{1,0:T(8,128)(2,1)S(1)}, u32[]{:S(2)}, u32[]{:S(2)}) collective-permute-start(bf16[96,768]{1,0:T(8,128)(2,1)S(1)} %get-tuple-element.64), channel_id=1, source_target_pairs={{0,2},{1,3},{2,0},{3,1},{4,6},{5,7},{6,4},{7,5},{8,10},{9,11},{10,... | collective-permute-start | bytes 442376 | tf_op jit(solution)/shard_map/ppermute | solution.py:449
  60.0 11.2 %collective-permute-start.1 = (bf16[4,96,256]{2,1,0:T(8,128)(2,1)S(1)}, bf16[4,96,256]{2,1,0:T(8,128)(2,1)S(1)}, u32[]{:S(2)}, u32[]{:S(2)}) collective-permute-start(bf16[4,96,256]{2,1,0:T(8,128)(2,1)S(1)} %slice_bitcast_fusion), channel_id=1, source_target_pairs={{0,16},{4,20},{8,24},{12,28},{16,0},{20,4},{24,8},{28,12},{1,17},{... | collective-permute-start | bytes 589832 | tf_op jit(solution)/shard_map/ppermute | solution.py:428
  60.0 6.0 %collective-permute-start.16 = (bf16[96,768]{1,0:T(8,128)(2,1)S(1)}, bf16[96,768]{1,0:T(8,128)(2,1)S(1)}, u32[]{:S(2)}, u32[]{:S(2)}) collective-permute-start(bf16[96,768]{1,0:T(8,128)(2,1)S(1)} %get-tuple-element.65), channel_id=1, source_target_pairs={{0,3},{1,2},{2,1},{3,0},{4,7},{5,6},{6,5},{7,4},{8,11},{9,10},{10,... | collective-permute-start | bytes 442376 | tf_op jit(solution)/shard_map/ppermute | solution.py:449
  60.9 10.3 %collective-permute-start.12 = (bf16[96,512]{1,0:T(8,128)(2,1)S(1)}, bf16[96,512]{1,0:T(8,128)(2,1)S(1)}, u32[]{:S(2)}, u32[]{:S(2)}) collective-permute-start(bf16[96,512]{1,0:T(8,128)(2,1)S(1)} %get-tuple-element.61), channel_id=1, source_target_pairs={{0,1},{1,0},{2,3},{3,2},{4,5},{5,4},{6,7},{7,6},{8,9},{9,8},{10,11... | collective-permute-start | bytes 294920 | tf_op jit(solution)/shard_map/ppermute | solution.py:449
  62.5 8.7 %collective-permute-start.13 = (bf16[96,512]{1,0:T(8,128)(2,1)S(1)}, bf16[96,512]{1,0:T(8,128)(2,1)S(1)}, u32[]{:S(2)}, u32[]{:S(2)}) collective-permute-start(bf16[96,512]{1,0:T(8,128)(2,1)S(1)} %get-tuple-element.62), channel_id=1, source_target_pairs={{0,2},{1,3},{2,0},{3,1},{4,6},{5,7},{6,4},{7,5},{8,10},{9,11},{10,... | collective-permute-start | bytes 294920 | tf_op jit(solution)/shard_map/ppermute | solution.py:449
  62.9 8.3 %collective-permute-start.14 = (bf16[96,512]{1,0:T(8,128)(2,1)S(1)}, bf16[96,512]{1,0:T(8,128)(2,1)S(1)}, u32[]{:S(2)}, u32[]{:S(2)}) collective-permute-start(bf16[96,512]{1,0:T(8,128)(2,1)S(1)} %get-tuple-element.63), channel_id=1, source_target_pairs={{0,3},{1,2},{2,1},{3,0},{4,7},{5,6},{6,5},{7,4},{8,11},{9,10},{10,... | collective-permute-start | bytes 294920 | tf_op jit(solution)/shard_map/ppermute | solution.py:449
